TPU v7x, 32 devices: a whole 2x2x4 slice. The times are simulated.
32 devices in a mesh: win: 16 (over z, y, core), rep: 2 (over x).
Axes of the slice: x: 2, y: 2, z: 4, core: 2. Of those that a mesh axis runs over, the one named last changes fastest.
Arguments:
- tokens: bfloat16 [2, 320, 50, 512], P('rep', 'win'), may hold values from -6 to 6
- patch_mask: int32 [2, 320, 49], P('rep', 'win'), may hold values 0 or 1
- keep_mask: int32 [2, 320, 3], P('rep', 'win'), may hold values 0 or 1
- image_map: int32 [2, 320], P('rep'), may hold values from 0 to 7
- qkv_weight: bfloat16 [3, 512, 512], replicated, may hold values from -0.25 to 0.25
- out_weight: bfloat16 [512, 512], replicated, may hold values from -0.75 to 0.75
- up_weight: bfloat16 [512, 2048], replicated, may hold values from -0.25 to 0.25
- down_weight: bfloat16 [2048, 512], replicated, may hold values from -0.125 to 0.125
- vectors: float32 [14, 512], replicated
- qkv_mom: float32 [3, 512, 512], P(None, 'win'), may hold values from -512 to 512
- out_mom: float32 [512, 512], P('win'), may hold values from -512 to 512
- up_mom: float32 [512, 2048], P('win'), may hold values from -512 to 512
- down_mom: float32 [2048, 512], P('win'), may hold values from -512 to 512
- vec_mom: float32 [7168], P('win'), may hold values from -512 to 512
- cotangent: bfloat16 [2, 320, 50, 512], P('rep', 'win'), may hold values from -6 to 6
Outputs:
- out_tokens: bfloat16 [2, 320, 50, 512], P('rep', 'win')
- grad_tokens: float32 [2, 320, 50, 512], P('rep', 'win')
- new_qkv_mom: float32 [3, 512, 512], P(None, 'win')
- new_qkv: float32 [3, 512, 512], P(None, 'win')
- new_out_mom: float32 [512, 512], P('win')
- new_out: float32 [512, 512], P('win')
- new_up_mom: float32 [512, 2048], P('win')
- new_up: float32 [512, 2048], P('win')
- new_down_mom: float32 [2048, 512], P('win')
- new_down: float32 [2048, 512], P('win')
- new_vec_mom: float32 [7168], P('win')
- new_vectors: float32 [7168], P('win')
Inputs may be any that keep to these rules, and one draw needn't show every extreme that they name: `image_map`: each window's image is independent of its position, so the windows of one image lie scattered over all devices of its group.
All inputs are finite; a program needn't handle non-finite values. No bound on the sum of `patch_mask` or of `keep_mask` on one device may be relied on, other than what follows from the above.
Results may differ from a plain program's by a relative error of at most 0.011.
Values may be sent and summed in bfloat16 or wider, within the bound.
No kernel may reach another device: no remote copies, remote signals or barrier semaphores. Data moves between devices by JAX's collectives and lax.ppermute only.
A program may use at most 192 MiB of HBM per device.

v0:
```python
import jax
import jax.numpy as jnp
from jax import lax
from jax.sharding import PartitionSpec as P

HEADS = 16
HEAD_DIM = 32


EPSILON = 1e-06
MOMENTUM_DECAY = 0.95
MATRIX_RATE = 0.5
VECTOR_RATE = 0.0002
KEEP_SHARE = 0.75
NEWTON_COEFFS = (3.4445, -4.775, 2.0315)
HIGHEST = lax.Precision.HIGHEST


def broadcast(array, axis, root):
    mine = lax.axis_index(axis) == root
    return lax.psum(jnp.where(mine, array, jnp.zeros_like(array)), axis)


def bfloat(values):
    return values.astype(jnp.bfloat16)


def product(left_side, right_side):
    return jnp.dot(left_side, right_side, preferred_element_type=jnp.float32)


def norm_rows(values, gain_row, shift_row):
    center = values - jnp.mean(values, -1, keepdims=True)
    spread = jnp.mean(center * center, -1, keepdims=True)
    return center * lax.rsqrt(spread + EPSILON) * gain_row + shift_row


def soft_scores(queries, keyset, allowed):
    logits = jnp.einsum(
        "bqhd,bkhd->bhqk", queries, keyset, preferred_element_type=jnp.float32
    ) * HEAD_DIM ** (-0.5)
    logits = jnp.where(allowed, logits, -1e30)
    row_top = jnp.max(logits, -1, keepdims=True)
    raised = jnp.exp(logits - row_top)
    return raised / jnp.sum(raised, -1, keepdims=True)


def mix_values(probs_low, values):
    return jnp.einsum("bhqk,bkhd->bqhd", probs_low, values, preferred_element_type=jnp.float32)


def attend_back(attn_probs, probs_low, queries, keyset, values, mix_grad):
    value_grad = jnp.einsum(
        "bhqk,bqhd->bkhd", probs_low, mix_grad, preferred_element_type=jnp.float32
    )
    prob_grad = jnp.einsum("bqhd,bkhd->bhqk", mix_grad, values, preferred_element_type=jnp.float32)
    score_low = bfloat(
        attn_probs * (prob_grad - jnp.sum(attn_probs * prob_grad, -1, keepdims=True))
    )
    factor = HEAD_DIM ** (-0.5)
    query_grad = (
        jnp.einsum("bhqk,bkhd->bqhd", score_low, keyset, preferred_element_type=jnp.float32)
        * factor
    )
    key_grad = (
        jnp.einsum("bhqk,bqhd->bkhd", score_low, queries, preferred_element_type=jnp.float32)
        * factor
    )
    return (query_grad, key_grad, value_grad)


def newton(matrix):
    is_tall = matrix.shape[0] > matrix.shape[1]
    iterate = matrix.T if is_tall else matrix
    iterate = iterate / (jnp.sqrt(jnp.sum(iterate * iterate)) + EPSILON)
    for sweep_count in range(5):
        gram_matrix = jnp.matmul(iterate, iterate.T, precision=HIGHEST)
        polynomial = NEWTON_COEFFS[1] * gram_matrix + NEWTON_COEFFS[2] * jnp.matmul(
            gram_matrix, gram_matrix, precision=HIGHEST
        )
        iterate = NEWTON_COEFFS[0] * iterate + jnp.matmul(polynomial, iterate, precision=HIGHEST)
    result = iterate.T if is_tall else iterate
    return result * max(1.0, matrix.shape[0] / matrix.shape[1]) ** 0.5


def owner_update(matrix, owner_rank, rep_index, rows_here, win_index):

    def compute_update():
        return newton(matrix)

    def zero_update():
        return jnp.zeros_like(matrix)

    local_part = lax.cond(rep_index == owner_rank, compute_update, zero_update)
    whole_update = broadcast(local_part.astype(jnp.bfloat16), "rep", owner_rank).astype(
        local_part.dtype
    )
    return lax.dynamic_slice_in_dim(whole_update, win_index * rows_here, rows_here, 0)


def local(
    tokens,
    patch_mask,
    keep_mask,
    image_map,
    qkv_weight,
    out_weight,
    up_weight,
    down_weight,
    vectors,
    qkv_mom,
    out_mom,
    up_mom,
    down_mom,
    vec_mom,
    cotangent,
):
    windows = tokens.shape[1]
    seq_len = tokens.shape[2]
    model_width = tokens.shape[3]
    hidden_width = up_weight.shape[1]
    row_count = windows * seq_len
    win_index = lax.axis_index("win")
    rep_index = lax.axis_index("rep")
    inputs = tokens[0].astype(jnp.float32)
    keeper = keep_mask[0].astype(jnp.float32) / KEEP_SHARE
    all_images = image_map[0]
    own_images = lax.dynamic_slice_in_dim(all_images, win_index * windows, windows)
    qkv_flat = jnp.concatenate([qkv_weight[0], qkv_weight[1], qkv_weight[2]], axis=1)
    qkv_bias = jnp.concatenate([vectors[6], jnp.zeros((model_width,), jnp.float32), vectors[7]])
    bias_up = vectors[10:].reshape(hidden_width)
    region = inputs[:, 0]
    region_norm = bfloat(norm_rows(region, vectors[0], vectors[1]))
    region_proj = product(region_norm, qkv_flat) + qkv_bias
    region_query = bfloat(region_proj[:, :model_width])
    region_key = bfloat(region_proj[:, model_width : 2 * model_width])
    region_value = bfloat(region_proj[:, 2 * model_width :])
    keys_all, values_all = (
        lax.all_gather(region_key, "win", axis=0, tiled=True),
        lax.all_gather(region_value, "win", axis=0, tiled=True),
    )
    head_shape = (1, -1, HEADS, HEAD_DIM)
    region_q4 = region_query.reshape(head_shape)
    keys_all4 = keys_all.reshape(head_shape)
    values_all4 = values_all.reshape(head_shape)
    region_allowed = (own_images[:, None] == all_images[None, :])[None, None]
    region_probs = soft_scores(region_q4, keys_all4, region_allowed)
    region_plow = bfloat(region_probs)
    region_mix = bfloat(mix_values(region_plow, values_all4).reshape(windows, model_width))
    region_branch = product(region_mix, out_weight) + vectors[8]
    region_new = region + keeper[:, 0:1] * region_branch
    sequence = jnp.concatenate([region_new[:, None], inputs[:, 1:]], axis=1)
    flat_seq = sequence.reshape(row_count, model_width)
    seq_norm = bfloat(norm_rows(flat_seq, vectors[2], vectors[3]))
    seq_proj = product(seq_norm, qkv_flat) + qkv_bias
    window_shape = (windows, seq_len, HEADS, HEAD_DIM)
    local_query = bfloat(seq_proj[:, :model_width]).reshape(window_shape)
    local_key = bfloat(seq_proj[:, model_width : 2 * model_width]).reshape(window_shape)
    local_value = bfloat(seq_proj[:, 2 * model_width :]).reshape(window_shape)
    key_valid = jnp.concatenate([jnp.ones((windows, 1), jnp.int32), patch_mask[0]], axis=1) == 1
    local_probs = soft_scores(local_query, local_key, key_valid[:, None, None, :])
    local_plow = bfloat(local_probs)
    local_mix = bfloat(mix_values(local_plow, local_value).reshape(row_count, model_width))
    local_branch = product(local_mix, out_weight) + vectors[8]
    keep_attn = jnp.broadcast_to(keeper[:, 1:2], (windows, seq_len)).reshape(row_count, 1)
    keep_mlp = jnp.broadcast_to(keeper[:, 2:3], (windows, seq_len)).reshape(row_count, 1)
    after_attn = flat_seq + keep_attn * local_branch
    mlp_norm = bfloat(norm_rows(after_attn, vectors[4], vectors[5]))
    up_value = product(mlp_norm, up_weight) + bias_up
    activated, gelu_back = jax.vjp(jax.nn.gelu, up_value)
    act_low = bfloat(activated)
    mlp_branch = product(act_low, down_weight) + vectors[9]
    output = after_attn + keep_mlp * mlp_branch
    grad_out = cotangent[0].astype(jnp.float32).reshape(row_count, model_width)
    mlp_grad = bfloat(keep_mlp * grad_out)
    grad_down = product(act_low.T, mlp_grad)
    grad_bm = jnp.sum(mlp_grad.astype(jnp.float32), 0)
    up_grad = bfloat(gelu_back(product(mlp_grad, down_weight.T))[0])
    grad_up = product(mlp_norm.T, up_grad)
    grad_bu = jnp.sum(up_grad.astype(jnp.float32), 0)
    norm3_back = jax.vjp(norm_rows, after_attn, vectors[4], vectors[5])[1](
        product(up_grad, up_weight.T)
    )
    attn_res_grad = grad_out + norm3_back[0]
    local_branch_grad = bfloat(keep_attn * attn_res_grad)
    grad_outw = product(local_mix.T, local_branch_grad)
    local_mix_grad = bfloat(product(local_branch_grad, out_weight.T)).reshape(window_shape)
    local_qg, local_kg, local_vg = attend_back(
        local_probs, local_plow, local_query, local_key, local_value, local_mix_grad
    )
    local_qkv_grad = bfloat(
        jnp.concatenate(
            [
                local_qg.reshape(row_count, model_width),
                local_kg.reshape(row_count, model_width),
                local_vg.reshape(row_count, model_width),
            ],
            axis=1,
        )
    )
    norm2_back = jax.vjp(norm_rows, flat_seq, vectors[2], vectors[3])[1](
        product(local_qkv_grad, qkv_flat.T)
    )
    seq_grad = (attn_res_grad + norm2_back[0]).reshape(windows, seq_len, model_width)
    region_new_grad = seq_grad[:, 0]
    region_branch_grad = bfloat(keeper[:, 0:1] * region_new_grad)
    grad_outw = grad_outw + product(region_mix.T, region_branch_grad)
    grad_bo = jnp.sum(local_branch_grad.astype(jnp.float32), 0) + jnp.sum(
        region_branch_grad.astype(jnp.float32), 0
    )
    region_mix_grad = bfloat(product(region_branch_grad, out_weight.T)).reshape(head_shape)
    region_qg, region_kg, region_vg = attend_back(
        region_probs, region_plow, region_q4, keys_all4, values_all4, region_mix_grad
    )
    group_rows = keys_all.shape[0]
    key_share, value_share = (
        lax.psum_scatter(
            region_kg.reshape(group_rows, model_width).astype(jnp.bfloat16),
            "win",
            scatter_dimension=0,
            tiled=True,
        ).astype(jnp.float32),
        lax.psum_scatter(
            region_vg.reshape(group_rows, model_width).astype(jnp.bfloat16),
            "win",
            scatter_dimension=0,
            tiled=True,
        ).astype(jnp.float32),
    )
    region_qkv_grad = bfloat(
        jnp.concatenate([region_qg.reshape(windows, model_width), key_share, value_share], axis=1)
    )
    norm1_back = jax.vjp(norm_rows, region, vectors[0], vectors[1])[1](
        product(region_qkv_grad, qkv_flat.T)
    )
    region_grad = region_new_grad + norm1_back[0]
    input_grad = jnp.concatenate([region_grad[:, None], seq_grad[:, 1:]], axis=1)
    all_norm = jnp.concatenate([seq_norm, region_norm], axis=0)
    all_qkv_grad = jnp.concatenate([local_qkv_grad, region_qkv_grad], axis=0)
    grad_qkv = jnp.stack(
        [
            product(all_norm.T, all_qkv_grad[:, number * model_width : (number + 1) * model_width])
            for number in range(3)
        ]
    )
    qkv_bias_grad = jnp.sum(all_qkv_grad.astype(jnp.float32), 0)
    grad_vec = jnp.concatenate(
        [
            jnp.stack(
                [
                    norm1_back[1],
                    norm1_back[2],
                    norm2_back[1],
                    norm2_back[2],
                    norm3_back[1],
                    norm3_back[2],
                    qkv_bias_grad[:model_width],
                    qkv_bias_grad[2 * model_width :],
                    grad_bo,
                    grad_bm,
                ]
            ),
            grad_bu.reshape(-1, model_width),
        ],
        axis=0,
    ).reshape(-1)
    gradients = (grad_qkv, grad_outw, grad_up, grad_down, grad_vec)
    shard_rows = out_mom.shape[0]
    ff_rows = down_mom.shape[0]
    vec_rows = vec_mom.shape[0]
    totals = lax.psum(
        (gradients[0], gradients[1], gradients[2], gradients[3], gradients[4]), ("win", "rep")
    )
    shares = (
        lax.dynamic_slice_in_dim(totals[0], win_index * shard_rows, shard_rows, 1),
        lax.dynamic_slice_in_dim(totals[1], win_index * shard_rows, shard_rows, 0),
        lax.dynamic_slice_in_dim(totals[2], win_index * shard_rows, shard_rows, 0),
        lax.dynamic_slice_in_dim(totals[3], win_index * ff_rows, ff_rows, 0),
        lax.dynamic_slice_in_dim(totals[4], win_index * vec_rows, vec_rows, 0),
    )
    new_qkv_mom = MOMENTUM_DECAY * qkv_mom + shares[0]
    new_out_mom = MOMENTUM_DECAY * out_mom + shares[1]
    new_up_mom = MOMENTUM_DECAY * up_mom + shares[2]
    new_down_mom = MOMENTUM_DECAY * down_mom + shares[3]
    new_vec_mom = MOMENTUM_DECAY * vec_mom + shares[4]
    new_vectors = (
        lax.dynamic_slice_in_dim(vectors.reshape(-1), win_index * vec_rows, vec_rows)
        - VECTOR_RATE * new_vec_mom
    )
    gathered = (
        lax.all_gather(new_qkv_mom.astype(jnp.bfloat16), "win", axis=1, tiled=True).astype(
            new_qkv_mom.dtype
        ),
        lax.all_gather(new_out_mom.astype(jnp.bfloat16), "win", axis=0, tiled=True).astype(
            new_out_mom.dtype
        ),
        lax.all_gather(new_up_mom.astype(jnp.bfloat16), "win", axis=0, tiled=True).astype(
            new_up_mom.dtype
        ),
        lax.all_gather(new_down_mom.astype(jnp.bfloat16), "win", axis=0, tiled=True).astype(
            new_down_mom.dtype
        ),
    )
    rep_count = lax.axis_size("rep")
    matrices = [
        gathered[0][0],
        gathered[0][1],
        gathered[0][2],
        gathered[1],
        gathered[2],
        gathered[3],
    ]
    row_counts = [shard_rows, shard_rows, shard_rows, shard_rows, shard_rows, ff_rows]
    updates = [
        owner_update(matrix, number % rep_count, rep_index, row_counts[number], win_index)
        for number, matrix in enumerate(matrices)
    ]

    def own_rows(matrix, rows_here):
        return lax.dynamic_slice_in_dim(matrix, win_index * rows_here, rows_here, 0)

    new_qkv = jnp.stack(
        [
            own_rows(qkv_weight[number], shard_rows).astype(jnp.float32)
            - MATRIX_RATE * updates[number]
            for number in range(3)
        ]
    )
    new_out = own_rows(out_weight, shard_rows).astype(jnp.float32) - MATRIX_RATE * updates[3]
    new_up = own_rows(up_weight, shard_rows).astype(jnp.float32) - MATRIX_RATE * updates[4]
    new_down = own_rows(down_weight, ff_rows).astype(jnp.float32) - MATRIX_RATE * updates[5]
    out_tokens = bfloat(output.reshape(1, windows, seq_len, model_width))
    return (
        out_tokens,
        input_grad[None],
        new_qkv_mom,
        new_qkv,
        new_out_mom,
        new_out,
        new_up_mom,
        new_up,
        new_down_mom,
        new_down,
        new_vec_mom,
        new_vectors,
    )


def solution(mesh):
    placed = (
        P("rep", "win", None, None),
        P("rep", "win", None),
        P("rep", "win", None),
        P("rep", None),
        P(),
        P(),
        P(),
        P(),
        P(),
        P(None, "win", None),
        P("win", None),
        P("win", None),
        P("win", None),
        P("win"),
        P("rep", "win", None, None),
    )
    return jax.shard_map(
        local,
        mesh=mesh,
        in_specs=placed,
        out_specs=(
            P("rep", "win", None, None),
            P("rep", "win", None, None),
            P(None, "win", None),
            P(None, "win", None),
            P("win", None),
            P("win", None),
            P("win", None),
            P("win", None),
            P("win", None),
            P("win", None),
            P("win"),
            P("win"),
        ),
        check_vma=False,
    )
```

profile of v0, /device:TPU:0, one launch (start us, length us, event | category | flops | bytes accessed | tf_op | source)
XLA Modules:
  0.0 1057.8 jit_solution(668958698392348489)
XLA Ops:
  19.5 24.2 %all-gather.1 = bf16[16,20,512]{2,1,0:T(8,128)(2,1)S(1)} all-gather(bf16[1,20,512]{2,1,0:T(8,128)(2,1)S(1)} %get-tuple-element.164), channel_id=1, replica_groups=mesh['win'=16,'rep'=2] {'win'}, dimensions={0}, use_global_device_ids=true | all-gather | bytes 348160 | tf_op jit(solution)/shard_map/all_gather | solution.py:139
  43.7 18.5 %all-gather = bf16[16,20,512]{2,1,0:T(8,128)(2,1)S(1)} all-gather(bf16[1,20,512]{2,1,0:T(8,128)(2,1)S(1)} %get-tuple-element.165), channel_id=1, replica_groups=mesh['win'=16,'rep'=2] {'win'}, dimensions={0}, use_global_device_ids=true | all-gather | bytes 348160 | tf_op jit(solution)/shard_map/all_gather | solution.py:140
  141.0 10.2 fusion.161
  171.4 8.8 convert_reduce_fusion
  200.9 8.5 convert_bitcast_fusion
  209.4 7.5 multiply_reduce_fusion.6
  216.9 10.9 %multiply_convert_fusion = bf16[20,16,50,50]{2,3,1,0:T(8,128)(2,1)} fusion(f32[20,16,50,50]{2,3,1,0:T(8,128)} %get-tuple-element.193, f32[20,16,50]{2,1,0:T(8,128)S(1)} %get-tuple-element.192, f32[20,16,50,50]{2,3,1,0:T(8,128)} %get-tuple-element.186, f32[20,16,50]{2,1,0:T(8,128)S(1)} %get-tuple-element.185), kind=kLoop, calls=%fused_computation.143 | loop fusion | flops 3200000 | bytes 8128000 | tf_op jit(solution)/shard_map/convert_element_type | solution.py:25
  227.9 7.2 fusion.75
  305.2 71.7 %all-reduce.12.cloned.1.call-done = (bf16[320,512]{0,1:T(8,128)(2,1)}, bf16[320,512]{0,1:T(8,128)(2,1)}) async-done(((bf16[320,512]{0,1:T(8,128)(2,1)}, bf16[320,512]{0,1:T(8,128)(2,1)}), (bf16[320,512]{0,1:T(8,128)(2,1)}, bf16[320,512]{0,1:T(8,128)(2,1)})) %all-reduce.12.cloned.1.call-update) | async-done | bytes 655376
  379.2 8.6 convert_reduce_fusion.1
  392.3 231.0 %all-reduce.10.cloned.1.call-done = (f32[3,512,512]{2,1,0:T(8,128)}, f32[512,512]{1,0:T(8,128)}, f32[512,2048]{1,0:T(8,128)}, f32[2048,512]{1,0:T(8,128)}) async-done(((f32[3,512,512]{2,1,0:T(8,128)}, f32[512,512]{1,0:T(8,128)}, f32[512,2048]{1,0:T(8,128)}, f32[2048,512]{1,0:T(8,128)}), (f32[3,512,512]{2,1,0:T(8,128)}, f32[512,512]{1,0:T(8,128)}, f32[512,2048]{1,0:T(8,128)}, ...) | async-done | bytes 12582928 | tf_op jit(solution)/shard_map/psum | solution.py:271
  630.2 22.5 %all_gather.21 = bf16[512,512]{1,0:T(8,128)(2,1)S(1)} all-gather(bf16[32,512]{1,0:T(8,128)(2,1)S(1)} %get-tuple-element.140), channel_id=1, replica_groups=mesh['win'=16,'rep'=2] {'win'}, dimensions={0}, use_global_device_ids=true | all-gather | bytes 557056 | tf_op jit(solution)/shard_map/all_gather | solution.py:294
  652.8 8.9 conditional.9
  668.7 9.4 conditional.7
  678.1 31.1 %conditional.8 = (bf16[512,512]{1,0:T(8,128)(2,1)}) conditional(s32[]{:T(128)} %convert_element_type.325, () %tuple.58, f32[3,512,512]{2,1,0:T(8,128)S(1)} %convert_element_type.327), branch_computations={%region_29.30_spmd, %region_30.32_spmd} | conditional | flops 24167317504 | bytes 38274084 | solution.py:94
  709.1 30.3 %conditional.6 = (bf16[512,512]{1,0:T(8,128)(2,1)S(1)}) conditional(s32[]{:T(128)} %convert_element_type.325, () %tuple.56, f32[3,512,512]{2,1,0:T(8,128)S(1)} %convert_element_type.327), branch_computations={%region_21.22_spmd, %region_22.24_spmd} | conditional | flops 24167317504 | bytes 38274084 | solution.py:94
  758.0 88.2 %conditional.10 = (bf16[512,2048]{1,0:T(8,128)(2,1)S(1)}) conditional(s32[]{:T(128)} %convert_element_type.325, () %tuple.60, f32[512,2048]{1,0:T(8,128)} %convert_element_type.344), branch_computations={%region_39.40_spmd, %region_40.42_spmd} | conditional | flops 72498282496 | bytes 102760520 | solution.py:94
  762.5 10.0 fusion.34
  806.4 7.4 multiply_add_fusion.1
  822.5 7.1 multiply_add_fusion
  829.7 7.1 fusion.182
  838.7 7.2 add_convert_fusion
  868.6 80.1 %psum.87 = f32[7168]{0:T(1024)S(1)} all-reduce(f32[7168]{0:T(1024)S(1)} %reshape.409), channel_id=1, replica_groups=mesh['win'=16,'rep'=2] {'win','rep'}, use_global_device_ids=true, to_apply=%region_59.60 | all-reduce | flops 7168 | bytes 57344 | tf_op jit(solution)/shard_map/psum | solution.py:271
  949.3 94.3 %all-reduce.14.cloned.1.call-done = (bf16[512,512]{1,0:T(8,128)(2,1)}, bf16[512,512]{1,0:T(8,128)(2,1)}, bf16[512,512]{1,0:T(8,128)(2,1)}, bf16[512,512]{1,0:T(8...) async-done(((bf16[512,512]{1,0:T(8,128)(2,1)}, bf16[512,512]{1,0:T(8,128)(2,1)}, bf16[512,512]{1,0:T(8,128)(2,1)}, bf16[512,512]{1,0:T(8,128)(2,1)}, ...) | async-done | bytes 6291472 | tf_op jit(solution)/shard_map/psum | solution.py:21
  (418 shorter events, 379.4 us)
Async XLA Ops:
  7.2 369.8 %all-reduce.12.cloned.1.call-start = ((), (), s32[]{:S(2)}) async-start(), calls=%async_computation.4 | async-start | bytes 1572864
  10.2 63.0 %copy-start.66 = (f32[1,512]{1,0:T(1,128)}, f32[1,512]{1,0:T(1,128)S(1)}, u32[]{:S(2)}) copy-start(f32[1,512]{1,0:T(1,128)S(1)} %get-tuple-element.173) | copy-start | bytes 6148
  14.2 59.1 %copy-start.71 = (f32[20]{0:T(128)}, f32[20]{0:T(128)S(1)}, u32[]{:S(2)}) copy-start(f32[20]{0:T(128)S(1)} %get-tuple-element.182) | copy-start | bytes 244
  19.5 50.8 %copy-start.50 = (bf16[20,16,32]{2,1,0:T(8,128)(2,1)}, bf16[20,16,32]{2,1,0:T(8,128)(2,1)S(1)}, u32[]{:S(2)}) copy-start(bf16[20,16,32]{2,1,0:T(8,128)(2,1)S(1)} %reshape.389) | copy-start | bytes 61444
  75.4 14.4 %copy-start.21 = (bf16[1,20,50,512]{3,2,1,0:T(8,128)(2,1)S(1)}, bf16[1,20,50,512]{3,2,1,0:T(8,128)(2,1)}, u32[]{:S(2)}) copy-start(bf16[1,20,50,512]{3,2,1,0:T(8,128)(2,1)} %param.41) | copy-start | bytes 3072004
  115.4 25.5 %copy-start.14 = (bf16[20,50,16,32]{1,3,2,0:T(8,128)(2,1)}, bf16[20,50,16,32]{1,3,2,0:T(8,128)(2,1)S(1)}, u32[]{:S(2)}) copy-start(bf16[20,50,16,32]{1,3,2,0:T(8,128)(2,1)S(1)} %copy.191) | copy-start | bytes 3072004
  164.6 121.5 %copy-start = (f32[1000,512]{1,0:T(8,128)}, f32[1000,512]{1,0:T(8,128)S(1)}, u32[]{:S(2)}) copy-start(f32[1000,512]{1,0:T(8,128)S(1)} %get-tuple-element.188) | copy-start | bytes 6144004
  281.5 21.2 %copy-start.34 = (f32[20,1,512]{2,1,0:T(1,128)}, f32[20,1,512]{2,1,0:T(1,128)S(1)}, u32[]{:S(2)}) copy-start(f32[20,1,512]{2,1,0:T(1,128)S(1)} %slice.162) | copy-start | bytes 122884
  285.8 337.5 %all-reduce.10.cloned.1.call-start = ((), (), s32[]{:S(2)}) async-start(), calls=%async_computation.3 | async-start | bytes 25165824 | tf_op jit(solution)/shard_map/psum | solution.py:271
  299.3 79.8 %copy-start.18 = (bf16[1000,1536]{0,1:T(8,128)(2,1)S(1)}, bf16[1000,1536]{0,1:T(8,128)(2,1)}, u32[]{:S(2)}) copy-start(bf16[1000,1536]{0,1:T(8,128)(2,1)} %copy-done.17) | copy-start | bytes 9216004
  301.4 86.4 %copy-start.46 = (bf16[1,20,16,32]{1,3,2,0:T(8,128)(2,1)}, bf16[1,20,16,32]{1,3,2,0:T(8,128)(2,1)S(1)}, u32[]{:S(2)}) copy-start(bf16[1,20,16,32]{1,3,2,0:T(8,128)(2,1)S(1)} %copy.224) | copy-start | bytes 61444
  378.0 9.8 copy-start.47
  379.1 8.7 copy-start.48
  379.1 8.7 copy-start.31
  392.2 231.1 %copy-start.56 = (f32[3,32,512]{2,1,0:T(8,128)S(1)}, f32[3,32,512]{2,1,0:T(8,128)}, u32[]{:S(2)}) copy-start(f32[3,32,512]{2,1,0:T(8,128)} %param.36) | copy-start | bytes 589828
  392.2 232.9 %copy-start.52 = (f32[128,512]{1,0:T(8,128)S(1)}, f32[128,512]{1,0:T(8,128)}, u32[]{:S(2)}) copy-start(f32[128,512]{1,0:T(8,128)} %param.39) | copy-start | bytes 786436
  392.2 234.7 %copy-start.53 = (f32[32,2048]{1,0:T(8,128)S(1)}, f32[32,2048]{1,0:T(8,128)}, u32[]{:S(2)}) copy-start(f32[32,2048]{1,0:T(8,128)} %param.38) | copy-start | bytes 786436
  392.2 236.5 %copy-start.58 = (f32[32,512]{1,0:T(8,128)S(1)}, f32[32,512]{1,0:T(8,128)}, u32[]{:S(2)}) copy-start(f32[32,512]{1,0:T(8,128)} %param.37) | copy-start | bytes 196612
  392.2 274.6 %all-gather.6.cloned.1.call-start = ((), (), s32[]{:S(2)}) async-start(), calls=%async_computation | async-start | bytes 1671168 | tf_op jit(solution)/shard_map/all_gather | solution.py:291
  625.0 118.1 %all-gather.10.cloned.1.call-start = ((), (), s32[]{:S(2)}) async-start(), calls=%async_computation.2 | async-start | bytes 2228224 | tf_op jit(solution)/shard_map/all_gather | solution.py:300
  626.8 127.1 %all-gather.8.cloned.1.call-start = ((), (), s32[]{:S(2)}) async-start(), calls=%async_computation.1 | async-start | bytes 2228224 | tf_op jit(solution)/shard_map/all_gather | solution.py:297
  628.6 414.9 %all-reduce.14.cloned.1.call-start = ((), (), s32[]{:S(2)}) async-start(), calls=%async_computation.5 | async-start | bytes 12582912 | tf_op jit(solution)/shard_map/psum | solution.py:21
  762.5 12.0 %copy-start.10 = (f32[512,2048]{1,0:T(8,128)S(1)}, f32[512,2048]{1,0:T(8,128)}, u32[]{:S(2)}) copy-start(f32[512,2048]{1,0:T(8,128)} %param.9) | copy-start | bytes 12582916 | tf_op jit(solution)/shard_map/cond
  865.1 83.5 %copy-start.97 = (f32[448]{0:T(512)S(1)}, f32[448]{0:T(512)}, u32[]{:S(2)}) copy-start(f32[448]{0:T(512)} %param.40) | copy-start | bytes 5380
  (85 other events, 326.4 us)
Sparse Core Ops, SparseCore 0:
  285.9 91.0 all-reduce.11
  392.3 230.9 all-reduce.9
  626.3 40.4 all-gather.5
  669.1 40.2 all-gather.9
  711.7 40.1 all-gather.7
  847.8 195.7 all-reduce.13
where the time goes:
time: 1060 us
  waiting for transfers between devices  401 us (38%)
  matrix products  248 us (23%)
  local copies, waits for them, and re-layouts  147 us (14%)
  blocking collectives  145 us (14%)
  other arithmetic  75.7 us (7%)
  loops' own time  24.3 us (2%)
  between operations  16.4 us (2%)
    psum x1, waiting for transfers between devices, local(): lax.psum((gradients[0], gradients[1], gradients[2], gradients[3], gradien...  231 us
    psum x1, waiting for transfers between devices, broadcast(): return lax.psum(jnp.where(mine, array, jnp.zeros_like(array)), axis)  94.3 us
    psum x1, blocking collectives, local(): lax.psum((gradients[0], gradients[1], gradients[2], gradients[3], gradien...  80.1 us
    unnamed x7, waiting for transfers between devices  71.8 us
    dot_general x15, matrix products, newton(): gram_matrix = jnp.matmul(iterate, iterate.T, precision=HIGHEST)  57.6 us
    dot_general x19, matrix products, product(): return jnp.dot(left_side, right_side, preferred_element_type=jnp.float32)  57.3 us
    dot_general x15, matrix products, newton(): jnp.matmul(polynomial, iterate, precision=HIGHEST)  54.8 us
    dot_general x15, matrix products, newton(): jnp.matmul(gram_matrix, gram_matrix, precision=HIGHEST)  28.3 us
  transfers between devices with their start and end apart: 6, of which 4 were waited for; matrix products, arithmetic and copies ran while one was open for 11% of the time, Pallas kernels for 0%

commit v1 on v0

v1 whole, which is shorter than its diff:
```python
import functools

import jax
import jax.numpy as jnp
from jax import lax
from jax.experimental import pallas as pl
from jax.experimental.pallas import tpu as pltpu
from jax.sharding import PartitionSpec as P

HEADS = 16
HEAD_DIM = 32


EPSILON = 1e-06
MOMENTUM_DECAY = 0.95
MATRIX_RATE = 0.5
VECTOR_RATE = 0.0002
KEEP_SHARE = 0.75
NEWTON_COEFFS = (3.4445, -4.775, 2.0315)


def bfloat(values):
    return values.astype(jnp.bfloat16)


def product(left_side, right_side):
    return jnp.dot(left_side, right_side, preferred_element_type=jnp.float32)


def norm_rows(values, gain_row, shift_row):
    center = values - jnp.mean(values, -1, keepdims=True)
    spread = jnp.mean(center * center, -1, keepdims=True)
    return center * lax.rsqrt(spread + EPSILON) * gain_row + shift_row


def bit_count(axis):
    return lax.axis_size(axis).bit_length() - 1


def swap(values, axis, bit):
    size = lax.axis_size(axis)
    return lax.ppermute(values, axis, [(i, i ^ (1 << bit)) for i in range(size)])


def my_bit(axis, bit):
    return (lax.axis_index(axis) >> bit) & 1


def gather_blocks(values, axis):
    done = []
    for bit in list(range(2, bit_count(axis))) + [1, 0]:
        other = swap(values, axis, bit)
        first = my_bit(axis, bit) == 0
        place = sum(1 for earlier in done if earlier > bit)
        values = jnp.stack(
            [jnp.where(first, values, other), jnp.where(first, other, values)], axis=place
        )
        done.append(bit)
    return values.reshape((lax.axis_size(axis),) + values.shape[len(done) :])


def halve_blocks(values, bit, bits_left):
    place = bits_left.index(bit)
    split = values.reshape((2,) * len(bits_left) + values.shape[1:])
    mine = my_bit("win", bit)
    kept = lax.dynamic_index_in_dim(split, mine, place, keepdims=False)
    sent = lax.dynamic_index_in_dim(split, 1 - mine, place, keepdims=False)
    total = kept + swap(bfloat(sent), "win", bit).astype(jnp.float32)
    left = [other for other in bits_left if other != bit]
    return total.reshape((-1,) + values.shape[1:]), left


def halve_columns(values):
    for bit in range(bit_count("rep")):
        half = values.shape[-1] // 2
        last = values.ndim - 1
        mine = my_bit("rep", bit)
        kept = lax.dynamic_slice_in_dim(values, mine * half, half, last)
        sent = lax.dynamic_slice_in_dim(values, (1 - mine) * half, half, last)
        values = kept + swap(bfloat(sent), "rep", bit).astype(jnp.float32)
    return values


def join_columns(values):
    values = bfloat(values)
    for bit in reversed(range(bit_count("rep"))):
        other = swap(values, "rep", bit)
        first = my_bit("rep", bit) == 0
        values = jnp.concatenate(
            [jnp.where(first, values, other), jnp.where(first, other, values)], axis=-1
        )
    return values.astype(jnp.float32)


def scatter_pair(first, second):
    bits = list(range(1, bit_count("win")))[::-1]
    first, left = halve_blocks(halve_columns(first), 1, bits)
    second = halve_columns(halve_blocks(second, 1, bits)[0])
    values = jnp.concatenate([first, second], axis=1)
    for bit in sorted(left):
        values, left = halve_blocks(values, bit, left)
    return join_columns(values)[0]


def sum_over_rep(values):
    for bit in range(bit_count("rep")):
        low = bfloat(values)
        values = low.astype(jnp.float32) + swap(low, "rep", bit).astype(jnp.float32)
    return values


def off_diagonal_step(iterate, exact):
    high = bfloat(iterate)
    gram = dot_as(high, high, NT)
    if exact:
        rest = bfloat(iterate - high.astype(jnp.float32))
        gram = gram + dot_as(high, rest, NT) + dot_as(rest, high, NT)
    size = gram.shape[0]
    row_ids = lax.broadcasted_iota(jnp.int32, (size, size), 0)
    on_diagonal = row_ids == lax.broadcasted_iota(jnp.int32, (size, size), 1)
    own = jnp.where(on_diagonal, gram, 0.0)
    own_column = jnp.sum(own, 1, keepdims=True)
    own_row = jnp.sum(own, 0, keepdims=True)
    off = jnp.where(on_diagonal, 0.0, gram)
    off_low = bfloat(off)
    square = product(off_low, off_low) + (own_column + own_row) * off
    poly = NEWTON_COEFFS[1] * off + NEWTON_COEFFS[2] * square
    poly_own = jnp.sum(jnp.where(on_diagonal, poly, 0.0), 1, keepdims=True)
    factor = (
        NEWTON_COEFFS[0]
        + poly_own
        + own_column * (NEWTON_COEFFS[1] + NEWTON_COEFFS[2] * own_column)
    )
    poly = jnp.where(on_diagonal, 0.0, poly)
    poly_high = bfloat(poly)
    moved = product(poly_high, high)
    if exact:
        poly_rest = bfloat(poly - poly_high.astype(jnp.float32))
        moved = moved + product(poly_high, rest) + product(poly_rest, high)
    return factor * iterate + moved


def unit_scale(values):
    total = jnp.sum(jnp.sum(values * values, 1, keepdims=True), 0, keepdims=True)
    return values * (1.0 / (jnp.sqrt(total) + EPSILON))


def big_newton_kernel(folds, place_ref, blocks_ref, out_ref, iterate_ref, turned_ref):
    blocks, rows, width = blocks_ref.shape
    part = rows // folds

    @pl.when(place_ref[0] == 0)
    def _():
        for block in range(blocks):
            for fold in range(folds):
                iterate_ref[
                    block * part : (block + 1) * part, fold * width : (fold + 1) * width
                ] = blocks_ref[block, fold * part : (fold + 1) * part, :].astype(jnp.float32)

    @pl.when(place_ref[0] != 0)
    def _():
        for block in range(blocks):
            iterate_ref[:, block * rows : (block + 1) * rows] = blocks_ref[block].astype(
                jnp.float32
            ).T

    iterate_ref[...] = unit_scale(iterate_ref[...])

    @pl.loop(0, 5)
    def _(_):
        iterate_ref[...] = off_diagonal_step(iterate_ref[...], False)

    @pl.when(place_ref[0] == 0)
    def _():
        start = pl.multiple_of(place_ref[1] * part, part)
        for fold in range(folds):
            out_ref[fold * part : (fold + 1) * part, :] = bfloat(
                iterate_ref[pl.ds(start, part), fold * width : (fold + 1) * width]
            )

    @pl.when(place_ref[0] != 0)
    def _():
        span = max(rows, 128)
        start = pl.multiple_of(place_ref[1] * rows // span * span, span)
        turned_ref[...] = iterate_ref[:, pl.ds(start, span)].T * float(folds) ** 0.5
        inner = pl.multiple_of(place_ref[1] * rows - start, rows)
        out_ref[...] = bfloat(turned_ref[pl.ds(inner, rows), :])


def small_newton_kernel(place_ref, blocks_ref, out_ref, iterate_ref):
    blocks, matrices, rows, width = blocks_ref.shape
    for number in range(matrices):
        for block in range(blocks):
            iterate_ref[number, block * rows : (block + 1) * rows, :] = blocks_ref[
                block, number
            ].astype(jnp.float32)

    @pl.loop(0, matrices)
    def _(number):
        iterate_ref[number] = unit_scale(iterate_ref[number])

        @pl.loop(0, 2)
        def _(_):
            iterate_ref[number] = off_diagonal_step(iterate_ref[number], False)

        @pl.loop(0, 3)
        def _(_):
            iterate_ref[number] = off_diagonal_step(iterate_ref[number], True)

    start = pl.multiple_of(place_ref[1] * rows, rows)
    for number in range(matrices):
        out_ref[number] = bfloat(iterate_ref[number, pl.ds(start, rows), :])


def newton_call(kernel, name, place, blocks, out_dims, scratch_dims, flops):
    return pl.pallas_call(
        kernel,
        in_specs=[
            pl.BlockSpec(memory_space=pltpu.SMEM),
            pl.BlockSpec(memory_space=pltpu.VMEM),
        ],
        out_specs=pl.BlockSpec(memory_space=pltpu.VMEM),
        out_shape=shape_of(out_dims, jnp.bfloat16),
        scratch_shapes=[pltpu.VMEM(dims, jnp.float32) for dims in scratch_dims],
        compiler_params=pltpu.CompilerParams(vmem_limit_bytes=VMEM_LIMIT),
        cost_estimate=pl.CostEstimate(
            flops=flops, bytes_accessed=2 * blocks.size, transcendentals=0
        ),
        name=name,
    )(place, blocks)


def big_update(place, blocks, folds):
    win, rows, width = blocks.shape
    return newton_call(
        functools.partial(big_newton_kernel, folds),
        "big_newton",
        place,
        blocks,
        (rows, width),
        [(width, win * rows), (max(rows, 128), width)],
        2 * 5 * width * width * (2 * win * rows + width),
    )


def small_update(place, blocks):
    win, matrices, rows, width = blocks.shape
    return newton_call(
        small_newton_kernel,
        "small_newton",
        place,
        blocks,
        (matrices, rows, width),
        [(matrices, width, width)],
        2 * 27 * matrices * width**3,
    )


def own_rows(matrix, rows_here):
    return lax.dynamic_slice_in_dim(matrix, lax.axis_index("win") * rows_here, rows_here, 0)


def own_block(values):
    return lax.dynamic_index_in_dim(values, lax.axis_index("win"), 0, keepdims=False)


def fold_columns(rows, width):
    count, columns = rows.shape
    return rows.reshape(count, columns // width, width).swapaxes(0, 1).reshape(-1, width)


def unfold_columns(rows, folds):
    total, width = rows.shape
    return rows.reshape(folds, total // folds, width).swapaxes(0, 1).reshape(-1, folds * width)


def pick_owner(first, here, there):
    return jnp.where(first, here, there), jnp.where(first, there, here)


def big_updates(up_folded, down_rows, folds):
    win_index = lax.axis_index("win")
    rep_index = lax.axis_index("rep")
    if lax.axis_size("rep") == 2:
        first = rep_index == 0
        place = jnp.stack([rep_index, win_index]).astype(jnp.int32)
        blocks = gather_blocks(bfloat(jnp.where(first, up_folded, down_rows)), "win")
        mine = big_update(place, blocks, folds)
        return pick_owner(first, mine, swap(mine, "rep", 0))
    updates = []
    for number, rows in enumerate([up_folded, down_rows]):
        place = jnp.stack([jnp.int32(number), win_index]).astype(jnp.int32)
        updates.append(big_update(place, gather_blocks(bfloat(rows), "win"), folds))
    return updates


def small_updates(rows):
    win_index = lax.axis_index("win")
    rep_index = lax.axis_index("rep")
    place = jnp.stack([rep_index, win_index]).astype(jnp.int32)
    if lax.axis_size("rep") == 2:
        first = rep_index == 0
        blocks = gather_blocks(bfloat(jnp.where(first, rows[:2], rows[2:])), "win")
        mine = small_update(place, blocks)
        return jnp.concatenate(pick_owner(first, mine, swap(mine, "rep", 0)))
    return small_update(place, gather_blocks(bfloat(rows), "win"))


GROUP_HEADS = 128 // HEAD_DIM
SCORE_SCALE = HEAD_DIM ** (-0.5)
LOG2_E = 1.4426950408889634
VMEM_LIMIT = 48 * 1024 * 1024
NT = (((1,), (1,)), ((), ()))
TN = (((0,), (0,)), ((), ()))


def dot_as(left_side, right_side, dims):
    return lax.dot_general(left_side, right_side, dims, preferred_element_type=jnp.float32)


def spread_heads(part, lane_head):
    return bfloat(
        jnp.concatenate(
            [jnp.where(lane_head == head, part, 0.0) for head in range(GROUP_HEADS)], axis=0
        )
    )


def join_heads(spread, lane_head, rows):
    joined = spread[:rows]
    for head in range(1, GROUP_HEADS):
        joined = jnp.where(lane_head == head, spread[head * rows : (head + 1) * rows], joined)
    return joined


def column_softmax(scores, bias_column):
    scores = scores + bias_column
    raised = jnp.exp2((scores - jnp.max(scores, 0, keepdims=True)) * (SCORE_SCALE * LOG2_E))
    return raised * (1.0 / jnp.sum(raised, 0, keepdims=True))


def load_windows(tokens_ref, region_ref, fill_ref, count, seq_len, padded, step):
    for window in range(count):
        base = window * padded
        fill_ref[base : base + seq_len, :] = tokens_ref[0, window].astype(jnp.float32)
        fill_ref[base : base + 1, :] = region_ref[pl.ds(step * count + window, 1), :]


def window_forward_kernel(
    count,
    seq_len,
    padded,
    tokens_ref,
    region_ref,
    bias_ref,
    keep_ref,
    qkv_ref,
    out_ref,
    vec_ref,
    norm_out,
    proj_out,
    mix_out,
    after_out,
    fill_ref,
    mix_ref,
):
    step = pl.program_id(0)
    width = tokens_ref.shape[-1]

    @pl.when(step == 0)
    def _():
        fill_ref[...] = jnp.zeros_like(fill_ref)

    load_windows(tokens_ref, region_ref, fill_ref, count, seq_len, padded, step)
    flat = fill_ref[...]
    normed = bfloat(norm_rows(flat, vec_ref[2:3, :], vec_ref[3:4, :]))
    lane_head = lax.broadcasted_iota(jnp.int32, (padded, 128), 1) // HEAD_DIM
    proj = product(normed, qkv_ref[...])
    query = proj[:, :width] + vec_ref[6:7, :]
    keyset = proj[:, width : 2 * width]
    values = proj[:, 2 * width :] + vec_ref[7:8, :]
    for window in range(count):
        rows = slice(window * padded, (window + 1) * padded)
        norm_out[window] = normed[rows]
        bias_column = bias_ref[window]
        for group in range(width // 128):
            lanes = slice(group * 128, (group + 1) * 128)
            spread = spread_heads(query[rows, lanes], lane_head)
            key_low = bfloat(keyset[rows, lanes])
            value_low = bfloat(values[rows, lanes])
            probs = column_softmax(dot_as(key_low, spread, NT), bias_column)
            mixed = dot_as(bfloat(probs), value_low, TN)
            mix_ref[rows, lanes] = join_heads(mixed, lane_head, padded)
            proj_out[window, :, lanes] = bfloat(query[rows, lanes])
            proj_out[window, :, width + group * 128 : width + (group + 1) * 128] = key_low
            proj_out[window, :, 2 * width + group * 128 : 2 * width + (group + 1) * 128] = value_low
    mixed_low = bfloat(mix_ref[...])
    branch = product(mixed_low, out_ref[...]) + vec_ref[8:9, :]
    for window in range(count):
        rows = slice(window * padded, (window + 1) * padded)
        mix_out[window] = mixed_low[rows]
        after_out[window] = flat[rows] + keep_ref[window] * branch[rows]


def window_backward_kernel(
    count,
    seq_len,
    padded,
    tokens_ref,
    region_ref,
    bias_ref,
    keep_ref,
    qkv_ref,
    out_ref,
    vec_ref,
    proj_ref,
    after_grad_ref,
    region_keep_ref,
    grad_out,
    region_grad_out,
    proj_grad_out,
    branch_grad_out,
    sums_out,
    region_branch_out,
    region_mix_out,
    fill_ref,
    proj_grad_ref,
):
    step = pl.program_id(0)
    width = tokens_ref.shape[-1]

    @pl.when(step == 0)
    def _():
        fill_ref[...] = jnp.zeros_like(fill_ref)
        sums_out[...] = jnp.zeros_like(sums_out)
        region_grad_out[...] = jnp.zeros_like(region_grad_out)

    load_windows(tokens_ref, region_ref, fill_ref, count, seq_len, padded, step)
    lane_head = lax.broadcasted_iota(jnp.int32, (padded, 128), 1) // HEAD_DIM
    branch_grad = bfloat(
        jnp.concatenate(
            [keep_ref[window] * after_grad_ref[window] for window in range(count)], axis=0
        )
    )
    mix_grad = dot_as(branch_grad, out_ref[...], NT)
    for window in range(count):
        rows = slice(window * padded, (window + 1) * padded)
        branch_grad_out[window] = branch_grad[rows]
        bias_column = bias_ref[window]
        for group in range(width // 128):
            lanes = slice(group * 128, (group + 1) * 128)
            key_lanes = slice(width + group * 128, width + (group + 1) * 128)
            value_lanes = slice(2 * width + group * 128, 2 * width + (group + 1) * 128)
            spread = spread_heads(proj_ref[window, :, lanes].astype(jnp.float32), lane_head)
            key_low = proj_ref[window, :, key_lanes]
            value_low = proj_ref[window, :, value_lanes]
            spread_grad = spread_heads(mix_grad[rows, lanes], lane_head)
            probs = column_softmax(dot_as(key_low, spread, NT), bias_column)
            probs_grad = dot_as(value_low, spread_grad, NT)
            weighted = probs * probs_grad
            score_grad = bfloat(weighted - probs * jnp.sum(weighted, 0, keepdims=True))
            value_grad = product(bfloat(probs), spread_grad)
            key_grad = product(score_grad, spread) * SCORE_SCALE
            query_grad = join_heads(dot_as(score_grad, key_low, TN), lane_head, padded)
            proj_grad_ref[rows, lanes] = query_grad * SCORE_SCALE
            proj_grad_ref[rows, key_lanes] = key_grad
            proj_grad_ref[rows, value_lanes] = value_grad
    proj_grad = bfloat(proj_grad_ref[...])
    norm_grad = dot_as(proj_grad, qkv_ref[...], NT)
    flat = fill_ref[...]
    center = flat - jnp.mean(flat, -1, keepdims=True)
    scale = lax.rsqrt(jnp.mean(center * center, -1, keepdims=True) + EPSILON)
    hat = center * scale
    hat_grad = norm_grad * vec_ref[2:3, :]
    flat_grad = scale * (
        hat_grad
        - jnp.mean(hat_grad, -1, keepdims=True)
        - hat * jnp.mean(hat_grad * hat, -1, keepdims=True)
    )
    sums_out[0:1, :width] += jnp.sum(norm_grad * hat, 0, keepdims=True)
    sums_out[1:2, :width] += jnp.sum(norm_grad, 0, keepdims=True)
    sums_out[2:3, :width] += jnp.sum(branch_grad.astype(jnp.float32), 0, keepdims=True)
    sums_out[3:4, :] += jnp.sum(proj_grad.astype(jnp.float32), 0, keepdims=True)
    for window in range(count):
        rows = slice(window * padded, (window + 1) * padded)
        proj_grad_out[window] = proj_grad[rows]
        seq_grad = after_grad_ref[window] + flat_grad[rows]
        grad_out[0, window] = seq_grad[:seq_len]
        region_grad_out[pl.ds(step * count + window, 1), :] = seq_grad[0:1]

    @pl.when(step == pl.num_programs(0) - 1)
    def _():
        region_branch = bfloat(region_keep_ref[...] * region_grad_out[...])
        sums_out[2:3, :width] += jnp.sum(region_branch.astype(jnp.float32), 0, keepdims=True)
        region_branch_out[...] = region_branch
        region_mix_out[...] = bfloat(dot_as(region_branch, out_ref[...], NT))


def window_step(windows):
    return next(count for count in (4, 2, 1) if windows % count == 0)


def whole_spec(shape):
    return pl.BlockSpec(shape, lambda step: (0,) * len(shape))


def step_spec(count, *rest):
    return pl.BlockSpec((count,) + rest, lambda step: (step,) + (0,) * len(rest))


def token_spec(count, *rest):
    return pl.BlockSpec((1, count) + rest, lambda step: (0, step) + (0,) * len(rest))


def shape_of(dims, kind=jnp.float32):
    return jax.ShapeDtypeStruct(dims, kind)


def window_forward(tokens, region, bias, keep, qkv_flat, out_weight, vectors, padded):
    _, windows, seq_len, width = tokens.shape
    count = window_step(windows)
    return pl.pallas_call(
        functools.partial(window_forward_kernel, count, seq_len, padded),
        grid=(windows // count,),
        in_specs=[
            token_spec(count, seq_len, width),
            whole_spec(region.shape),
            step_spec(count, padded, 1),
            step_spec(count, 1, 1),
            whole_spec(qkv_flat.shape),
            whole_spec(out_weight.shape),
            whole_spec(vectors.shape),
        ],
        out_specs=[
            step_spec(count, padded, width),
            step_spec(count, padded, 3 * width),
            step_spec(count, padded, width),
            step_spec(count, padded, width),
        ],
        out_shape=[
            shape_of((windows, padded, width), jnp.bfloat16),
            shape_of((windows, padded, 3 * width), jnp.bfloat16),
            shape_of((windows, padded, width), jnp.bfloat16),
            shape_of((windows, padded, width)),
        ],
        scratch_shapes=[
            pltpu.VMEM((count * padded, width), jnp.float32),
            pltpu.VMEM((count * padded, width), jnp.float32),
        ],
        compiler_params=pltpu.CompilerParams(vmem_limit_bytes=VMEM_LIMIT),
        name="window_forward",
    )(tokens, region, bias, keep, qkv_flat, out_weight, vectors)


def window_backward(
    tokens, region, bias, keep, qkv_flat, out_weight, vectors, proj, after_grad, region_keep, padded
):
    _, windows, seq_len, width = tokens.shape
    count = window_step(windows)
    return pl.pallas_call(
        functools.partial(window_backward_kernel, count, seq_len, padded),
        grid=(windows // count,),
        in_specs=[
            token_spec(count, seq_len, width),
            whole_spec(region.shape),
            step_spec(count, padded, 1),
            step_spec(count, 1, 1),
            whole_spec(qkv_flat.shape),
            whole_spec(out_weight.shape),
            whole_spec(vectors.shape),
            step_spec(count, padded, 3 * width),
            step_spec(count, padded, width),
            whole_spec(region_keep.shape),
        ],
        out_specs=[
            token_spec(count, seq_len, width),
            whole_spec(region.shape),
            step_spec(count, padded, 3 * width),
            step_spec(count, padded, width),
            whole_spec((8, 3 * width)),
            whole_spec(region.shape),
            whole_spec(region.shape),
        ],
        out_shape=[
            shape_of(tokens.shape),
            shape_of(region.shape),
            shape_of((windows, padded, 3 * width), jnp.bfloat16),
            shape_of((windows, padded, width), jnp.bfloat16),
            shape_of((8, 3 * width)),
            shape_of(region.shape, jnp.bfloat16),
            shape_of(region.shape, jnp.bfloat16),
        ],
        scratch_shapes=[
            pltpu.VMEM((count * padded, width), jnp.float32),
            pltpu.VMEM((count * padded, 3 * width), jnp.float32),
        ],
        compiler_params=pltpu.CompilerParams(vmem_limit_bytes=VMEM_LIMIT),
        name="window_backward",
    )(tokens, region, bias, keep, qkv_flat, out_weight, vectors, proj, after_grad, region_keep)


def image_bias(keys_ref, queries_ref):
    return jnp.where(keys_ref[...] == queries_ref[...], 0.0, -1e30)


def region_forward_kernel(
    all_ref,
    own_ref,
    keep_ref,
    key_image_ref,
    query_image_ref,
    qkv_ref,
    out_ref,
    vec_ref,
    norm_out,
    proj_out,
    mix_out,
    new_out,
):
    rows, width = own_ref.shape
    vec = vec_ref[...]
    normed = bfloat(norm_rows(all_ref[...].astype(jnp.float32), vec[0:1], vec[1:2]))
    norm_out[...] = normed
    proj = product(normed, qkv_ref[...])
    query = bfloat(proj[:, :width] + vec[6:7])
    keyset = bfloat(proj[:, width : 2 * width])
    values = bfloat(proj[:, 2 * width :] + vec[7:8])
    proj_out[:, :width] = query
    proj_out[:, width : 2 * width] = keyset
    proj_out[:, 2 * width :] = values
    region = own_ref[...].astype(jnp.float32)
    own_norm = bfloat(norm_rows(region, vec[0:1], vec[1:2]))
    own_query = product(own_norm, qkv_ref[:, :width]) + vec[6:7]
    bias = image_bias(key_image_ref, query_image_ref)
    lane_head = lax.broadcasted_iota(jnp.int32, (rows, 128), 1) // HEAD_DIM
    parts = []
    for group in range(width // 128):
        lanes = slice(group * 128, (group + 1) * 128)
        spread = spread_heads(own_query[:, lanes], lane_head)
        probs = column_softmax(dot_as(keyset[:, lanes], spread, NT), bias)
        mixed = dot_as(bfloat(probs), values[:, lanes], TN)
        parts.append(join_heads(mixed, lane_head, rows))
    mixed_low = bfloat(jnp.concatenate(parts, axis=1))
    mix_out[...] = mixed_low
    branch = product(mixed_low, out_ref[...]) + vec[8:9]
    new_out[...] = region + keep_ref[...] * branch


def region_forward(all_rows, own_rows_, keep, key_images, query_images, qkv_flat, out_weight, vectors):
    total, width = all_rows.shape
    return pl.pallas_call(
        region_forward_kernel,
        out_shape=[
            shape_of((total, width), jnp.bfloat16),
            shape_of((total, 3 * width), jnp.bfloat16),
            shape_of(own_rows_.shape, jnp.bfloat16),
            shape_of(own_rows_.shape),
        ],
        compiler_params=pltpu.CompilerParams(vmem_limit_bytes=VMEM_LIMIT),
        name="region_forward",
    )(all_rows, own_rows_, keep, key_images, query_images, qkv_flat, out_weight, vectors)


def region_backward_kernel(
    place_ref,
    all_ref,
    norm_ref,
    proj_ref,
    mix_grad_ref,
    key_image_ref,
    query_image_ref,
    new_grad_ref,
    qkv_ref,
    vec_ref,
    grad_out,
    weight_out,
    sums_out,
    bias_ref,
    proj_grad_ref,
    region_grad_ref,
    weight_ref,
):
    total, width = all_ref.shape
    rows = new_grad_ref.shape[0]
    bias_ref[...] = image_bias(key_image_ref, query_image_ref)
    lane_head = lax.broadcasted_iota(jnp.int32, (total, 128), 1) // HEAD_DIM

    @pl.loop(0, width // 128)
    def _(group):
        query_lanes = pl.ds(pl.multiple_of(group * 128, 128), 128)
        key_lanes = pl.ds(pl.multiple_of(width + group * 128, 128), 128)
        value_lanes = pl.ds(pl.multiple_of(2 * width + group * 128, 128), 128)
        query = proj_ref[:, query_lanes]
        key_low = proj_ref[:, key_lanes]
        value_low = proj_ref[:, value_lanes]
        mix_grad = mix_grad_ref[:, query_lanes]
        zero = jnp.zeros((total, 128), jnp.float32)
        query_grad, key_grad, value_grad = zero, zero, zero
        for head in range(GROUP_HEADS):
            here = lane_head == head
            head_query = jnp.where(here, query, jnp.zeros_like(query))
            head_grad = jnp.where(here, mix_grad, jnp.zeros_like(mix_grad))
            probs = column_softmax(dot_as(key_low, head_query, NT), bias_ref[...])
            probs_grad = dot_as(value_low, head_grad, NT)
            weighted = probs * probs_grad
            score_grad = bfloat(weighted - probs * jnp.sum(weighted, 0, keepdims=True))
            value_grad += product(bfloat(probs), head_grad)
            key_grad += product(score_grad, head_query)
            query_grad = jnp.where(here, dot_as(score_grad, key_low, TN), query_grad)
        proj_grad_ref[:, query_lanes] = bfloat(query_grad * SCORE_SCALE)
        proj_grad_ref[:, key_lanes] = bfloat(key_grad * SCORE_SCALE)
        proj_grad_ref[:, value_lanes] = bfloat(value_grad)

    proj_grad = proj_grad_ref[...]
    norm_grad = dot_as(proj_grad, qkv_ref[...], NT)
    region = all_ref[...].astype(jnp.float32)
    center = region - jnp.mean(region, -1, keepdims=True)
    scale = lax.rsqrt(jnp.mean(center * center, -1, keepdims=True) + EPSILON)
    hat = center * scale
    hat_grad = norm_grad * vec_ref[0:1, :]
    region_grad_ref[...] = scale * (
        hat_grad
        - jnp.mean(hat_grad, -1, keepdims=True)
        - hat * jnp.mean(hat_grad * hat, -1, keepdims=True)
    )
    start = pl.multiple_of(place_ref[1] * rows, 8)
    grad_out[...] = new_grad_ref[...] + region_grad_ref[pl.ds(start, rows), :]
    bias_sums = jnp.sum(proj_grad.astype(jnp.float32), 0, keepdims=True)
    sums_out[0:1, :] = jnp.sum(norm_grad * hat, 0, keepdims=True)
    sums_out[1:2, :] = jnp.sum(norm_grad, 0, keepdims=True)
    sums_out[2:3, :] = bias_sums[:, :width]
    sums_out[3:4, :] = bias_sums[:, 2 * width :]
    sums_out[4:8, :] = jnp.zeros((4, width), jnp.float32)
    weight_ref[...] = dot_as(norm_ref[...], proj_grad, TN)
    weight_rows = weight_out.shape[1]
    weight_start = pl.multiple_of(place_ref[1] * weight_rows, 8)
    for number in range(3):
        weight_out[number] = weight_ref[
            pl.ds(weight_start, weight_rows), number * width : (number + 1) * width
        ]


def region_backward(
    place, all_rows, normed, proj, mix_grad, key_images, query_images, new_grad, qkv_flat, vectors, weight_rows
):
    total, width = all_rows.shape
    vmem = pl.BlockSpec(memory_space=pltpu.VMEM)
    return pl.pallas_call(
        region_backward_kernel,
        in_specs=[pl.BlockSpec(memory_space=pltpu.SMEM)] + [vmem] * 9,
        out_specs=[vmem] * 3,
        out_shape=[
            shape_of(new_grad.shape),
            shape_of((3, weight_rows, width)),
            shape_of((8, width)),
        ],
        scratch_shapes=[
            pltpu.VMEM((total, total), jnp.float32),
            pltpu.VMEM((total, 3 * width), jnp.bfloat16),
            pltpu.VMEM((total, width), jnp.float32),
            pltpu.VMEM((width, 3 * width), jnp.float32),
        ],
        compiler_params=pltpu.CompilerParams(vmem_limit_bytes=VMEM_LIMIT),
        name="region_backward",
    )(place, all_rows, normed, proj, mix_grad, key_images, query_images, new_grad, qkv_flat, vectors)


def split_cores(values, core):
    own_first = core == 0
    kept = jnp.where(own_first, values[:, 0], values[:, 1])
    sent = jnp.where(own_first, values[:, 1], values[:, 0])
    return kept, bfloat(sent)


def big_gradient_kernel(
    place_ref, norm_ref, up_grad_ref, act_ref, down_grad_ref, up_kept, up_sent, down_kept, down_sent
):
    core = place_ref[1] % 2
    width = norm_ref.shape[1]
    blocks, _, rows, _ = up_kept.shape
    total = dot_as(norm_ref[...], up_grad_ref[...], TN).reshape(blocks, 2, rows, width)
    up_kept[:, 0], up_sent[:, 0] = split_cores(total, core)
    blocks, rows, _ = down_kept.shape
    total = dot_as(act_ref[...], down_grad_ref[...], TN).reshape(blocks, 2, rows, width)
    down_kept[...], down_sent[...] = split_cores(total, core)


def big_gradients(place, normed, up_grad, act, down_grad, win_count):
    rows, width = normed.shape
    folds = up_grad.shape[1] // width
    half = win_count // 2
    up_rows = width // win_count
    whole = pl.BlockSpec((rows, width), lambda fold: (0, 0))
    part = pl.BlockSpec((rows, width), lambda fold: (0, fold))
    up_spec = pl.BlockSpec((half, 1, up_rows, width), lambda fold: (0, fold, 0, 0))
    down_spec = pl.BlockSpec((half // folds, up_rows * folds, width), lambda fold: (fold, 0, 0))
    up_dims = (half, folds, up_rows, width)
    down_dims = (half, up_rows * folds, width)
    kept_up, sent_up, kept_down, sent_down = pl.pallas_call(
        big_gradient_kernel,
        grid=(folds,),
        in_specs=[pl.BlockSpec(memory_space=pltpu.SMEM), whole, part, part, whole],
        out_specs=[up_spec, up_spec, down_spec, down_spec],
        out_shape=[
            shape_of(up_dims),
            shape_of(up_dims, jnp.bfloat16),
            shape_of(down_dims),
            shape_of(down_dims, jnp.bfloat16),
        ],
        compiler_params=pltpu.CompilerParams(vmem_limit_bytes=VMEM_LIMIT),
        cost_estimate=pl.CostEstimate(
            flops=4 * rows * width * width * folds,
            bytes_accessed=4 * rows * width * (folds + 1) + 12 * width * width * folds,
            transcendentals=0,
        ),
        name="big_gradients",
    )(place, normed, up_grad, act, down_grad)
    return (kept_up.reshape(down_dims), sent_up.reshape(down_dims)), (kept_down, sent_down)


def small_gradient_kernel(
    place_ref, norm_ref, proj_grad_ref, mix_ref, branch_ref, region_mix_ref, region_branch_ref, kept, sent
):
    core = place_ref[1] % 2
    number = pl.program_id(0)
    width = norm_ref.shape[1]
    blocks, _, rows, _ = kept.shape

    @pl.when(number < 3)
    def _():
        total = dot_as(norm_ref[...], proj_grad_ref[...], TN).reshape(blocks, 2, rows, width)
        kept[:, 0], sent[:, 0] = split_cores(total, core)

    @pl.when(number == 3)
    def _():
        total = dot_as(mix_ref[...], branch_ref[...], TN)
        total = total + dot_as(region_mix_ref[...], region_branch_ref[...], TN)
        total = total.reshape(blocks, 2, rows, width)
        kept[:, 0], sent[:, 0] = split_cores(total, core)


def small_gradients(place, normed, proj_grad, mix, branch, region_mix, region_branch, win_count):
    rows, width = normed.shape
    half = win_count // 2
    weight_rows = width // win_count
    whole = pl.BlockSpec((rows, width), lambda number: (0, 0))
    part = pl.BlockSpec((rows, width), lambda number: (0, jnp.minimum(number, 2)))
    region = pl.BlockSpec(region_mix.shape, lambda number: (0, 0))
    out_spec = pl.BlockSpec((half, 1, weight_rows, width), lambda number: (0, number, 0, 0))
    dims = (half, 4, weight_rows, width)
    kept, sent = pl.pallas_call(
        small_gradient_kernel,
        grid=(4,),
        in_specs=[pl.BlockSpec(memory_space=pltpu.SMEM), whole, part, whole, whole, region, region],
        out_specs=[out_spec, out_spec],
        out_shape=[shape_of(dims), shape_of(dims, jnp.bfloat16)],
        compiler_params=pltpu.CompilerParams(vmem_limit_bytes=VMEM_LIMIT),
        cost_estimate=pl.CostEstimate(
            flops=8 * rows * width * width,
            bytes_accessed=12 * rows * width + 24 * width * width,
            transcendentals=0,
        ),
        name="small_gradients",
    )(place, normed, proj_grad, mix, branch, region_mix, region_branch)
    flat = (half, 4 * weight_rows, width)
    return kept.reshape(flat), sent.reshape(flat)


def core_hop(kept, sent):
    return kept + swap(sent, "win", 0).astype(jnp.float32)


def local(
    tokens,
    patch_mask,
    keep_mask,
    image_map,
    qkv_weight,
    out_weight,
    up_weight,
    down_weight,
    vectors,
    qkv_mom,
    out_mom,
    up_mom,
    down_mom,
    vec_mom,
    cotangent,
):
    windows = tokens.shape[1]
    seq_len = tokens.shape[2]
    model_width = tokens.shape[3]
    hidden_width = up_weight.shape[1]
    folds = hidden_width // model_width
    shard_rows = out_mom.shape[0]
    ff_rows = down_mom.shape[0]
    vec_rows = vec_mom.shape[0]
    padded = (seq_len + 7) // 8 * 8
    region_rows = (windows + 7) // 8 * 8
    row_count = windows * padded
    win_count = lax.axis_size("win")
    win_index = lax.axis_index("win")
    place = jnp.stack([lax.axis_index("rep"), win_index]).astype(jnp.int32)

    def pad_rows(values, rows, fill=0):
        widths = ((0, rows - values.shape[0]),) + ((0, 0),) * (values.ndim - 1)
        return jnp.pad(values, widths, constant_values=fill)

    region_own = pad_rows(tokens[0, :, 0], region_rows)
    region_all = gather_blocks(region_own, "win").reshape(-1, model_width)
    keeper = keep_mask[0].astype(jnp.float32) / KEEP_SHARE
    images = image_map[0].reshape(win_count, windows)
    images = jnp.pad(images, ((0, 0), (0, region_rows - windows)), constant_values=-1)
    key_images = images.reshape(-1, 1)
    own_images = jnp.tile(own_block(images)[None], (1, GROUP_HEADS))
    qkv_flat = jnp.concatenate([qkv_weight[0], qkv_weight[1], qkv_weight[2]], axis=1)
    bias_up = vectors[10:].reshape(hidden_width)
    region_keep = pad_rows(keeper[:, 0:1], region_rows)

    region_norm, region_proj, region_mix, region_new = region_forward(
        region_all, region_own, region_keep, key_images, own_images, qkv_flat, out_weight, vectors
    )

    key_valid = jnp.concatenate([jnp.ones((windows, 1), jnp.int32), patch_mask[0]], axis=1) == 1
    key_bias = jnp.where(key_valid, 0.0, -1e30)
    key_bias = jnp.pad(key_bias, ((0, 0), (0, padded - seq_len)), constant_values=-1e30)
    key_bias = key_bias[:, :, None]
    keep_window = keeper[:, 1].reshape(windows, 1, 1)
    seq_norm, seq_proj, local_mix, after_attn = window_forward(
        tokens, region_new, key_bias, keep_window, qkv_flat, out_weight, vectors, padded
    )
    seq_norm = seq_norm.reshape(row_count, model_width)
    local_mix = local_mix.reshape(row_count, model_width)
    after_attn = after_attn.reshape(row_count, model_width)
    keep_mlp = jnp.broadcast_to(keeper[:, 2:3], (windows, padded)).reshape(row_count, 1)

    mlp_norm = bfloat(norm_rows(after_attn, vectors[4], vectors[5]))
    up_value = product(mlp_norm, up_weight) + bias_up
    activated, gelu_back = jax.vjp(jax.nn.gelu, up_value)
    act_low = bfloat(activated)
    mlp_branch = product(act_low, down_weight) + vectors[9]
    output = after_attn + keep_mlp * mlp_branch
    grad_out = jnp.pad(cotangent[0], ((0, 0), (0, padded - seq_len), (0, 0)))
    grad_out = grad_out.astype(jnp.float32).reshape(row_count, model_width)
    mlp_grad = bfloat(keep_mlp * grad_out)
    grad_bm = jnp.sum(mlp_grad.astype(jnp.float32), 0)
    up_grad = bfloat(gelu_back(product(mlp_grad, down_weight.T))[0])
    grad_bu = jnp.sum(up_grad.astype(jnp.float32), 0)
    norm3_back = jax.vjp(norm_rows, after_attn, vectors[4], vectors[5])[1](
        product(up_grad, up_weight.T)
    )
    attn_res_grad = grad_out + norm3_back[0]
    up_half, down_half = big_gradients(place, mlp_norm, up_grad, act_low, mlp_grad, win_count)
    up_half, down_half, attn_res_grad = lax.optimization_barrier(
        (up_half, down_half, attn_res_grad)
    )
    big_total = scatter_pair(core_hop(*up_half), core_hop(*down_half))

    (
        seq_grad,
        region_new_grad,
        local_qkv_grad,
        local_branch_grad,
        seq_sums,
        region_branch_grad,
        region_mix_grad,
    ) = window_backward(
        tokens,
        region_new,
        key_bias,
        keep_window,
        qkv_flat,
        out_weight,
        vectors,
        seq_proj,
        attn_res_grad.reshape(windows, padded, model_width),
        region_keep,
        padded,
    )

    region_grad, region_weight_grad, region_sums = region_backward(
        place,
        region_all,
        region_norm,
        region_proj,
        gather_blocks(region_mix_grad, "win").reshape(-1, model_width),
        key_images,
        key_images.reshape(1, -1),
        region_new_grad,
        qkv_flat,
        vectors,
        shard_rows,
    )
    input_grad = lax.dynamic_update_slice(
        seq_grad, region_grad[None, :windows, None], (0, 0, 0, 0)
    )

    small_kept, small_sent = small_gradients(
        place,
        seq_norm,
        local_qkv_grad.reshape(row_count, 3 * model_width),
        local_mix,
        local_branch_grad.reshape(row_count, model_width),
        region_mix,
        region_branch_grad,
        win_count,
    )

    def vector_blocks(rows):
        blocks = jnp.concatenate(rows, axis=0).reshape(win_count, vec_rows)
        return jnp.pad(blocks, ((0, 0), (0, model_width - vec_rows)))

    zero_row = jnp.zeros((1, model_width), jnp.float32)
    seq_vectors = vector_blocks(
        [
            zero_row,
            zero_row,
            seq_sums[0:1, :model_width],
            seq_sums[1:2, :model_width],
            norm3_back[1][None],
            norm3_back[2][None],
            seq_sums[3:4, :model_width],
            seq_sums[3:4, 2 * model_width :],
            seq_sums[2:3, :model_width],
            grad_bm[None],
            grad_bu.reshape(-1, model_width),
        ]
    )
    region_vectors = vector_blocks(
        [region_sums[0:2], jnp.tile(zero_row, (4, 1)), region_sums[2:4], jnp.tile(zero_row, (6, 1))]
    )
    core = win_index % 2
    vector_pairs = seq_vectors.reshape(win_count // 2, 2, 1, model_width)
    vector_pairs = jnp.pad(vector_pairs, ((0, 0), (0, 0), (0, 7), (0, 0)))
    small_kept = jnp.concatenate(
        [small_kept, lax.dynamic_index_in_dim(vector_pairs, core, 1, keepdims=False)], axis=1
    )
    small_sent = jnp.concatenate(
        [
            small_sent,
            bfloat(lax.dynamic_index_in_dim(vector_pairs, 1 - core, 1, keepdims=False)),
        ],
        axis=1,
    )
    small_half = core_hop(small_kept, small_sent)
    small_total = scatter_pair(
        small_half[:, : 2 * shard_rows], small_half[:, 2 * shard_rows :]
    )
    region_total = sum_over_rep(
        jnp.concatenate(
            [
                region_weight_grad.reshape(-1, model_width),
                pad_rows(own_block(region_vectors)[None], 8),
            ],
            axis=0,
        )
    )
    matrix_rows = 4 * shard_rows
    region_matrix = region_total[: 3 * shard_rows].reshape(3, shard_rows, model_width)
    small_matrix = small_total[:matrix_rows].reshape(4, shard_rows, model_width)
    new_qkv_mom = MOMENTUM_DECAY * qkv_mom + (small_matrix[:3] + region_matrix)
    new_out_mom = MOMENTUM_DECAY * out_mom + small_matrix[3]
    vec_total = small_total[matrix_rows, :vec_rows] + region_total[3 * shard_rows, :vec_rows]
    new_vec_mom = MOMENTUM_DECAY * vec_mom + vec_total
    new_vectors = (
        lax.dynamic_slice_in_dim(vectors.reshape(-1), win_index * vec_rows, vec_rows)
        - VECTOR_RATE * new_vec_mom
    )
    folded_up_mom = MOMENTUM_DECAY * fold_columns(up_mom, model_width) + big_total[:ff_rows]
    new_up_mom = unfold_columns(folded_up_mom, folds)
    new_down_mom = MOMENTUM_DECAY * down_mom + big_total[ff_rows:]
    up_update, down_update = big_updates(folded_up_mom, new_down_mom, folds)
    updates = small_updates(jnp.concatenate([new_qkv_mom, new_out_mom[None]]))

    def stepped(weight, rows_here, update):
        rows = own_rows(weight, rows_here).astype(jnp.float32)
        return rows - MATRIX_RATE * update.astype(jnp.float32)

    new_qkv = jnp.stack(
        [stepped(qkv_weight[number], shard_rows, updates[number]) for number in range(3)]
    )
    new_out = stepped(out_weight, shard_rows, updates[3])
    new_up = stepped(up_weight, shard_rows, unfold_columns(up_update, folds))
    new_down = stepped(down_weight, ff_rows, down_update)
    out_tokens = bfloat(output.reshape(1, windows, padded, model_width)[:, :, :seq_len])
    return (
        out_tokens,
        input_grad,
        new_qkv_mom,
        new_qkv,
        new_out_mom,
        new_out,
        new_up_mom,
        new_up,
        new_down_mom,
        new_down,
        new_vec_mom,
        new_vectors,
    )


def solution(mesh):
    placed = (
        P("rep", "win", None, None),
        P("rep", "win", None),
        P("rep", "win", None),
        P("rep", None),
        P(),
        P(),
        P(),
        P(),
        P(),
        P(None, "win", None),
        P("win", None),
        P("win", None),
        P("win", None),
        P("win"),
        P("rep", "win", None, None),
    )
    return jax.shard_map(
        local,
        mesh=mesh,
        in_specs=placed,
        out_specs=(
            P("rep", "win", None, None),
            P("rep", "win", None, None),
            P(None, "win", None),
            P(None, "win", None),
            P("win", None),
            P("win", None),
            P("win", None),
            P("win", None),
            P("win", None),
            P("win", None),
            P("win"),
            P("win"),
        ),
        check_vma=False,
    )
```

time: 1060 us -> 326 us (0.31)
  waiting for transfers between devices: 401 us -> 77 us
  matrix products: 248 us -> 24 us
  blocking collectives: 145 us -> 0 us
  local copies, waits for them, and re-layouts: 147 us -> 21.7 us
  Pallas kernels: 0 us -> 124 us
  other arithmetic: 75.7 us -> 28.3 us
  starting transfers between devices: 0.5 us -> 44.7 us
  loops' own time: 24.3 us -> 0 us
  between operations: 16.4 us -> 2.11 us
    psum x2 -> x0, waiting for transfers between devices: 325 us -> none  [the longest x1 231 us: local(): lax.psum((gradients[0], gradients[1], gradients[2], gradients[3], gradien...]
    dot_general x55 -> x0, matrix products: 179 us -> none  [the longest x15 57.6 us: newton(): gram_matrix = jnp.matmul(iterate, iterate.T, precision=HIGHEST)]
    pallas_call x0 -> x8, Pallas kernels: none -> 124 us  [the longest x2 35.4 us: newton_call(): pl.pallas_call(kernel, in_specs=[pl.BlockSpec(memory_space=pltpu.SMEM), p...]
    psum x1 -> x0, blocking collectives: 80.1 us -> none  [local(): lax.psum((gradients[0], gradients[1], gradients[2], gradients[3], gradien...]
    ppermute x0 -> x36, waiting for transfers between devices: none -> 77 us  [swap(): return lax.ppermute(values, axis, [(i, i ^ 1 << bit) for i in range(size)])]
    unnamed x7 -> x0, waiting for transfers between devices: 71.8 us -> none
    reshape x15 -> x5, local copies, waits for them, and re-layouts: 68 us -> 1.04 us  [the longest x1 0.72 us: unfold_columns(): rows.reshape(folds, total // folds, width).swapaxes(0, 1)]
    all_gather x3 -> x0, blocking collectives: 65.2 us -> none  [the longest x1 24.2 us: local(): lax.all_gather(region_key, 'win', axis=0, tiled=True)]
  transfers between devices with their start and end apart: 6 -> 36, of which waited for: 4 -> 20; matrix products, arithmetic and copies ran while one was open for 11% -> 11% of each run, Pallas kernels for 0% -> 12%
where the time goes in v1:
time: 326 us; the launch traced here: 322 us
  Pallas kernels  124 us (38%)
  waiting for transfers between devices  77 us (24%)
  starting transfers between devices  44.7 us (14%)
  other arithmetic  28.3 us (9%)
  matrix products  24 us (7%)
  local copies, waits for them, and re-layouts  21.7 us (7%)
    ppermute x36, waiting for transfers between devices, swap(): return lax.ppermute(values, axis, [(i, i ^ 1 << bit) for i in range(size)])  77 us
    ppermute x36, starting transfers between devices, swap(): return lax.ppermute(values, axis, [(i, i ^ 1 << bit) for i in range(size)])  44.7 us
    pallas_call x2, Pallas kernels, newton_call(): pl.pallas_call(kernel, in_specs=[pl.BlockSpec(memory_space=pltpu.SMEM), p...  35.4 us
    pallas_call x1, Pallas kernels, window_backward(): pl.pallas_call(functools.partial(window_backward_kernel, count, seq_len,...  29.6 us
    pallas_call x1, Pallas kernels, window_forward(): pl.pallas_call(functools.partial(window_forward_kernel, count, seq_len, p...  26.5 us
    dot_general x4, matrix products, product(): return jnp.dot(left_side, right_side, preferred_element_type=jnp.float32)  24 us
    pallas_call x1, Pallas kernels, region_backward(): pl.pallas_call(region_backward_kernel, in_specs=[pl.BlockSpec(memory_spac...  13.7 us
    unnamed x81, local copies, waits for them, and re-layouts  11.7 us
  transfers between devices with their start and end apart: 36, of which 20 were waited for; matrix products, arithmetic and copies ran while one was open for 11% of the time, Pallas kernels for 12%

profile of v1, /device:TPU:0, one launch (start us, length us, event | category | flops | bytes accessed | tf_op | source)
XLA Modules:
  0.0 322.0 jit_solution(7436365979966208697)
XLA Ops:
  1.6 3.1 collective-permute-start
  25.0 26.5 %window_forward.1 = (bf16[20,56,512]{2,1,0:T(8,128)(2,1)S(1)}, bf16[20,56,1536]{2,1,0:T(8,128)(2,1)}, bf16[20,56,512]{2,1,0:T(8,128)(2,1)S(1)}, f32[20,56,512]{2,1,0:T(8,128)}) custom-call(bf16[1,20,50,512]{3,2,1,0:T(8,128)(2,1)S(1)} %copy-done.1, f32[24,512]{1,0:T(8,128)S(1)} %get-tuple-element.41.region_ref, f32[20,56,1]{2,1,0:T(8,128)S(1)} %copy.68.bias_ref, ...), custom_call_target="tpu_custom_call" | custom-call | tf_op jit(solution)/shard_map/window_forward/pallas_call | solution.py:522
  60.4 6.0 %multiply_convert_fusion = (bf16[1120,2048]{1,0:T(8,128)(2,1)}, f32[1120,2048]{1,0:T(8,128)S(1)}) fusion(f32[2048]{0:T(1024)S(1)} %bitcast.301, bf16[1120,512]{1,0:T(8,128)(2,1)S(1)} %get-tuple-element.114.norm_ref, bf16[512,2048]{1,0:T(8,128)(2,1)S(1)} %copy-done.33), kind=kOutput, calls=%fused_computation.10 | convolution fusion | flops 2371747840 | bytes 17014784 | tf_op jit(solution)/shard_map/dot_general | solution.py:27
  66.4 8.4 %convert_reduce_fusion = (f32[2048]{0:T(1024)S(1)}, bf16[1120,2048]{1,0:T(8,128)(2,1)S(1)}) fusion(f32[1120,2048]{1,0:T(8,128)S(1)} %get-tuple-element.176, bf16[1120,512]{1,0:T(8,128)(2,1)S(1)} %get-tuple-element.180.down_grad_ref, bf16[2048,512]{1,0:T(8,128)(2,1)S(1)} %copy-done.32), kind=kOutput, calls=%fused_computation.9 | convolution fusion | flops 2399270912 | bytes 17014784 | tf_op jit(solution)/shard_map/dot_general | solution.py:27
  80.9 10.2 %big_gradients.1 = (f32[8,4,32,512]{3,2,1,0:T(8,128)}, bf16[8,4,32,512]{3,2,1,0:T(8,128)(2,1)}, f32[8,128,512]{2,1,0:T(8,128)}, bf16[8,128,512]{2,1,0:T(8,128)(2,1)}) custom-call(s32[2]{0:T(128)S(1)} %pad_add_fusion.place_ref, bf16[1120,512]{1,0:T(8,128)(2,1)S(1)} %get-tuple-element.114.norm_ref, bf16[1120,2048]{1,0:T(8,128)(2,1)} %copy-done.36, ...), custom_call_target="tpu_custom_call" | custom-call | flops 4697620480 | bytes 24051712 | tf_op jit(solution)/shard_map/big_gradients/pallas_call | solution.py:799
  91.1 29.6 %window_backward.1 = (f32[1,20,50,512]{3,2,1,0:T(8,128)}, f32[24,512]{1,0:T(8,128)S(1)}, bf16[20,56,1536]{2,1,0:T(8,128)(2,1)}, bf16[20,56,512]{2,1,0:T(8,128)(2...) custom-call(bf16[1,20,50,512]{3,2,1,0:T(8,128)(2,1)S(1)} %copy-done.2, ...), custom_call_target="tpu_custom_call" | custom-call | tf_op jit(solution)/shard_map/window_backward/pallas_call | solution.py:560
  120.8 6.4 %small_gradients.1 = (f32[8,4,32,512]{3,2,1,0:T(8,128)}, bf16[8,4,32,512]{3,2,1,0:T(8,128)(2,1)S(1)}) custom-call(s32[2]{0:T(128)S(1)} %pad_add_fusion.place_ref, bf16[1120,512]{1,0:T(8,128)(2,1)S(1)} %bitcast.247, bf16[1120,1536]{1,0:T(8,128)(2,1)} %bitcast.305, bf16[1120,512]{1,0:T(8,128)(2,1)S(1)} %bitcast.248, bf16[1120,512]{1,0:T(8,128)(2,1)S(1)} %bitcast.249, ...), custom_call_target="tpu_custom_call" | custom-call | flops 2348810240 | bytes 13172736 | tf_op jit(solution)/shard_map/small_gradients/pallas_call | solution.py:851
  128.4 3.1 collective-permute-start.5
  139.4 6.7 %fusion.9 = bf16[1120,512]{1,0:T(8,128)(2,1)} fusion(f32[1120,512]{1,0:T(8,128)S(1)} %bitcast.250, bf16[1120,2048]{1,0:T(8,128)(2,1)} %get-tuple-element.175.act_ref, bf16[2048,512]{1,0:T(8,128)(2,1)} %param.22, f32[512]{0:T(512)S(1)} %bitcast.304, f32[1120]{0:T(1024)S(1)} %mul.233), kind=kOutput, calls=%fused_computation.16 | convolution fusion | flops 2351104000 | bytes 10131840 | tf_op jit(solution)/shard_map/dot_general | solution.py:27
  147.4 13.7 %region_backward.1 = (f32[24,512]{1,0:T(8,128)S(1)}, f32[3,32,512]{2,1,0:T(8,128)S(1)}, f32[8,512]{1,0:T(8,128)S(1)}) custom-call(s32[2]{0:T(128)S(1)} %pad_add_fusion.place_ref, bf16[384,512]{1,0:T(8,128)(2,1)S(1)} %bitcast.242, bf16[384,512]{1,0:T(8,128)(2,1)S(1)} %copy-done.8, bf16[384,1536]{1,0:T(8,128)(2,1)S(1)} %copy-done.4, ...), custom_call_target="tpu_custom_call" | custom-call | tf_op jit(solution)/shard_map/region_backward/pallas_call | solution.py:748
  165.0 5.2 %copy.88 = f32[1,20,50,512]{3,0,2,1:T(1,128)} copy(f32[1,20,50,512]{3,2,1,0:T(8,128)} %dynamic_update_slice.3) | data formatting | bytes 4096000
  180.0 11.6 %collective-permute-done.9 = bf16[8,64,256]{2,1,0:T(8,128)(2,1)S(1)} collective-permute-done((bf16[8,64,256]{2,1,0:T(8,128)(2,1)S(1)}, bf16[8,64,256]{2,1,0:T(8,128)(2,1)S(1)}, u32[]{:S(2)}, u32[]{:S(2)}) %collective-permute-start.9) | collective-permute-done | bytes 262176 | tf_op jit(solution)/shard_map/ppermute | solution.py:42
  193.3 5.5 %collective-permute-done.11 = bf16[2,2,72,512]{3,2,1,0:T(8,128)(2,1)S(1)} collective-permute-done((bf16[2,2,72,512]{3,2,1,0:T(8,128)(2,1)S(1)}, bf16[2,2,72,512]{3,2,1,0:T(8,128)(2,1)S(1)}, u32[]{:S(2)}, u32[]{:S(2)}) %collective-permute-start.11) | collective-permute-done | bytes 294944 | tf_op jit(solution)/shard_map/ppermute | solution.py:42
  200.5 3.6 %collective-permute-done.12 = bf16[4,72,256]{2,1,0:T(8,128)(2,1)S(1)} collective-permute-done((bf16[4,72,256]{2,1,0:T(8,128)(2,1)S(1)}, bf16[4,72,256]{2,1,0:T(8,128)(2,1)S(1)}, u32[]{:S(2)}, u32[]{:S(2)}) %collective-permute-start.12) | collective-permute-done | bytes 147488 | tf_op jit(solution)/shard_map/ppermute | solution.py:42
  212.1 3.2 %collective-permute-done.14 = bf16[136,256]{1,0:T(8,128)(2,1)S(1)} collective-permute-done((bf16[136,256]{1,0:T(8,128)(2,1)S(1)}, bf16[136,256]{1,0:T(8,128)(2,1)S(1)}, u32[]{:S(2)}, u32[]{:S(2)}) %collective-permute-start.14) | collective-permute-done | bytes 69664 | tf_op jit(solution)/shard_map/ppermute | solution.py:42
  219.9 3.5 %collective-permute-done.27 = bf16[4,128,256]{2,1,0:T(8,128)(2,1)S(1)} collective-permute-done((bf16[4,128,256]{2,1,0:T(8,128)(2,1)S(1)}, bf16[4,128,256]{2,1,0:T(8,128)(2,1)S(1)}, u32[]{:S(2)}, u32[]{:S(2)}) %collective-permute-start.27) | collective-permute-done | bytes 262176 | tf_op jit(solution)/shard_map/ppermute | solution.py:42
  225.9 4.3 %collective-permute-done.28 = bf16[2,256,256]{2,1,0:T(8,128)(2,1)S(1)} collective-permute-done((bf16[2,256,256]{2,1,0:T(8,128)(2,1)S(1)}, bf16[2,256,256]{2,1,0:T(8,128)(2,1)S(1)}, u32[]{:S(2)}, u32[]{:S(2)}) %collective-permute-start.28) | collective-permute-done | bytes 262176 | tf_op jit(solution)/shard_map/ppermute | solution.py:42
  232.5 5.4 %collective-permute-done.29 = bf16[256,256]{1,0:T(8,128)(2,1)S(1)} collective-permute-done((bf16[256,256]{1,0:T(8,128)(2,1)S(1)}, bf16[256,256]{1,0:T(8,128)(2,1)S(1)}, u32[]{:S(2)}, u32[]{:S(2)}) %collective-permute-start.29) | collective-permute-done | bytes 131104 | tf_op jit(solution)/shard_map/ppermute | solution.py:42
  244.4 5.4 %collective-permute-done.18 = bf16[2,2,32,512]{3,2,1,0:T(8,128)(2,1)S(1)} collective-permute-done((bf16[2,2,32,512]{3,2,1,0:T(8,128)(2,1)S(1)}, bf16[2,2,32,512]{3,2,1,0:T(8,128)(2,1)S(1)}, u32[]{:S(2)}, u32[]{:S(2)}) %collective-permute-start.18) | collective-permute-done | bytes 131104 | tf_op jit(solution)/shard_map/ppermute | solution.py:42
  252.4 3.8 %collective-permute-done.19 = bf16[2,2,2,32,512]{4,3,2,1,0:T(8,128)(2,1)S(1)} collective-permute-done((bf16[2,2,2,32,512]{4,3,2,1,0:T(8,128)(2,1)S(1)}, bf16[2,2,2,32,512]{4,3,2,1,0:T(8,128)(2,1)S(1)}, u32[]{:S(2)}, u32[]{:S(2)}) %collective-permute-start.19) | collective-permute-done | bytes 262176 | tf_op jit(solution)/shard_map/ppermute | solution.py:42
  256.4 5.1 %collective-permute-done.32 = bf16[2,128,512]{2,1,0:T(8,128)(2,1)S(1)} collective-permute-done((bf16[2,128,512]{2,1,0:T(8,128)(2,1)S(1)}, bf16[2,128,512]{2,1,0:T(8,128)(2,1)S(1)}, u32[]{:S(2)}, u32[]{:S(2)}) %collective-permute-start.32) | collective-permute-done | bytes 262176 | tf_op jit(solution)/shard_map/ppermute | solution.py:42
  264.4 6.6 %collective-permute-done.33 = bf16[2,2,128,512]{3,2,1,0:T(8,128)(2,1)S(1)} collective-permute-done((bf16[2,2,128,512]{3,2,1,0:T(8,128)(2,1)S(1)}, bf16[2,2,128,512]{3,2,1,0:T(8,128)(2,1)S(1)}, u32[]{:S(2)}, u32[]{:S(2)}) %collective-permute-start.33) | collective-permute-done | bytes 524320 | tf_op jit(solution)/shard_map/ppermute | solution.py:42
  271.3 19.9 %small_newton.1 = bf16[2,32,512]{2,1,0:T(8,128)(2,1)S(1)} custom-call(s32[2]{0:T(128)S(1)} %pad_add_fusion.place_ref, bf16[16,2,32,512]{3,2,1,0:T(8,128)(2,1)S(1)} %bitcast.246), custom_call_target="tpu_custom_call" | custom-call | flops 14495514624 | bytes 1048576 | tf_op jit(solution)/shard_map/small_newton/pallas_call | solution.py:216
  297.8 15.5 %big_newton.1 = bf16[128,512]{1,0:T(8,128)(2,1)S(1)} custom-call(s32[2]{0:T(128)S(1)} %pad_add_fusion.place_ref, bf16[16,128,512]{2,1,0:T(8,128)(2,1)S(1)} %bitcast.243), custom_call_target="tpu_custom_call" | custom-call | flops 12079595520 | bytes 2097152 | tf_op jit(solution)/shard_map/big_newton/pallas_call | solution.py:216
  (297 shorter events, 107.6 us)
Async XLA Ops:
  1.6 7.5 %collective-permute-start = (bf16[24,512]{1,0:T(8,128)(2,1)S(1)}, bf16[24,512]{1,0:T(8,128)(2,1)S(1)}, u32[]{:S(2)}, u32[]{:S(2)}) collective-permute-start(bf16[24,512]{1,0:T(8,128)(2,1)S(1)} %pad.37.own_ref), channel_id=1, source_target_pairs={{0,8},{2,10},{4,12},{6,14},{8,0},{10,2},{12,4},{14,6},{16,24},{18,... | collective-permute-start | bytes 73736 | tf_op jit(solution)/shard_map/ppermute | solution.py:42
  120.7 7.7 %collective-permute-start.4 = (bf16[24,512]{1,0:T(8,128)(2,1)S(1)}, bf16[24,512]{1,0:T(8,128)(2,1)S(1)}, u32[]{:S(2)}, u32[]{:S(2)}) collective-permute-start(bf16[24,512]{1,0:T(8,128)(2,1)S(1)} %get-tuple-element.52), channel_id=1, source_target_pairs={{0,8},{2,10},{4,12},{6,14},{8,0},{10,2},{12,4},{14,6},{16,24},{18,... | collective-permute-start | bytes 73736 | tf_op jit(solution)/shard_map/ppermute | solution.py:42
  138.3 34.4 %collective-permute-start.8 = (bf16[8,136,512]{2,1,0:T(8,128)(2,1)}, bf16[8,136,512]{2,1,0:T(8,128)(2,1)}, u32[]{:S(2)}, u32[]{:S(2)}) collective-permute-start(bf16[8,136,512]{2,1,0:T(8,128)(2,1)} %pad_maximum_fusion.2), channel_id=1, source_target_pairs={{0,2},{2,0},{4,6},{6,4},{8,10},{10,8},{12,14},{14,12},{16,18},{18,... | collective-permute-start | bytes 3342344 | tf_op jit(solution)/shard_map/ppermute | solution.py:42
  138.3 32.0 %collective-permute-start.22 = (bf16[8,128,512]{2,1,0:T(8,128)(2,1)}, bf16[8,128,512]{2,1,0:T(8,128)(2,1)}, u32[]{:S(2)}, u32[]{:S(2)}) collective-permute-start(bf16[8,128,512]{2,1,0:T(8,128)(2,1)} %bitcast.27), channel_id=1, source_target_pairs={{0,2},{2,0},{4,6},{6,4},{8,10},{10,8},{12,14},{14,12},{16,18},{18,... | collective-permute-start | bytes 3145736 | tf_op jit(solution)/shard_map/ppermute | solution.py:42
  138.8 37.2 %collective-permute-start.25 = (bf16[8,128,512]{2,1,0:T(8,128)(2,1)}, bf16[8,128,512]{2,1,0:T(8,128)(2,1)}, u32[]{:S(2)}, u32[]{:S(2)}) collective-permute-start(bf16[8,128,512]{2,1,0:T(8,128)(2,1)} %get-tuple-element.69), channel_id=1, source_target_pairs={{0,2},{2,0},{4,6},{6,4},{8,10},{10,8},{12,14},{14,12},{16,18},{18,... | collective-permute-start | bytes 3145736 | tf_op jit(solution)/shard_map/ppermute | solution.py:42
  138.9 7.4 %collective-permute-start.7 = (bf16[2,2,2,24,512]{4,3,1,0,2:T(8,128)(2,1)S(1)}, bf16[2,2,2,24,512]{4,3,1,0,2:T(8,128)(2,1)S(1)}, u32[]{:S(2)}, u32[]{:S(2)}) collective-permute-start(bf16[2,2,2,24,512]{4,3,1,0,2:T(8,128)(2,1)S(1)} %pad_maximum_fusion.12), channel_id=1, source_target_pairs={{0,2},{2,0},{4,6},{6,4},{8,10},{10,8},{12,14},{14,12},{16,18},{18,... | collective-permute-start | bytes 589832 | tf_op jit(solution)/shard_map/ppermute | solution.py:42
  161.4 8.8 %collective-permute-start.16 = (bf16[104,512]{1,0:T(8,128)(2,1)S(1)}, bf16[104,512]{1,0:T(8,128)(2,1)S(1)}, u32[]{:S(2)}, u32[]{:S(2)}) collective-permute-start(bf16[104,512]{1,0:T(8,128)(2,1)S(1)} %fusion.40), channel_id=1, source_target_pairs={{0,1},{1,0},{2,3},{3,2},{4,5},{5,4},{6,7},{7,6},{8,9},{9,8},{10,11... | collective-permute-start | bytes 319496 | tf_op jit(solution)/shard_map/ppermute | solution.py:42
  172.1 33.5 %collective-permute-start.23 = (bf16[8,128,256]{2,1,0:T(8,128)(2,1)S(1)}, bf16[8,128,256]{2,1,0:T(8,128)(2,1)S(1)}, u32[]{:S(2)}, u32[]{:S(2)}) collective-permute-start(bf16[8,128,256]{2,1,0:T(8,128)(2,1)S(1)} %dynamic-slice_convert_fusion.1), channel_id=1, source_target_pairs={{0,1},{1,0},{2,3},{3,2},{4,5},{5,4},{6,7},{7,6},{8,9},{9,8},{10,11... | collective-permute-start | bytes 1572872 | tf_op jit(solution)/shard_map/ppermute | solution.py:42
  174.4 17.1 %collective-permute-start.9 = (bf16[8,64,256]{2,1,0:T(8,128)(2,1)S(1)}, bf16[8,64,256]{2,1,0:T(8,128)(2,1)S(1)}, u32[]{:S(2)}, u32[]{:S(2)}) collective-permute-start(bf16[8,64,256]{2,1,0:T(8,128)(2,1)S(1)} %dynamic-slice_convert_fusion.4), channel_id=1, source_target_pairs={{0,1},{1,0},{2,3},{3,2},{4,5},{5,4},{6,7},{7,6},{8,9},{9,8},{10,11... | collective-permute-start | bytes 786440 | tf_op jit(solution)/shard_map/ppermute | solution.py:42
  177.7 34.2 %collective-permute-start.26 = (bf16[2,2,128,512]{3,2,1,0:T(8,128)(2,1)S(1)}, bf16[2,2,128,512]{3,2,1,0:T(8,128)(2,1)S(1)}, u32[]{:S(2)}, u32[]{:S(2)}) collective-permute-start(bf16[2,2,128,512]{3,2,1,0:T(8,128)(2,1)S(1)} %fusion.12), channel_id=1, source_target_pairs={{0,4},{2,6},{4,0},{6,2},{8,12},{10,14},{12,8},{14,10},{16,20},{18,... | collective-permute-start | bytes 1572872 | tf_op jit(solution)/shard_map/ppermute | solution.py:42
  179.2 19.5 %collective-permute-start.11 = (bf16[2,2,72,512]{3,2,1,0:T(8,128)(2,1)S(1)}, bf16[2,2,72,512]{3,2,1,0:T(8,128)(2,1)S(1)}, u32[]{:S(2)}, u32[]{:S(2)}) collective-permute-start(bf16[2,2,72,512]{3,2,1,0:T(8,128)(2,1)S(1)} %fusion.18), channel_id=1, source_target_pairs={{0,4},{2,6},{4,0},{6,2},{8,12},{10,14},{12,8},{14,10},{16,20},{18,... | collective-permute-start | bytes 884744 | tf_op jit(solution)/shard_map/ppermute | solution.py:42
  191.7 8.8 %collective-permute-start.10 = (bf16[2,2,64,256]{3,2,0,1:T(8,128)(2,1)S(1)}, bf16[2,2,64,256]{3,2,0,1:T(8,128)(2,1)S(1)}, u32[]{:S(2)}, u32[]{:S(2)}) collective-permute-start(bf16[2,2,64,256]{3,2,0,1:T(8,128)(2,1)S(1)} %fusion.36), channel_id=1, source_target_pairs={{0,4},{2,6},{4,0},{6,2},{8,12},{10,14},{12,8},{14,10},{16,20},{18,... | collective-permute-start | bytes 393224 | tf_op jit(solution)/shard_map/ppermute | solution.py:42
  205.8 14.0 %collective-permute-start.24 = (bf16[2,2,128,256]{3,2,0,1:T(8,128)(2,1)S(1)}, bf16[2,2,128,256]{3,2,0,1:T(8,128)(2,1)S(1)}, u32[]{:S(2)}, u32[]{:S(2)}) collective-permute-start(bf16[2,2,128,256]{3,2,0,1:T(8,128)(2,1)S(1)} %fusion.24), channel_id=1, source_target_pairs={{0,4},{2,6},{4,0},{6,2},{8,12},{10,14},{12,8},{14,10},{16,20},{18,... | collective-permute-start | bytes 786440 | tf_op jit(solution)/shard_map/ppermute | solution.py:42
  217.0 6.4 %collective-permute-start.27 = (bf16[4,128,256]{2,1,0:T(8,128)(2,1)S(1)}, bf16[4,128,256]{2,1,0:T(8,128)(2,1)S(1)}, u32[]{:S(2)}, u32[]{:S(2)}) collective-permute-start(bf16[4,128,256]{2,1,0:T(8,128)(2,1)S(1)} %dynamic-slice_convert_fusion.3), channel_id=1, source_target_pairs={{0,1},{1,0},{2,3},{3,2},{4,5},{5,4},{6,7},{7,6},{8,9},{9,8},{10,11... | collective-permute-start | bytes 786440 | tf_op jit(solution)/shard_map/ppermute | solution.py:42
  223.6 6.6 %collective-permute-start.28 = (bf16[2,256,256]{2,1,0:T(8,128)(2,1)S(1)}, bf16[2,256,256]{2,1,0:T(8,128)(2,1)S(1)}, u32[]{:S(2)}, u32[]{:S(2)}) collective-permute-start(bf16[2,256,256]{2,1,0:T(8,128)(2,1)S(1)} %fusion.25), channel_id=1, source_target_pairs={{0,8},{2,10},{4,12},{6,14},{8,0},{10,2},{12,4},{14,6},{16,24},{18,... | collective-permute-start | bytes 786440 | tf_op jit(solution)/shard_map/ppermute | solution.py:42
  225.2 13.8 %collective-permute-start.17 = (bf16[2,32,512]{2,1,0:T(8,128)(2,1)S(1)}, bf16[2,32,512]{2,1,0:T(8,128)(2,1)S(1)}, u32[]{:S(2)}, u32[]{:S(2)}) collective-permute-start(bf16[2,32,512]{2,1,0:T(8,128)(2,1)S(1)} %fusion.39), channel_id=1, source_target_pairs={{0,8},{2,10},{4,12},{6,14},{8,0},{10,2},{12,4},{14,6},{16,24},{18,... | collective-permute-start | bytes 196616 | tf_op jit(solution)/shard_map/ppermute | solution.py:42
  230.3 7.6 %collective-permute-start.29 = (bf16[256,256]{1,0:T(8,128)(2,1)S(1)}, bf16[256,256]{1,0:T(8,128)(2,1)S(1)}, u32[]{:S(2)}, u32[]{:S(2)}) collective-permute-start(bf16[256,256]{1,0:T(8,128)(2,1)S(1)} %fusion.34), channel_id=1, source_target_pairs={{0,16},{2,18},{4,20},{6,22},{8,24},{10,26},{12,28},{14,30},{16,0},... | collective-permute-start | bytes 393224 | tf_op jit(solution)/shard_map/ppermute | solution.py:42
  239.1 10.7 %collective-permute-start.18 = (bf16[2,2,32,512]{3,2,1,0:T(8,128)(2,1)S(1)}, bf16[2,2,32,512]{3,2,1,0:T(8,128)(2,1)S(1)}, u32[]{:S(2)}, u32[]{:S(2)}) collective-permute-start(bf16[2,2,32,512]{3,2,1,0:T(8,128)(2,1)S(1)} %pad_maximum_fusion.15), channel_id=1, source_target_pairs={{0,16},{2,18},{4,20},{6,22},{8,24},{10,26},{12,28},{14,30},{16,0},... | collective-permute-start | bytes 393224 | tf_op jit(solution)/shard_map/ppermute | solution.py:42
  244.0 7.8 %collective-permute-start.31 = (bf16[128,512]{1,0:T(8,128)(2,1)S(1)}, bf16[128,512]{1,0:T(8,128)(2,1)S(1)}, u32[]{:S(2)}, u32[]{:S(2)}) collective-permute-start(bf16[128,512]{1,0:T(8,128)(2,1)S(1)} %get-tuple-element.112), channel_id=1, source_target_pairs={{0,8},{2,10},{4,12},{6,14},{8,0},{10,2},{12,4},{14,6},{16,24},{18,... | collective-permute-start | bytes 393224 | tf_op jit(solution)/shard_map/ppermute | solution.py:42
  249.8 6.4 %collective-permute-start.19 = (bf16[2,2,2,32,512]{4,3,2,1,0:T(8,128)(2,1)S(1)}, bf16[2,2,2,32,512]{4,3,2,1,0:T(8,128)(2,1)S(1)}, u32[]{:S(2)}, u32[]{:S(2)}) collective-permute-start(bf16[2,2,2,32,512]{4,3,2,1,0:T(8,128)(2,1)S(1)} %pad_maximum_fusion.9), channel_id=1, source_target_pairs={{0,4},{2,6},{4,0},{6,2},{8,12},{10,14},{12,8},{14,10},{16,20},{18,... | collective-permute-start | bytes 786440 | tf_op jit(solution)/shard_map/ppermute | solution.py:42
  251.8 9.7 %collective-permute-start.32 = (bf16[2,128,512]{2,1,0:T(8,128)(2,1)S(1)}, bf16[2,128,512]{2,1,0:T(8,128)(2,1)S(1)}, u32[]{:S(2)}, u32[]{:S(2)}) collective-permute-start(bf16[2,128,512]{2,1,0:T(8,128)(2,1)S(1)} %pad_maximum_fusion.10), channel_id=1, source_target_pairs={{0,16},{2,18},{4,20},{6,22},{8,24},{10,26},{12,28},{14,30},{16,0},... | collective-permute-start | bytes 786440 | tf_op jit(solution)/shard_map/ppermute | solution.py:42
  256.4 7.8 %collective-permute-start.20 = (bf16[2,2,2,2,32,512]{5,4,3,1,0,2:T(8,128)(2,1)S(1)}, bf16[2,2,2,2,32,512]{5,4,3,1,0,2:T(8,128)(2,1)S(1)}, u32[]{:S(2)}, u32[]{:S(2)}) collective-permute-start(bf16[2,2,2,2,32,512]{5,4,3,1,0,2:T(8,128)(2,1)S(1)} %pad_maximum_fusion.5), channel_id=1, source_target_pairs={{0,2},{2,0},{4,6},{6,4},{8,10},{10,8},{12,14},{14,12},{16,18},{18,... | collective-permute-start | bytes 1572872 | tf_op jit(solution)/shard_map/ppermute | solution.py:42
  261.6 9.4 %collective-permute-start.33 = (bf16[2,2,128,512]{3,2,1,0:T(8,128)(2,1)S(1)}, bf16[2,2,128,512]{3,2,1,0:T(8,128)(2,1)S(1)}, u32[]{:S(2)}, u32[]{:S(2)}) collective-permute-start(bf16[2,2,128,512]{3,2,1,0:T(8,128)(2,1)S(1)} %pad_maximum_fusion.6), channel_id=1, source_target_pairs={{0,4},{2,6},{4,0},{6,2},{8,12},{10,14},{12,8},{14,10},{16,20},{18,... | collective-permute-start | bytes 1572872 | tf_op jit(solution)/shard_map/ppermute | solution.py:42
  271.2 26.0 %collective-permute-start.34 = (bf16[2,2,2,128,512]{4,3,1,0,2:T(8,128)(2,1)S(1)}, bf16[2,2,2,128,512]{4,3,1,0,2:T(8,128)(2,1)S(1)}, u32[]{:S(2)}, u32[]{:S(2)}) collective-permute-start(bf16[2,2,2,128,512]{4,3,1,0,2:T(8,128)(2,1)S(1)} %pad_maximum_fusion.4), channel_id=1, source_target_pairs={{0,2},{2,0},{4,6},{6,4},{8,10},{10,8},{12,14},{14,12},{16,18},{18,... | collective-permute-start | bytes 3145736 | tf_op jit(solution)/shard_map/ppermute | solution.py:42
  (51 other events, 369.8 us)

commit v2 on v1

v2 whole, which is shorter than its diff:
```python
import functools

import jax
import jax.numpy as jnp
from jax import lax
from jax.experimental import pallas as pl
from jax.experimental.pallas import tpu as pltpu
from jax.sharding import PartitionSpec as P

HEADS = 16
HEAD_DIM = 32


EPSILON = 1e-06
MOMENTUM_DECAY = 0.95
MATRIX_RATE = 0.5
VECTOR_RATE = 0.0002
KEEP_SHARE = 0.75
NEWTON_COEFFS = (3.4445, -4.775, 2.0315)


def bfloat(values):
    return values.astype(jnp.bfloat16)


def product(left_side, right_side):
    return jnp.dot(left_side, right_side, preferred_element_type=jnp.float32)


def norm_rows(values, gain_row, shift_row):
    center = values - jnp.mean(values, -1, keepdims=True)
    spread = jnp.mean(center * center, -1, keepdims=True)
    return center * lax.rsqrt(spread + EPSILON) * gain_row + shift_row


def bit_count(axis):
    return lax.axis_size(axis).bit_length() - 1


def swap(values, axis, bit):
    size = lax.axis_size(axis)
    return lax.ppermute(values, axis, [(i, i ^ (1 << bit)) for i in range(size)])


def my_bit(axis, bit):
    return (lax.axis_index(axis) >> bit) & 1


def far_bits():
    return list(range(2, bit_count("win")))


def gather_masks(low=0):
    masks = [0]
    for bit in far_bits() + [1, 0]:
        if bit >= low:
            masks += [mask | (1 << bit) for mask in masks]
    return masks


def gather_far(values):
    size = lax.axis_size("win")
    values = values[None]
    if len(far_bits()) == 2:
        others = [
            lax.ppermute(values, "win", [(i, i ^ mask) for i in range(size)]) for mask in (4, 8, 12)
        ]
        return jnp.concatenate([values] + others)
    for bit in far_bits():
        values = gather_bit(values, bit)
    return values


def gather_bit(values, bit):
    return jnp.concatenate([values, swap(values, "win", bit)])


def gather_stages(low=0):
    stages = [gather_far]
    for bit in (1, 0):
        if bit >= low:
            stages.append(functools.partial(gather_bit, bit=bit))
    return stages


def gather_blocks(values, low=0):
    for stage in gather_stages(low):
        values = stage(values)
    return values


def index_order(blocks):
    masks = gather_masks()
    by_mask = sorted(range(len(masks)), key=masks.__getitem__)
    places = lax.axis_index("win") ^ jnp.arange(len(masks))
    return blocks[jnp.array(by_mask)][places]


class Chain:
    def __init__(self, value, stages):
        self.value = value
        self.stages = list(stages)

    def step(self):
        if self.stages:
            self.value = self.stages.pop(0)(self.value)


def tie(*values):
    return lax.optimization_barrier(values)


def step_together(*chains):
    for chain in chains:
        chain.step()
    for chain, value in zip(chains, tie(*[chain.value for chain in chains])):
        chain.value = value


def halve_blocks(values, bit, bits_left):
    place = bits_left.index(bit)
    split = values.reshape((2,) * len(bits_left) + values.shape[1:])
    mine = my_bit("win", bit)
    kept = lax.dynamic_index_in_dim(split, mine, place, keepdims=False)
    sent = lax.dynamic_index_in_dim(split, 1 - mine, place, keepdims=False)
    total = kept + swap(bfloat(sent), "win", bit).astype(jnp.float32)
    left = [other for other in bits_left if other != bit]
    return total.reshape((-1,) + values.shape[1:]), left


def halve_columns(values):
    for bit in range(bit_count("rep")):
        half = values.shape[-1] // 2
        last = values.ndim - 1
        mine = my_bit("rep", bit)
        kept = lax.dynamic_slice_in_dim(values, mine * half, half, last)
        sent = lax.dynamic_slice_in_dim(values, (1 - mine) * half, half, last)
        values = kept + swap(bfloat(sent), "rep", bit).astype(jnp.float32)
    return values


def join_columns(values):
    values = bfloat(values)
    for bit in reversed(range(bit_count("rep"))):
        other = swap(values, "rep", bit)
        first = my_bit("rep", bit) == 0
        values = jnp.concatenate(
            [jnp.where(first, values, other), jnp.where(first, other, values)], axis=-1
        )
    return values.astype(jnp.float32)


def scatter_stages():
    bits = list(range(1, bit_count("win")))[::-1]
    left = bits[:-1]

    def first_stage(pair):
        return halve_columns(pair[0]), halve_blocks(pair[1], 1, bits)[0]

    def second_stage(pair):
        return halve_blocks(pair[0], 1, bits)[0], halve_columns(pair[1])

    def far_stage(number):
        def stage(values):
            if number == 0:
                values = jnp.concatenate(values, axis=1)
            rest = [other for other in left if other not in far_bits()[:number]]
            return halve_blocks(values, far_bits()[number], rest)[0]

        return stage

    return (
        [first_stage, second_stage]
        + [far_stage(number) for number in range(len(far_bits()))]
        + [lambda values: join_columns(values)[0]]
    )


def sum_over_rep(values):
    for bit in range(bit_count("rep")):
        low = bfloat(values)
        values = low.astype(jnp.float32) + swap(low, "rep", bit).astype(jnp.float32)
    return values


def off_diagonal_step(iterate, exact):
    high = bfloat(iterate)
    gram = dot_as(high, high, NT)
    if exact:
        rest = bfloat(iterate - high.astype(jnp.float32))
        gram = gram + dot_as(high, rest, NT) + dot_as(rest, high, NT)
    size = gram.shape[0]
    row_ids = lax.broadcasted_iota(jnp.int32, (size, size), 0)
    on_diagonal = row_ids == lax.broadcasted_iota(jnp.int32, (size, size), 1)
    own = jnp.where(on_diagonal, gram, 0.0)
    own_column = jnp.sum(own, 1, keepdims=True)
    own_row = jnp.sum(own, 0, keepdims=True)
    off = jnp.where(on_diagonal, 0.0, gram)
    off_low = bfloat(off)
    square = product(off_low, off_low) + (own_column + own_row) * off
    poly = NEWTON_COEFFS[1] * off + NEWTON_COEFFS[2] * square
    poly_own = jnp.sum(jnp.where(on_diagonal, poly, 0.0), 1, keepdims=True)
    factor = (
        NEWTON_COEFFS[0]
        + poly_own
        + own_column * (NEWTON_COEFFS[1] + NEWTON_COEFFS[2] * own_column)
    )
    poly = jnp.where(on_diagonal, 0.0, poly)
    poly_high = bfloat(poly)
    moved = product(poly_high, high)
    if exact:
        poly_rest = bfloat(poly - poly_high.astype(jnp.float32))
        moved = moved + product(poly_high, rest) + product(poly_rest, high)
    return factor * iterate + moved


def unit_scale(values):
    total = jnp.sum(jnp.sum(values * values, 1, keepdims=True), 0, keepdims=True)
    return values * (1.0 / (jnp.sqrt(total) + EPSILON))


def block_start(place_ref, masks, block, rows, shift=0):
    if masks is None:
        return block * rows
    return pl.multiple_of(((place_ref[1] ^ masks[block]) >> shift) * rows, rows)


def big_newton_kernel(folds, masks, place_ref, blocks_ref, out_ref, iterate_ref, turned_ref):
    blocks, rows, width = blocks_ref.shape
    part = rows // folds

    @pl.when(place_ref[0] == 0)
    def _():
        for block in range(blocks):
            for fold in range(folds):
                start = block_start(place_ref, masks, block, part)
                iterate_ref[pl.ds(start, part), fold * width : (fold + 1) * width] = blocks_ref[block, fold * part : (fold + 1) * part, :].astype(jnp.float32)

    @pl.when(place_ref[0] != 0)
    def _():
        for block in range(blocks):
            start = block_start(place_ref, masks, block, rows)
            iterate_ref[:, pl.ds(start, rows)] = blocks_ref[block].astype(jnp.float32).T

    iterate_ref[...] = unit_scale(iterate_ref[...])

    @pl.loop(0, 5)
    def _(_):
        iterate_ref[...] = off_diagonal_step(iterate_ref[...], False)

    @pl.when(place_ref[0] == 0)
    def _():
        start = pl.multiple_of(place_ref[1] * part, part)
        for fold in range(folds):
            out_ref[fold * part : (fold + 1) * part, :] = bfloat(
                iterate_ref[pl.ds(start, part), fold * width : (fold + 1) * width]
            )

    @pl.when(place_ref[0] != 0)
    def _():
        span = max(rows, 128)
        start = pl.multiple_of(place_ref[1] * rows // span * span, span)
        turned_ref[...] = iterate_ref[:, pl.ds(start, span)].T * float(folds) ** 0.5
        inner = pl.multiple_of(place_ref[1] * rows - start, rows)
        out_ref[...] = bfloat(turned_ref[pl.ds(inner, rows), :])


def small_newton_kernel(masks, place_ref, blocks_ref, out_ref, iterate_ref):
    blocks, matrices, rows, width = blocks_ref.shape
    for number in range(matrices):
        for block in range(blocks):
            start = block_start(place_ref, masks, block, rows, 1)
            iterate_ref[number, pl.ds(start, rows), :] = blocks_ref[block, number].astype(
                jnp.float32
            )

    @pl.loop(0, matrices)
    def _(number):
        iterate_ref[number] = unit_scale(iterate_ref[number])

        @pl.loop(0, 2)
        def _(_):
            iterate_ref[number] = off_diagonal_step(iterate_ref[number], False)

        @pl.loop(0, 3)
        def _(_):
            iterate_ref[number] = off_diagonal_step(iterate_ref[number], True)

    start = pl.multiple_of((place_ref[1] if masks is None else place_ref[1] >> 1) * rows, rows)
    for number in range(matrices):
        out_ref[number] = bfloat(iterate_ref[number, pl.ds(start, rows), :])


def newton_call(kernel, name, place, blocks, out_dims, scratch_dims, flops):
    return pl.pallas_call(
        kernel,
        in_specs=[
            pl.BlockSpec(memory_space=pltpu.SMEM),
            pl.BlockSpec(memory_space=pltpu.VMEM),
        ],
        out_specs=pl.BlockSpec(memory_space=pltpu.VMEM),
        out_shape=shape_of(out_dims, jnp.bfloat16),
        scratch_shapes=[pltpu.VMEM(dims, jnp.float32) for dims in scratch_dims],
        compiler_params=pltpu.CompilerParams(vmem_limit_bytes=VMEM_LIMIT),
        cost_estimate=pl.CostEstimate(
            flops=flops, bytes_accessed=2 * blocks.size, transcendentals=0
        ),
        name=name,
    )(place, blocks)


def big_update(place, blocks, folds, masks):
    win, rows, width = blocks.shape
    return newton_call(
        functools.partial(big_newton_kernel, folds, masks),
        "big_newton",
        place,
        blocks,
        (rows, width),
        [(width, win * rows), (max(rows, 128), width)],
        2 * 5 * width * width * (2 * win * rows + width),
    )


def small_update(place, blocks, masks):
    win, matrices, rows, width = blocks.shape
    return newton_call(
        functools.partial(small_newton_kernel, masks),
        "small_newton",
        place,
        blocks,
        (matrices, rows, width),
        [(matrices, width, width)],
        2 * 27 * matrices * width**3,
    )


def own_rows(matrix, rows_here):
    return lax.dynamic_slice_in_dim(matrix, lax.axis_index("win") * rows_here, rows_here, 0)


def fold_columns(rows, width):
    count, columns = rows.shape
    return rows.reshape(count, columns // width, width).swapaxes(0, 1).reshape(-1, width)


def unfold_columns(rows, folds):
    total, width = rows.shape
    return rows.reshape(folds, total // folds, width).swapaxes(0, 1).reshape(-1, folds * width)


def pick_owner(first, here, there):
    return jnp.where(first, here, there), jnp.where(first, there, here)


def every_update(place, big_rows, small_rows, folds):
    updates = []
    for number, rows in enumerate(big_rows):
        here = jnp.stack([jnp.int32(number), place[1]])
        blocks = index_order(gather_blocks(bfloat(rows)))
        updates.append(big_update(here, blocks, folds, None))
    blocks = index_order(gather_blocks(bfloat(small_rows)))
    return updates[0], updates[1], small_update(place, blocks, None)


GROUP_HEADS = 128 // HEAD_DIM
SCORE_SCALE = HEAD_DIM ** (-0.5)
LOG2_E = 1.4426950408889634
VMEM_LIMIT = 44 * 1024 * 1024
WINDOW_COST = 10**9
NT = (((1,), (1,)), ((), ()))
TN = (((0,), (0,)), ((), ()))


def dot_as(left_side, right_side, dims):
    return lax.dot_general(left_side, right_side, dims, preferred_element_type=jnp.float32)


def spread_heads(part, lane_head):
    return bfloat(
        jnp.concatenate(
            [jnp.where(lane_head == head, part, 0.0) for head in range(GROUP_HEADS)], axis=0
        )
    )


def join_heads(spread, lane_head, rows):
    joined = spread[:rows]
    for head in range(1, GROUP_HEADS):
        joined = jnp.where(lane_head == head, spread[head * rows : (head + 1) * rows], joined)
    return joined


def column_softmax(scores, bias_column):
    scores = scores + bias_column
    raised = jnp.exp2((scores - jnp.max(scores, 0, keepdims=True)) * (SCORE_SCALE * LOG2_E))
    return raised * (1.0 / jnp.sum(raised, 0, keepdims=True))


def load_windows(tokens_ref, region_ref, fill_ref, count, seq_len, padded, step):
    for window in range(count):
        base = window * padded
        fill_ref[base : base + seq_len, :] = tokens_ref[0, window].astype(jnp.float32)
        fill_ref[base : base + 1, :] = region_ref[pl.ds(step * count + window, 1), :]


def window_forward_kernel(
    count,
    seq_len,
    padded,
    tokens_ref,
    region_ref,
    bias_ref,
    keep_ref,
    qkv_ref,
    out_ref,
    vec_ref,
    norm_out,
    proj_out,
    mix_out,
    after_out,
    fill_ref,
    mix_ref,
    scores_ref,
    probs_ref,
):
    step = pl.program_id(0)
    width = tokens_ref.shape[-1]

    @pl.when(step == 0)
    def _():
        fill_ref[...] = jnp.zeros_like(fill_ref)

    load_windows(tokens_ref, region_ref, fill_ref, count, seq_len, padded, step)
    flat = fill_ref[...]
    normed = bfloat(norm_rows(flat, vec_ref[2:3, :], vec_ref[3:4, :]))
    lane_head = lax.broadcasted_iota(jnp.int32, (padded, 128), 1) // HEAD_DIM
    query = product(normed, qkv_ref[0]) + vec_ref[6:7, :]
    keyset = product(normed, qkv_ref[1])
    values = product(normed, qkv_ref[2]) + vec_ref[7:8, :]
    pairs = [(window, group) for window in range(count) for group in range(width // 128)]
    for window in range(count):
        rows = slice(window * padded, (window + 1) * padded)
        norm_out[window] = normed[rows]
        proj_out[window, :, :width] = bfloat(query[rows])
        proj_out[window, :, width : 2 * width] = bfloat(keyset[rows])
        proj_out[window, :, 2 * width :] = bfloat(values[rows])
    for number, (window, group) in enumerate(pairs):
        rows = slice(window * padded, (window + 1) * padded)
        lanes = slice(group * 128, (group + 1) * 128)
        spread = spread_heads(query[rows, lanes], lane_head)
        scores_ref[number] = dot_as(bfloat(keyset[rows, lanes]), spread, NT)
    for number, (window, group) in enumerate(pairs):
        probs_ref[number] = bfloat(column_softmax(scores_ref[number], bias_ref[window]))
    for number, (window, group) in enumerate(pairs):
        rows = slice(window * padded, (window + 1) * padded)
        lanes = slice(group * 128, (group + 1) * 128)
        mixed = dot_as(probs_ref[number], bfloat(values[rows, lanes]), TN)
        mix_ref[rows, lanes] = join_heads(mixed, lane_head, padded)
    mixed_low = bfloat(mix_ref[...])
    branch = product(mixed_low, out_ref[...]) + vec_ref[8:9, :]
    for window in range(count):
        rows = slice(window * padded, (window + 1) * padded)
        mix_out[window] = mixed_low[rows]
        after_out[window] = flat[rows] + keep_ref[window] * branch[rows]


def window_backward_kernel(
    count,
    first_step,
    last,
    seq_len,
    padded,
    tokens_ref,
    region_ref,
    bias_ref,
    keep_ref,
    qkv_ref,
    out_ref,
    vec_ref,
    proj_ref,
    after_grad_ref,
    region_keep_ref,
    sums_before_ref,
    *rest,
):
    scratch_count = 8
    if last:
        region_branch_out, region_mix_out = rest[-scratch_count - 2 : -scratch_count]
        rest = rest[: -scratch_count - 2] + rest[-scratch_count:]
    (
        region_grad_out,
        sums_out,
        grad_out,
        proj_grad_out,
        branch_grad_out,
        fill_ref,
        proj_grad_ref,
        spread_ref,
        spread_grad_ref,
        scores_ref,
        probs_grad_ref,
        probs_ref,
        score_grad_ref,
    ) = rest[-13:]
    step = pl.program_id(0) + first_step
    width = tokens_ref.shape[-1]

    @pl.when(pl.program_id(0) == 0)
    def _():
        fill_ref[...] = jnp.zeros_like(fill_ref)
        sums_out[...] = sums_before_ref[...]
        if first_step == 0:
            region_grad_out[...] = jnp.zeros_like(region_grad_out)
        else:
            region_grad_out[...] = rest[0][...]

    load_windows(tokens_ref, region_ref, fill_ref, count, seq_len, padded, step)
    lane_head = lax.broadcasted_iota(jnp.int32, (padded, 128), 1) // HEAD_DIM
    branch_grad = bfloat(
        jnp.concatenate(
            [keep_ref[window] * after_grad_ref[window] for window in range(count)], axis=0
        )
    )
    mix_grad = dot_as(branch_grad, out_ref[...], NT)
    for window in range(count):
        branch_grad_out[window] = branch_grad[window * padded : (window + 1) * padded]
    pairs = [(window, group) for window in range(count) for group in range(width // 128)]

    def lanes_of(part, group):
        return slice(part * width + group * 128, part * width + (group + 1) * 128)

    for number, (window, group) in enumerate(pairs):
        query = proj_ref[window, :, lanes_of(0, group)].astype(jnp.float32)
        spread_ref[number] = spread_heads(query, lane_head)
        rows = slice(window * padded, (window + 1) * padded)
        spread_grad_ref[number] = spread_heads(mix_grad[rows, lanes_of(0, group)], lane_head)
    for number, (window, group) in enumerate(pairs):
        scores_ref[number] = dot_as(
            proj_ref[window, :, lanes_of(1, group)], spread_ref[number], NT
        )
        probs_grad_ref[number] = dot_as(
            proj_ref[window, :, lanes_of(2, group)], spread_grad_ref[number], NT
        )
    for number, (window, group) in enumerate(pairs):
        probs = column_softmax(scores_ref[number], bias_ref[window])
        weighted = probs * probs_grad_ref[number]
        probs_ref[number] = bfloat(probs)
        score_grad_ref[number] = bfloat(weighted - probs * jnp.sum(weighted, 0, keepdims=True))
    for number, (window, group) in enumerate(pairs):
        rows = slice(window * padded, (window + 1) * padded)
        proj_grad_ref[rows, lanes_of(2, group)] = product(
            probs_ref[number], spread_grad_ref[number]
        )
        proj_grad_ref[rows, lanes_of(1, group)] = (
            product(score_grad_ref[number], spread_ref[number]) * SCORE_SCALE
        )
    for number, (window, group) in enumerate(pairs):
        rows = slice(window * padded, (window + 1) * padded)
        query_grad = dot_as(score_grad_ref[number], proj_ref[window, :, lanes_of(1, group)], TN)
        proj_grad_ref[rows, lanes_of(0, group)] = (
            join_heads(query_grad, lane_head, padded) * SCORE_SCALE
        )
    proj_grad = bfloat(proj_grad_ref[...])
    norm_grad = sum(
        dot_as(proj_grad[:, number * width : (number + 1) * width], qkv_ref[number], NT)
        for number in range(3)
    )
    flat = fill_ref[...]
    center = flat - jnp.mean(flat, -1, keepdims=True)
    scale = lax.rsqrt(jnp.mean(center * center, -1, keepdims=True) + EPSILON)
    hat = center * scale
    hat_grad = norm_grad * vec_ref[2:3, :]
    flat_grad = scale * (
        hat_grad
        - jnp.mean(hat_grad, -1, keepdims=True)
        - hat * jnp.mean(hat_grad * hat, -1, keepdims=True)
    )
    proj_sums = jnp.sum(proj_grad.astype(jnp.float32), 0, keepdims=True)
    sums_out[2:3, :] += jnp.sum(norm_grad * hat, 0, keepdims=True)
    sums_out[3:4, :] += jnp.sum(norm_grad, 0, keepdims=True)
    sums_out[6:7, :] += proj_sums[:, :width]
    sums_out[7:8, :] += proj_sums[:, 2 * width :]
    sums_out[8:9, :] += jnp.sum(branch_grad.astype(jnp.float32), 0, keepdims=True)
    for window in range(count):
        rows = slice(window * padded, (window + 1) * padded)
        proj_grad_out[window] = proj_grad[rows]
        seq_grad = after_grad_ref[window] + flat_grad[rows]
        for group in range(width // 128):
            lanes = slice(group * 128, (group + 1) * 128)
            grad_out[window, pl.ds(group, seq_len, stride=width // 128), :] = seq_grad[
                :seq_len, lanes
            ]
        region_grad_out[pl.ds(step * count + window, 1), :] = seq_grad[0:1]

    if last:

        @pl.when(pl.program_id(0) == pl.num_programs(0) - 1)
        def _():
            region_branch = bfloat(region_keep_ref[...] * region_grad_out[...])
            sums_out[8:9, :] += jnp.sum(region_branch.astype(jnp.float32), 0, keepdims=True)
            region_branch_out[...] = region_branch
            region_mix_out[...] = bfloat(dot_as(region_branch, out_ref[...], NT))


def window_step(windows):
    return next(count for count in (4, 2, 1) if windows % count == 0)


def whole_spec(shape):
    return pl.BlockSpec(shape, lambda step: (0,) * len(shape))


def step_spec(count, *rest):
    return pl.BlockSpec((count,) + rest, lambda step: (step,) + (0,) * len(rest))


def token_spec(count, *rest):
    return pl.BlockSpec((1, count) + rest, lambda step: (0, step) + (0,) * len(rest))


def kept_spec():
    return pl.BlockSpec(memory_space=pltpu.VMEM)


def in_hbm(values):
    return pltpu.with_memory_space_constraint(values, pltpu.HBM)


def hbm_shape(dims, kind=jnp.float32):
    return pltpu.HBM(dims, kind)


def shape_of(dims, kind=jnp.float32):
    return jax.ShapeDtypeStruct(dims, kind)


def window_forward(tokens, region, bias, keep, qkv_weight, out_weight, vectors, padded):
    _, windows, seq_len, width = tokens.shape
    count = window_step(windows)
    pairs = count * width // 128
    return pl.pallas_call(
        functools.partial(window_forward_kernel, count, seq_len, padded),
        grid=(windows // count,),
        in_specs=[
            token_spec(count, seq_len, width),
            whole_spec(region.shape),
            step_spec(count, padded, 1),
            step_spec(count, 1, 1),
            kept_spec(),
            kept_spec(),
            whole_spec(vectors.shape),
        ],
        out_specs=[
            step_spec(count, padded, width),
            step_spec(count, padded, 3 * width),
            step_spec(count, padded, width),
            step_spec(count, padded, width),
        ],
        out_shape=[
            hbm_shape((windows, padded, width), jnp.bfloat16),
            hbm_shape((windows, padded, 3 * width), jnp.bfloat16),
            hbm_shape((windows, padded, width), jnp.bfloat16),
            hbm_shape((windows, padded, width)),
        ],
        scratch_shapes=[
            pltpu.VMEM((count * padded, width), jnp.float32),
            pltpu.VMEM((count * padded, width), jnp.float32),
            pltpu.VMEM((pairs, padded, GROUP_HEADS * padded), jnp.float32),
            pltpu.VMEM((pairs, padded, GROUP_HEADS * padded), jnp.bfloat16),
        ],
        compiler_params=pltpu.CompilerParams(vmem_limit_bytes=VMEM_LIMIT),
        name="window_forward",
    )(in_hbm(tokens), region, bias, keep, qkv_weight, out_weight, vectors)


def window_backward(
    tokens,
    region,
    bias,
    keep,
    qkv_weight,
    out_weight,
    vectors,
    proj,
    after_grad,
    region_keep,
    before,
    steps,
    padded,
):
    _, windows, seq_len, width = tokens.shape
    count = window_step(windows)
    first_step, last_step = steps
    here = (last_step - first_step) * count
    pairs = count * width // 128
    spread_rows = GROUP_HEADS * padded

    def moved(*dims, lead=0):
        zeros = (0,) * (len(dims) - 1)
        if lead:
            return pl.BlockSpec((1,) + dims, lambda step: (0, step + first_step) + zeros)
        return pl.BlockSpec(dims, lambda step: (step + first_step,) + zeros)

    flat_rows = seq_len * width // 128

    grad_before, sums_before, region_before = before
    operands = [in_hbm(tokens), region, bias, keep, qkv_weight, out_weight, vectors]
    operands += [in_hbm(proj), in_hbm(after_grad), region_keep, in_hbm(sums_before)]
    in_specs = [
        moved(count, seq_len, width, lead=1),
        whole_spec(region.shape),
        moved(count, padded, 1),
        moved(count, 1, 1),
        kept_spec(),
        kept_spec(),
        whole_spec(vectors.shape),
        moved(count, padded, 3 * width),
        moved(count, padded, width),
        whole_spec(region_keep.shape),
        whole_spec(sums_before.shape),
    ]
    aliases = {}
    if first_step:
        aliases = {len(operands) + 1: 2}
        operands += [in_hbm(region_before), in_hbm(grad_before)]
        in_specs += [whole_spec(region.shape), pl.BlockSpec(memory_space=pl.ANY)]
    last = last_step * count == windows
    out_specs = [
        whole_spec(region.shape),
        whole_spec(vectors.shape),
        moved(count, flat_rows, 128),
        step_spec(count, padded, 3 * width),
        step_spec(count, padded, width),
    ]
    out_shape = [
        hbm_shape(region.shape),
        hbm_shape(vectors.shape),
        hbm_shape((windows, flat_rows, 128)),
        hbm_shape((here, padded, 3 * width), jnp.bfloat16),
        hbm_shape((here, padded, width), jnp.bfloat16),
    ]
    if last:
        out_specs += [whole_spec(region.shape)] * 2
        out_shape += [shape_of(region.shape, jnp.bfloat16)] * 2
    return pl.pallas_call(
        functools.partial(window_backward_kernel, count, first_step, last, seq_len, padded),
        grid=(last_step - first_step,),
        in_specs=in_specs,
        out_specs=out_specs,
        out_shape=out_shape,
        scratch_shapes=[
            pltpu.VMEM((count * padded, width), jnp.float32),
            pltpu.VMEM((count * padded, 3 * width), jnp.float32),
            pltpu.VMEM((pairs, spread_rows, 128), jnp.bfloat16),
            pltpu.VMEM((pairs, spread_rows, 128), jnp.bfloat16),
            pltpu.VMEM((pairs, padded, spread_rows), jnp.float32),
            pltpu.VMEM((pairs, padded, spread_rows), jnp.float32),
            pltpu.VMEM((pairs, padded, spread_rows), jnp.bfloat16),
            pltpu.VMEM((pairs, padded, spread_rows), jnp.bfloat16),
        ],
        input_output_aliases=aliases,
        compiler_params=pltpu.CompilerParams(vmem_limit_bytes=VMEM_LIMIT),
        cost_estimate=pl.CostEstimate(
            flops=here * WINDOW_COST, bytes_accessed=here * padded * width * 20, transcendentals=0
        ),
        name="window_backward",
    )(*operands)


def insert_kernel(rows_ref, region_ref, out_ref):
    out_ref[...] = rows_ref[...]
    for window in range(rows_ref.shape[0]):
        for group in range(region_ref.shape[1] // 128):
            out_ref[window, group : group + 1, :] = region_ref[
                window : window + 1, group * 128 : (group + 1) * 128
            ]


def insert_regions(grad, region_grad):
    rows = pl.BlockSpec((grad.shape[0], 8, 128), lambda step: (0, 0, 0))
    return pl.pallas_call(
        insert_kernel,
        grid=(1,),
        in_specs=[rows, whole_spec(region_grad.shape)],
        out_specs=rows,
        out_shape=shape_of(grad.shape),
        input_output_aliases={0: 0},
        compiler_params=pltpu.CompilerParams(vmem_limit_bytes=VMEM_LIMIT),
        name="insert_regions",
    )(grad, region_grad)


GELU_IN = 0.7978845608028654
GELU_CUBE = 0.044715


def gelu_both(values):
    square = values * values
    bent = jnp.tanh(values * (GELU_IN + (GELU_IN * GELU_CUBE) * square))
    share = 0.5 + 0.5 * bent
    slope = share + (0.5 * values) * (1.0 - bent * bent) * (
        GELU_IN + (3.0 * GELU_IN * GELU_CUBE) * square
    )
    return values * share, slope


def split_cores(values, core):
    own_first = core == 0
    kept = jnp.where(own_first, values[:, 0], values[:, 1])
    sent = jnp.where(own_first, values[:, 1], values[:, 0])
    return kept, bfloat(sent)


def mlp_kernel(
    count,
    seq_len,
    padded,
    place_ref,
    after_ref,
    cot_ref,
    keep_ref,
    vec_ref,
    up_ref,
    down_ref,
    out_ref,
    grad_ref,
    sums_ref,
    up_kept,
    up_sent,
    down_kept,
    down_sent,
    cot_fill,
    up_total,
    down_total,
):
    step = pl.program_id(0)
    width = up_ref.shape[0]
    folds = up_ref.shape[1] // width

    @pl.when(step == 0)
    def _():
        cot_fill[...] = jnp.zeros_like(cot_fill)
        sums_ref[...] = jnp.zeros_like(sums_ref)
        up_total[...] = jnp.zeros_like(up_total)
        down_total[...] = jnp.zeros_like(down_total)

    keeps = []
    for window in range(count):
        base = window * padded
        cot_fill[base : base + seq_len, :] = cot_ref[0, window].astype(jnp.float32)
        keeps.append(jnp.broadcast_to(keep_ref[window], (padded, 1)))
    keep = jnp.concatenate(keeps, axis=0)
    flat = after_ref[...]
    center = flat - jnp.mean(flat, -1, keepdims=True)
    scale = lax.rsqrt(jnp.mean(center * center, -1, keepdims=True) + EPSILON)
    hat = center * scale
    normed = bfloat(hat * vec_ref[4:5, :] + vec_ref[5:6, :])
    normed_turned = normed.T
    cot = cot_fill[...]
    branch_grad = bfloat(keep * cot)
    branch = jnp.zeros_like(flat)
    norm_grad = jnp.zeros_like(flat)
    for fold in range(folds):
        lanes = slice(fold * width, (fold + 1) * width)
        up_part, down_part = up_ref[:, lanes], down_ref[lanes, :]
        hidden = product(normed, up_part) + vec_ref[10 + fold : 11 + fold, :]
        act, slope = gelu_both(hidden)
        act = bfloat(act)
        branch += product(act, down_part)
        hidden_grad = bfloat(slope * dot_as(branch_grad, down_part, NT))
        norm_grad += dot_as(hidden_grad, up_part, NT)
        up_total[fold] += product(normed_turned, hidden_grad)
        down_total[fold] += dot_as(act, branch_grad, TN)
        sums_ref[10 + fold : 11 + fold, :] += jnp.sum(
            hidden_grad.astype(jnp.float32), 0, keepdims=True
        )
    output = bfloat(flat + keep * (branch + vec_ref[9:10, :]))
    hat_grad = norm_grad * vec_ref[4:5, :]
    flat_grad = cot + scale * (
        hat_grad
        - jnp.mean(hat_grad, -1, keepdims=True)
        - hat * jnp.mean(hat_grad * hat, -1, keepdims=True)
    )
    sums_ref[4:5, :] += jnp.sum(norm_grad * hat, 0, keepdims=True)
    sums_ref[5:6, :] += jnp.sum(norm_grad, 0, keepdims=True)
    sums_ref[9:10, :] += jnp.sum(branch_grad.astype(jnp.float32), 0, keepdims=True)
    grad_ref[...] = flat_grad
    for window in range(count):
        out_ref[0, window] = output[window * padded : window * padded + seq_len]

    @pl.when(step == pl.num_programs(0) - 1)
    def _():
        core = place_ref[1] % 2
        blocks, _, rows, _ = up_kept.shape
        for fold in range(folds):
            total = up_total[fold].reshape(blocks, 2, rows, width)
            up_kept[:, fold], up_sent[:, fold] = split_cores(total, core)
        blocks, rows, _ = down_kept.shape
        here = blocks // folds
        for fold in range(folds):
            total = down_total[fold].reshape(here, 2, rows, width)
            part = slice(fold * here, (fold + 1) * here)
            down_kept[part], down_sent[part] = split_cores(total, core)


def mlp(place, after, cotangent, keep, vectors, up_weight, down_weight, padded, win_count):
    _, windows, seq_len, width = cotangent.shape
    count = window_step(windows)
    rows = count * padded
    folds = up_weight.shape[1] // width
    half = win_count // 2
    up_rows = width // win_count
    up_dims = (half, folds, up_rows, width)
    down_dims = (half, up_rows * folds, width)
    flat_rows = pl.BlockSpec((rows, width), lambda step: (step, 0))
    output, grad, sums, kept_up, sent_up, kept_down, sent_down = pl.pallas_call(
        functools.partial(mlp_kernel, count, seq_len, padded),
        grid=(windows // count,),
        in_specs=[
            pl.BlockSpec(memory_space=pltpu.SMEM),
            flat_rows,
            token_spec(count, seq_len, width),
            step_spec(count, 1, 1),
            whole_spec(vectors.shape),
            kept_spec(),
            kept_spec(),
        ],
        out_specs=[
            token_spec(count, seq_len, width),
            flat_rows,
            whole_spec(vectors.shape),
            whole_spec(up_dims),
            whole_spec(up_dims),
            whole_spec(down_dims),
            whole_spec(down_dims),
        ],
        out_shape=[
            hbm_shape(cotangent.shape, jnp.bfloat16),
            hbm_shape(after.shape),
            hbm_shape(vectors.shape),
            hbm_shape(up_dims),
            hbm_shape(up_dims, jnp.bfloat16),
            hbm_shape(down_dims),
            hbm_shape(down_dims, jnp.bfloat16),
        ],
        scratch_shapes=[
            pltpu.VMEM((rows, width), jnp.float32),
            pltpu.VMEM((folds, width, width), jnp.float32),
            pltpu.VMEM((folds, width, width), jnp.float32),
        ],
        compiler_params=pltpu.CompilerParams(vmem_limit_bytes=VMEM_LIMIT),
        cost_estimate=pl.CostEstimate(
            flops=12 * after.size * width * folds,
            bytes_accessed=16 * after.size,
            transcendentals=0,
        ),
        name="mlp",
    )(place, in_hbm(after), in_hbm(cotangent), keep, vectors, up_weight, down_weight)
    up_half = (kept_up.reshape(down_dims), sent_up.reshape(down_dims))
    return output, grad, sums, up_half, (kept_down, sent_down)


def image_bias(keys_ref, queries_ref):
    return jnp.where(keys_ref[...] == queries_ref[...], 0.0, -1e30)


def region_forward_kernel(
    all_ref,
    own_ref,
    keep_ref,
    key_image_ref,
    query_image_ref,
    qkv_ref,
    out_ref,
    vec_ref,
    norm_out,
    proj_out,
    mix_out,
    new_out,
):
    rows, width = own_ref.shape
    vec = vec_ref[...]
    normed = bfloat(norm_rows(all_ref[...].astype(jnp.float32), vec[0:1], vec[1:2]))
    norm_out[...] = normed
    query = bfloat(product(normed, qkv_ref[0]) + vec[6:7])
    keyset = bfloat(product(normed, qkv_ref[1]))
    values = bfloat(product(normed, qkv_ref[2]) + vec[7:8])
    proj_out[:, :width] = query
    proj_out[:, width : 2 * width] = keyset
    proj_out[:, 2 * width :] = values
    region = own_ref[...].astype(jnp.float32)
    own_norm = bfloat(norm_rows(region, vec[0:1], vec[1:2]))
    own_query = product(own_norm, qkv_ref[0]) + vec[6:7]
    bias = image_bias(key_image_ref, query_image_ref)
    lane_head = lax.broadcasted_iota(jnp.int32, (rows, 128), 1) // HEAD_DIM
    parts = []
    for group in range(width // 128):
        lanes = slice(group * 128, (group + 1) * 128)
        spread = spread_heads(own_query[:, lanes], lane_head)
        probs = column_softmax(dot_as(keyset[:, lanes], spread, NT), bias)
        mixed = dot_as(bfloat(probs), values[:, lanes], TN)
        parts.append(join_heads(mixed, lane_head, rows))
    mixed_low = bfloat(jnp.concatenate(parts, axis=1))
    mix_out[...] = mixed_low
    branch = product(mixed_low, out_ref[...]) + vec[8:9]
    new_out[...] = region + keep_ref[...] * branch


def region_forward(all_rows, own_rows_, keep, key_images, query_images, qkv_weight, out_weight, vectors):
    total, width = all_rows.shape
    return pl.pallas_call(
        region_forward_kernel,
        out_shape=[
            hbm_shape((total, width), jnp.bfloat16),
            hbm_shape((total, 3 * width), jnp.bfloat16),
            hbm_shape(own_rows_.shape, jnp.bfloat16),
            shape_of(own_rows_.shape),
        ],
        compiler_params=pltpu.CompilerParams(vmem_limit_bytes=VMEM_LIMIT),
        name="region_forward",
    )(all_rows, own_rows_, keep, key_images, query_images, qkv_weight, out_weight, vectors)


def region_backward_kernel(
    place_ref,
    all_ref,
    norm_ref,
    proj_ref,
    mix_grad_ref,
    key_image_ref,
    query_image_ref,
    new_grad_ref,
    qkv_ref,
    vec_ref,
    grad_out,
    weight_out,
    sums_out,
    bias_ref,
    proj_grad_ref,
    region_grad_ref,
    weight_ref,
    scores_ref,
    probs_grad_ref,
    probs_ref,
    score_grad_ref,
):
    total, width = all_ref.shape
    rows = new_grad_ref.shape[0]
    bias_ref[...] = image_bias(key_image_ref, query_image_ref)
    lane_head = lax.broadcasted_iota(jnp.int32, (total, 128), 1) // HEAD_DIM

    @pl.loop(0, width // 128)
    def _(group):
        query_lanes = pl.ds(pl.multiple_of(group * 128, 128), 128)
        key_lanes = pl.ds(pl.multiple_of(width + group * 128, 128), 128)
        value_lanes = pl.ds(pl.multiple_of(2 * width + group * 128, 128), 128)
        query = proj_ref[:, query_lanes]
        key_low = proj_ref[:, key_lanes]
        value_low = proj_ref[:, value_lanes]
        mix_grad = mix_grad_ref[:, query_lanes]
        heads = range(GROUP_HEADS)
        head_query = [jnp.where(lane_head == head, query, jnp.zeros_like(query)) for head in heads]
        head_grad = [
            jnp.where(lane_head == head, mix_grad, jnp.zeros_like(mix_grad)) for head in heads
        ]
        for head in heads:
            scores_ref[head] = dot_as(key_low, head_query[head], NT)
            probs_grad_ref[head] = dot_as(value_low, head_grad[head], NT)
        for head in heads:
            probs = column_softmax(scores_ref[head], bias_ref[...])
            weighted = probs * probs_grad_ref[head]
            probs_ref[head] = bfloat(probs)
            score_grad_ref[head] = bfloat(weighted - probs * jnp.sum(weighted, 0, keepdims=True))
        zero = jnp.zeros((total, 128), jnp.float32)
        value_grad = sum((product(probs_ref[head], head_grad[head]) for head in heads), zero)
        key_grad = sum((product(score_grad_ref[head], head_query[head]) for head in heads), zero)
        query_grad = zero
        for head in heads:
            head_part = dot_as(score_grad_ref[head], key_low, TN)
            query_grad = jnp.where(lane_head == head, head_part, query_grad)
        proj_grad_ref[:, query_lanes] = bfloat(query_grad * SCORE_SCALE)
        proj_grad_ref[:, key_lanes] = bfloat(key_grad * SCORE_SCALE)
        proj_grad_ref[:, value_lanes] = bfloat(value_grad)

    proj_grad = proj_grad_ref[...]
    norm_grad = sum(
        dot_as(proj_grad[:, number * width : (number + 1) * width], qkv_ref[number], NT)
        for number in range(3)
    )
    region = all_ref[...].astype(jnp.float32)
    center = region - jnp.mean(region, -1, keepdims=True)
    scale = lax.rsqrt(jnp.mean(center * center, -1, keepdims=True) + EPSILON)
    hat = center * scale
    hat_grad = norm_grad * vec_ref[0:1, :]
    region_grad_ref[...] = scale * (
        hat_grad
        - jnp.mean(hat_grad, -1, keepdims=True)
        - hat * jnp.mean(hat_grad * hat, -1, keepdims=True)
    )
    grad_out[...] = new_grad_ref[...] + region_grad_ref[:rows, :]
    bias_sums = jnp.sum(proj_grad.astype(jnp.float32), 0, keepdims=True)
    sums_out[...] = jnp.zeros_like(sums_out)
    sums_out[0:1, :] = jnp.sum(norm_grad * hat, 0, keepdims=True)
    sums_out[1:2, :] = jnp.sum(norm_grad, 0, keepdims=True)
    sums_out[6:7, :] = bias_sums[:, :width]
    sums_out[7:8, :] = bias_sums[:, 2 * width :]
    weight_ref[...] = dot_as(norm_ref[...], proj_grad, TN)
    weight_rows = weight_out.shape[1]
    weight_start = pl.multiple_of(place_ref[1] * weight_rows, 8)
    for number in range(3):
        weight_out[number] = weight_ref[
            pl.ds(weight_start, weight_rows), number * width : (number + 1) * width
        ]


def region_backward(
    place, all_rows, normed, proj, mix_grad, key_images, query_images, new_grad, qkv_weight, vectors, weight_rows
):
    total, width = all_rows.shape
    vmem = pl.BlockSpec(memory_space=pltpu.VMEM)
    return pl.pallas_call(
        region_backward_kernel,
        in_specs=[pl.BlockSpec(memory_space=pltpu.SMEM)] + [vmem] * 9,
        out_specs=[vmem] * 3,
        out_shape=[
            shape_of(new_grad.shape),
            shape_of((3, weight_rows, width)),
            shape_of(vectors.shape),
        ],
        scratch_shapes=[
            pltpu.VMEM((total, total), jnp.float32),
            pltpu.VMEM((total, 3 * width), jnp.bfloat16),
            pltpu.VMEM((total, width), jnp.float32),
            pltpu.VMEM((width, 3 * width), jnp.float32),
            pltpu.VMEM((GROUP_HEADS, total, total), jnp.float32),
            pltpu.VMEM((GROUP_HEADS, total, total), jnp.float32),
            pltpu.VMEM((GROUP_HEADS, total, total), jnp.bfloat16),
            pltpu.VMEM((GROUP_HEADS, total, total), jnp.bfloat16),
        ],
        compiler_params=pltpu.CompilerParams(vmem_limit_bytes=VMEM_LIMIT),
        name="region_backward",
    )(place, all_rows, normed, proj, mix_grad, key_images, query_images, new_grad, qkv_weight, vectors)


def small_gradient_kernel(pieces, place_ref, *refs):
    norm_refs = refs[:pieces]
    proj_grad_refs = refs[pieces : 2 * pieces]
    mix_refs = refs[2 * pieces : 3 * pieces]
    branch_refs = refs[3 * pieces : 4 * pieces]
    region_mix_ref, region_branch_ref, kept, sent = refs[4 * pieces :]
    core = place_ref[1] % 2
    number = pl.program_id(0)
    blocks, _, rows, width = kept.shape

    def write(total):
        kept[:, 0], sent[:, 0] = split_cores(total.reshape(blocks, 2, rows, width), core)

    @pl.when(number < 3)
    def _():
        write(
            sum(
                dot_as(norm_ref[...], grad_ref[...], TN)
                for norm_ref, grad_ref in zip(norm_refs, proj_grad_refs)
            )
        )

    @pl.when(number == 3)
    def _():
        write(
            sum(
                dot_as(mix_ref[...], branch_ref[...], TN)
                for mix_ref, branch_ref in zip(mix_refs, branch_refs)
            )
            + dot_as(region_mix_ref[...], region_branch_ref[...], TN)
        )


def small_gradients(place, normed, proj_grads, mix, branches, region_mix, region_branch, win_count):
    width = normed.shape[1]
    half = win_count // 2
    weight_rows = width // win_count
    pieces = len(proj_grads)
    operands, in_specs = [place], [pl.BlockSpec(memory_space=pltpu.SMEM)]

    def add_rows(whole):
        start = 0
        for piece in branches:
            here = piece.shape[0]
            if start % here:
                operands.append(whole[start : start + here])
                block = 0
            else:
                operands.append(in_hbm(whole))
                block = start // here
            in_specs.append(pl.BlockSpec(piece.shape, lambda number, block=block: (block, 0)))
            start += here

    add_rows(normed)
    for piece in proj_grads:
        operands.append(in_hbm(piece))
        in_specs.append(
            pl.BlockSpec((piece.shape[0], width), lambda number: (0, jnp.minimum(number, 2)))
        )
    add_rows(mix)
    for piece in branches + [region_mix, region_branch]:
        operands.append(in_hbm(piece))
        in_specs.append(pl.BlockSpec(piece.shape, lambda number: (0, 0)))
    out_spec = pl.BlockSpec((half, 1, weight_rows, width), lambda number: (0, number, 0, 0))
    dims = (half, 4, weight_rows, width)
    rows = normed.shape[0]
    kept, sent = pl.pallas_call(
        functools.partial(small_gradient_kernel, pieces),
        grid=(4,),
        in_specs=in_specs,
        out_specs=[out_spec, out_spec],
        out_shape=[hbm_shape(dims), hbm_shape(dims, jnp.bfloat16)],
        compiler_params=pltpu.CompilerParams(vmem_limit_bytes=VMEM_LIMIT),
        cost_estimate=pl.CostEstimate(
            flops=8 * rows * width * width,
            bytes_accessed=12 * rows * width + 24 * width * width,
            transcendentals=0,
        ),
        name="small_gradients",
    )(*operands)
    flat = (half, 4 * weight_rows, width)
    return kept.reshape(flat), sent.reshape(flat)


def core_hop(kept, sent):
    return kept + swap(sent, "win", 0).astype(jnp.float32)


def local(
    tokens,
    patch_mask,
    keep_mask,
    image_map,
    qkv_weight,
    out_weight,
    up_weight,
    down_weight,
    vectors,
    qkv_mom,
    out_mom,
    up_mom,
    down_mom,
    vec_mom,
    cotangent,
):
    windows = tokens.shape[1]
    seq_len = tokens.shape[2]
    model_width = tokens.shape[3]
    hidden_width = up_weight.shape[1]
    folds = hidden_width // model_width
    shard_rows = out_mom.shape[0]
    ff_rows = down_mom.shape[0]
    vec_rows = vec_mom.shape[0]
    padded = (seq_len + 7) // 8 * 8
    region_rows = (windows + 7) // 8 * 8
    row_count = windows * padded
    win_count = lax.axis_size("win")
    win_index = lax.axis_index("win")
    place = jnp.stack([lax.axis_index("rep"), win_index]).astype(jnp.int32)

    def pad_rows(values, rows, fill=0):
        widths = ((0, rows - values.shape[0]),) + ((0, 0),) * (values.ndim - 1)
        return jnp.pad(values, widths, constant_values=fill)

    region_own = pad_rows(tokens[0, :, 0], region_rows)
    region_all = gather_blocks(region_own).reshape(-1, model_width)
    keeper = keep_mask[0].astype(jnp.float32) / KEEP_SHARE
    images = image_map[0].reshape(win_count, windows)[win_index ^ jnp.array(gather_masks())]
    images = jnp.pad(images, ((0, 0), (0, region_rows - windows)), constant_values=-1)
    key_images = images.reshape(-1, 1)
    own_images = jnp.tile(images[:1], (1, GROUP_HEADS))
    region_keep = pad_rows(keeper[:, 0:1], region_rows)

    region_norm, region_proj, region_mix, region_new = region_forward(
        region_all, region_own, region_keep, key_images, own_images, qkv_weight, out_weight, vectors
    )

    key_valid = jnp.concatenate([jnp.ones((windows, 1), jnp.int32), patch_mask[0]], axis=1) == 1
    key_bias = jnp.where(key_valid, 0.0, -1e30)
    key_bias = jnp.pad(key_bias, ((0, 0), (0, padded - seq_len)), constant_values=-1e30)
    key_bias = key_bias[:, :, None]
    keep_window = keeper[:, 1].reshape(windows, 1, 1)
    seq_norm, seq_proj, local_mix, after_attn = window_forward(
        tokens, region_new, key_bias, keep_window, qkv_weight, out_weight, vectors, padded
    )
    seq_norm = seq_norm.reshape(row_count, model_width)
    local_mix = local_mix.reshape(row_count, model_width)
    after_attn = after_attn.reshape(row_count, model_width)

    out_tokens, attn_res_grad, mlp_sums, up_half, down_half = mlp(
        place,
        after_attn,
        cotangent,
        keeper[:, 2].reshape(windows, 1, 1),
        vectors,
        up_weight,
        down_weight,
        padded,
        win_count,
    )

    steps = windows // window_step(windows)
    cuts = [0, steps * 2 // 5, steps * 4 // 5, steps]
    after_grad = attn_res_grad.reshape(windows, padded, model_width)
    big = Chain(
        (up_half, down_half),
        [lambda halves: (core_hop(*halves[0]), core_hop(*halves[1]))] + scatter_stages(),
    )
    before = (None, mlp_sums, None)
    proj_grads, branch_grads = [], []
    for piece in range(3):
        region_new_grad, sums, seq_grad, proj_grad, branch_grad, *region_parts = window_backward(
            tokens,
            region_new,
            key_bias,
            keep_window,
            qkv_weight,
            out_weight,
            vectors,
            seq_proj,
            after_grad,
            region_keep,
            before,
            (cuts[piece], cuts[piece + 1]),
            padded,
        )
        before = (seq_grad, sums, region_new_grad)
        proj_grads.append(proj_grad.reshape(-1, 3 * model_width))
        branch_grads.append(branch_grad.reshape(-1, model_width))
        big.step()
        if piece < 2:
            big.value, after_grad = tie(big.value, after_grad)
    region_branch_grad, region_mix_grad = region_parts

    small_kept, small_sent = small_gradients(
        place,
        seq_norm,
        proj_grads,
        local_mix,
        branch_grads,
        region_mix,
        region_branch_grad,
        win_count,
    )
    core = win_index % 2
    vector_pairs = sums.reshape(win_count // 2, 2, 1, vec_rows)
    vector_pairs = jnp.pad(
        vector_pairs, ((0, 0), (0, 0), (0, 7), (0, model_width - vec_rows))
    )
    small_kept = jnp.concatenate(
        [small_kept, lax.dynamic_index_in_dim(vector_pairs, core, 1, keepdims=False)], axis=1
    )
    small_sent = jnp.concatenate(
        [
            small_sent,
            bfloat(lax.dynamic_index_in_dim(vector_pairs, 1 - core, 1, keepdims=False)),
        ],
        axis=1,
    )

    def split_pair(halves):
        total = core_hop(*halves)
        return total[:, : 2 * shard_rows], total[:, 2 * shard_rows :]

    small = Chain((small_kept, small_sent), [split_pair] + scatter_stages())
    mixes = Chain(region_mix_grad, gather_stages())
    for _ in range(3):
        step_together(big, small, mixes)

    region_grad, region_weight_grad, region_sums = region_backward(
        place,
        region_all,
        region_norm,
        region_proj,
        mixes.value.reshape(-1, model_width),
        key_images,
        key_images.reshape(1, -1),
        region_new_grad,
        qkv_weight,
        vectors,
        shard_rows,
    )
    input_grad = insert_regions(seq_grad, region_grad).reshape(tokens.shape)
    region_vectors = jnp.pad(
        lax.dynamic_slice_in_dim(region_sums.reshape(-1), win_index * vec_rows, vec_rows)[None],
        ((0, 7), (0, model_width - vec_rows)),
    )
    region_part = Chain(
        jnp.concatenate([region_weight_grad.reshape(-1, model_width), region_vectors], axis=0),
        [sum_over_rep],
    )

    first = lax.axis_index("rep") == 0
    low_core = core == 0
    two_owners = lax.axis_size("rep") == 2
    while big.stages:
        big.step()
    folded_up_mom = MOMENTUM_DECAY * fold_columns(up_mom, model_width) + big.value[:ff_rows]
    new_down_mom = MOMENTUM_DECAY * down_mom + big.value[ff_rows:]
    if two_owners:
        big = Chain(bfloat(jnp.where(first, folded_up_mom, new_down_mom)), gather_stages())
        big.step()
        small.step()
        big.value, small.value, region_part.value = tie(
            big.value, small.value, region_part.value
        )
        step_together(big, small, region_part)
        step_together(big, small)
    while small.stages or region_part.stages:
        small.step()
        region_part.step()
    small_total, region_total = small.value, region_part.value
    matrix_rows = 4 * shard_rows
    region_matrix = region_total[: 3 * shard_rows].reshape(3, shard_rows, model_width)
    small_matrix = small_total[:matrix_rows].reshape(4, shard_rows, model_width)
    new_qkv_mom = MOMENTUM_DECAY * qkv_mom + (small_matrix[:3] + region_matrix)
    new_out_mom = MOMENTUM_DECAY * out_mom + small_matrix[3]
    vec_total = small_total[matrix_rows, :vec_rows] + region_total[3 * shard_rows, :vec_rows]
    new_vec_mom = MOMENTUM_DECAY * vec_mom + vec_total
    new_vectors = (
        lax.dynamic_slice_in_dim(vectors.reshape(-1), win_index * vec_rows, vec_rows)
        - VECTOR_RATE * new_vec_mom
    )
    new_up_mom = unfold_columns(folded_up_mom, folds)
    small_rows = jnp.concatenate([new_qkv_mom, new_out_mom[None]])
    if two_owners:
        pair = bfloat(jnp.where(first, small_rows[:2], small_rows[2:]))
        kept, sent = pick_owner(low_core, pair[0], pair[1])
        shards = jnp.concatenate(pick_owner(low_core, kept, swap(sent, "win", 0)))
        shards, big.value = tie(shards, big.value)
        small = Chain(shards, gather_stages(1))
        small.step()
        big_mine = big_update(place, big.value, folds, gather_masks())
        big_mine, small.value = tie(big_mine, small.value)
        small.step()
        up_update, down_update = pick_owner(first, big_mine, swap(big_mine, "rep", 0))
        small_mine = small_update(place, small.value[:, None], gather_masks(1))[0]
        small_mine = small_mine.reshape(2, shard_rows, model_width)
        kept, sent = pick_owner(low_core, small_mine[0], small_mine[1])
        pair = jnp.stack(pick_owner(low_core, kept, swap(sent, "win", 0)))
        updates = jnp.concatenate(pick_owner(first, pair, swap(pair, "rep", 0)))
    else:
        up_update, down_update, updates = every_update(
            place, (folded_up_mom, new_down_mom), small_rows, folds
        )

    def stepped(weight, rows_here, update):
        rows = own_rows(weight, rows_here).astype(jnp.float32)
        return rows - MATRIX_RATE * update.astype(jnp.float32)

    new_qkv = jnp.stack(
        [stepped(qkv_weight[number], shard_rows, updates[number]) for number in range(3)]
    )
    new_out = stepped(out_weight, shard_rows, updates[3])
    new_up = stepped(up_weight, shard_rows, unfold_columns(up_update, folds))
    new_down = stepped(down_weight, ff_rows, down_update)
    return (
        out_tokens,
        input_grad,
        new_qkv_mom,
        new_qkv,
        new_out_mom,
        new_out,
        new_up_mom,
        new_up,
        new_down_mom,
        new_down,
        new_vec_mom,
        new_vectors,
    )


def solution(mesh):
    placed = (
        P("rep", "win", None, None),
        P("rep", "win", None),
        P("rep", "win", None),
        P("rep", None),
        P(),
        P(),
        P(),
        P(),
        P(),
        P(None, "win", None),
        P("win", None),
        P("win", None),
        P("win", None),
        P("win"),
        P("rep", "win", None, None),
    )
    return jax.shard_map(
        local,
        mesh=mesh,
        in_specs=placed,
        out_specs=(
            P("rep", "win", None, None),
            P("rep", "win", None, None),
            P(None, "win", None),
            P(None, "win", None),
            P("win", None),
            P("win", None),
            P("win", None),
            P("win", None),
            P("win", None),
            P("win", None),
            P("win"),
            P("win"),
        ),
        check_vma=False,
    )
```

time: 326 us -> 250 us (0.77)
  waiting for transfers between devices: 77 us -> 37.7 us
  matrix products: 24 us -> 0 us
  Pallas kernels: 124 us -> 115 us
  local copies, waits for them, and re-layouts: 21.7 us -> 15.5 us
    ppermute x36 -> x29, waiting for transfers between devices: 77 us -> 32.8 us  [swap(): return lax.ppermute(values, axis, [(i, i ^ 1 << bit) for i in range(size)])]
    dot_general x4 -> x0, matrix products: 24 us -> none  [product(): return jnp.dot(left_side, right_side, preferred_element_type=jnp.float32)]
    ppermute x0 -> x12, starting transfers between devices: none -> 18.9 us  [gather_far(): lax.ppermute(values, 'win', [(i, i ^ mask) for i in range(size)])]
    pallas_call x4 -> x7, Pallas kernels: 48.7 us -> 64.9 us  [the longest x1 29.6 us: mlp(): pl.pallas_call(functools.partial(mlp_kernel, count, seq_len, padded), gri...]
    ppermute x36 -> x29, starting transfers between devices: 44.7 us -> 28.6 us  [swap(): return lax.ppermute(values, axis, [(i, i ^ 1 << bit) for i in range(size)])]
    pallas_call x1, Pallas kernels: 26.5 us -> 11.1 us  [window_forward(): pl.pallas_call(functools.partial(window_forward_kernel, count, seq_len, p...]
    pallas_call x2, Pallas kernels: 35.4 us -> 25.9 us  [newton_call(): pl.pallas_call(kernel, in_specs=[pl.BlockSpec(memory_space=pltpu.SMEM), p...]
    unnamed x81 -> x64, local copies, waits for them, and re-layouts: 11.7 us -> 4.84 us
  transfers between devices with their start and end apart: 36 -> 41, of which waited for: 20 -> 18; matrix products, arithmetic and copies ran while one was open for 11% -> 11% of each run, Pallas kernels for 12% -> 29%
where the time goes in v2:
time: 250 us; the launch traced here: 246 us
  Pallas kernels  115 us (46%)
  starting transfers between devices  47.5 us (19%)
  waiting for transfers between devices  37.7 us (15%)
  other arithmetic  28.2 us (11%)
  local copies, waits for them, and re-layouts  15.5 us (6%)
    ppermute x29, waiting for transfers between devices, swap(): return lax.ppermute(values, axis, [(i, i ^ 1 << bit) for i in range(size)])  32.8 us
    pallas_call x1, Pallas kernels, mlp(): pl.pallas_call(functools.partial(mlp_kernel, count, seq_len, padded), gri...  29.6 us
    ppermute x29, starting transfers between devices, swap(): return lax.ppermute(values, axis, [(i, i ^ 1 << bit) for i in range(size)])  28.6 us
    pallas_call x2, Pallas kernels, newton_call(): pl.pallas_call(kernel, in_specs=[pl.BlockSpec(memory_space=pltpu.SMEM), p...  25.9 us
    pallas_call x3, Pallas kernels, window_backward(): pl.pallas_call(functools.partial(window_backward_kernel, count, first_ste...  22.5 us
    ppermute x12, starting transfers between devices, gather_far(): lax.ppermute(values, 'win', [(i, i ^ mask) for i in range(size)])  18.9 us
    pallas_call x1, Pallas kernels, region_backward(): pl.pallas_call(region_backward_kernel, in_specs=[pl.BlockSpec(memory_spac...  13.6 us
    pallas_call x1, Pallas kernels, window_forward(): pl.pallas_call(functools.partial(window_forward_kernel, count, seq_len, p...  11.1 us
  transfers between devices with their start and end apart: 41, of which 18 were waited for; matrix products, arithmetic and copies ran while one was open for 11% of the time, Pallas kernels for 29%

profile of v2, /device:TPU:0, one launch (start us, length us, event | category | flops | bytes accessed | tf_op | source)
XLA Modules:
  0.0 246.2 jit_solution(16978800358017682216)
XLA Ops:
  1.8 3.1 %collective-permute-start = (bf16[1,24,512]{2,1,0:T(8,128)(2,1)S(1)}, bf16[1,24,512]{2,1,0:T(8,128)(2,1)S(1)}, u32[]{:S(2)}, u32[]{:S(2)}) collective-permute-start(bf16[1,24,512]{2,1,0:T(8,128)(2,1)S(1)} %get-tuple-element.195), channel_id=1, source_target_pairs={{0,8},{2,10},{4,12},{6,14},{8,0},{10,2},{12,4},{14,6},{16,24},{18,... | collective-permute-start | bytes 73736 | tf_op jit(solution)/shard_map/ppermute | solution.py:66
  4.9 2.6 %collective-permute-start.1 = (bf16[1,24,512]{2,1,0:T(8,128)(2,1)S(1)}, bf16[1,24,512]{2,1,0:T(8,128)(2,1)S(1)}, u32[]{:S(2)}, u32[]{:S(2)}) collective-permute-start(bf16[1,24,512]{2,1,0:T(8,128)(2,1)S(1)} %get-tuple-element.195), channel_id=1, source_target_pairs={{0,16},{2,18},{4,20},{6,22},{8,24},{10,26},{12,28},{14,30},{16,0},... | collective-permute-start | bytes 73736 | tf_op jit(solution)/shard_map/ppermute | solution.py:66
  21.2 3.3 %region_forward.1 = (bf16[384,512]{1,0:T(8,128)(2,1)}, bf16[384,1536]{1,0:T(8,128)(2,1)}, bf16[24,512]{1,0:T(8,128)(2,1)}, f32[24,512]{1,0:T(8,128)S(1)}) custom-call(bf16[384,512]{1,0:T(8,128)(2,1)S(1)} %bitcast.166, bf16[24,512]{1,0:T(8,128)(2,1)S(1)} %get-tuple-element.194.own_ref, f32[24,1]{1,0:T(8,128)S(1)} %pad.26.keep_ref.region_keep_ref, ...), custom_call_target="tpu_custom_call" | custom-call | tf_op jit(solution)/shard_map/region_forward/pallas_call | solution.py:1012
  24.5 11.1 %window_forward.1 = (bf16[20,56,512]{2,1,0:T(8,128)(2,1)}, bf16[20,56,1536]{2,1,0:T(8,128)(2,1)}, bf16[20,56,512]{2,1,0:T(8,128)(2,1)}, f32[20,56,512]{2,1,0:T(8,128)}) custom-call(bf16[1,20,50,512]{3,2,1,0:T(8,128)(2,1)} %tokens_ref.7, f32[24,512]{1,0:T(8,128)S(1)} %get-tuple-element.79.region_ref, f32[20,56,1]{2,1,0:T(8,128)S(1)} %copy.46.bias_ref, ...), custom_call_target="tpu_custom_call" | custom-call | tf_op jit(solution)/shard_map/window_forward/pallas_call | solution.py:642
  35.6 29.6 %mlp.1 = (bf16[1,20,50,512]{3,2,1,0:T(8,128)(2,1)}, f32[1120,512]{1,0:T(8,128)}, f32[14,512]{1,0:T(8,128)}, f32[8,4,32,512]{3,2,1,0:T(8,128)}, bf16[8,4,32,512]{...) custom-call(s32[2]{0:T(128)S(1)} %pad_add_fusion.place_ref, f32[1120,512]{1,0:T(8,128)} %bitcast.224, ...), custom_call_target="tpu_custom_call" | custom-call | flops 14092861440 | bytes 9175040 | tf_op jit(solution)/shard_map/mlp/pallas_call | solution.py:917
  65.8 8.5 %window_backward.3 = (f32[24,512]{1,0:T(8,128)}, f32[14,512]{1,0:T(8,128)}, f32[20,200,128]{2,1,0:T(8,128)}, bf16[8,56,1536]{2,1,0:T(8,128)(2,1)}, bf16[8,56,512]{2,1,0:T(8,128)(2,1)}) custom-call(bf16[1,20,50,512]{3,2,1,0:T(8,128)(2,1)} %tokens_ref.7, f32[24,512]{1,0:T(8,128)S(1)} %get-tuple-element.79.region_ref, f32[20,56,1]{2,1,0:T(8,128)S(1)} %copy.46.bias_ref, ...), custom_call_target="tpu_custom_call" | custom-call | flops 8000000000 | bytes 4587520 | tf_op jit(solution)/shard_map/window_backward/pallas_call | solution.py:746
  80.0 8.6 %window_backward.4 = (f32[24,512]{1,0:T(8,128)}, f32[14,512]{1,0:T(8,128)}, f32[20,200,128]{2,1,0:T(8,128)}, bf16[8,56,1536]{2,1,0:T(8,128)(2,1)}, bf16[8,56,512]{2,1,0:T(8,128)(2,1)}) custom-call(bf16[1,20,50,512]{3,2,1,0:T(8,128)(2,1)} %tokens_ref.7, f32[24,512]{1,0:T(8,128)S(1)} %get-tuple-element.79.region_ref, ...), custom_call_target="tpu_custom_call", output_to_operand_aliasing={{2}: (12, {})} | custom-call | flops 8000000000 | bytes 4587520 | tf_op jit(solution)/shard_map/window_backward/pallas_call | solution.py:746
  95.9 5.4 %window_backward.5 = (f32[24,512]{1,0:T(8,128)}, f32[14,512]{1,0:T(8,128)}, f32[20,200,128]{2,1,0:T(8,128)}, bf16[4,56,1536]{2,1,0:T(8,128)(2,1)}, bf16[4,56,512...) custom-call(bf16[1,20,50,512]{3,2,1,0:T(8,128)(2,1)} %tokens_ref.7, ...), custom_call_target="tpu_custom_call", output_to_operand_aliasing={{2}: (12, {})} | custom-call | flops 4000000000 | bytes 2293760 | tf_op jit(solution)/shard_map/window_backward/pallas_call | solution.py:746
  101.9 7.8 %small_gradients.1 = (f32[8,4,32,512]{3,2,1,0:T(8,128)}, bf16[8,4,32,512]{3,2,1,0:T(8,128)(2,1)}) custom-call(s32[2]{0:T(128)S(1)} %pad_add_fusion.place_ref, bf16[1120,512]{1,0:T(8,128)(2,1)} %bitcast.174, bf16[1120,512]{1,0:T(8,128)(2,1)} %bitcast.175, bf16[1120,512]{1,0:T(8,128)(2,1)} %bitcast.176, bf16[448,1536]{1,0:T(8,128)(2,1)} %bitcast.198, ...), custom_call_target="tpu_custom_call" | custom-call | flops 2348810240 | bytes 13172736 | tf_op jit(solution)/shard_map/small_gradients/pallas_call | solution.py:1212
  109.9 2.4 pad_maximum_fusion.1
  118.5 2.7 %collective-permute-start.15 = (bf16[1,24,512]{2,1,0:T(8,128)(2,1)S(1)}, bf16[1,24,512]{2,1,0:T(8,128)(2,1)S(1)}, u32[]{:S(2)}, u32[]{:S(2)}) collective-permute-start(bf16[1,24,512]{2,1,0:T(8,128)(2,1)S(1)} %bitcast.170), channel_id=1, source_target_pairs={{0,24},{2,26},{4,28},{6,30},{8,16},{10,18},{12,20},{14,22},{16,8},... | collective-permute-start | bytes 73736 | tf_op jit(solution)/shard_map/ppermute | solution.py:66
  122.9 3.7 %collective-permute-done.15 = bf16[1,24,512]{2,1,0:T(8,128)(2,1)S(1)} collective-permute-done((bf16[1,24,512]{2,1,0:T(8,128)(2,1)S(1)}, bf16[1,24,512]{2,1,0:T(8,128)(2,1)S(1)}, u32[]{:S(2)}, u32[]{:S(2)}) %collective-permute-start.15) | collective-permute-done | bytes 24608 | tf_op jit(solution)/shard_map/ppermute | solution.py:66
  134.8 3.6 %collective-permute-done.19 = bf16[4,24,512]{2,1,0:T(8,128)(2,1)S(1)} collective-permute-done((bf16[4,24,512]{2,1,0:T(8,128)(2,1)S(1)}, bf16[4,24,512]{2,1,0:T(8,128)(2,1)S(1)}, u32[]{:S(2)}, u32[]{:S(2)}) %collective-permute-start.19) | collective-permute-done | bytes 98336 | tf_op jit(solution)/shard_map/ppermute | solution.py:42
  138.7 3.9 %collective-permute-done.18 = bf16[2,2,72,512]{3,2,1,0:T(8,128)(2,1)S(1)} collective-permute-done((bf16[2,2,72,512]{3,2,1,0:T(8,128)(2,1)S(1)}, bf16[2,2,72,512]{3,2,1,0:T(8,128)(2,1)S(1)}, u32[]{:S(2)}, u32[]{:S(2)}) %collective-permute-start.18) | collective-permute-done | bytes 294944 | tf_op jit(solution)/shard_map/ppermute | solution.py:42
  150.4 2.2 collective-permute-start.26
  156.9 13.6 %region_backward.1 = (f32[24,512]{1,0:T(8,128)S(1)}, f32[3,32,512]{2,1,0:T(8,128)S(1)}, f32[14,512]{1,0:T(8,128)S(1)}) custom-call(s32[2]{0:T(128)S(1)} %pad_add_fusion.place_ref, bf16[384,512]{1,0:T(8,128)(2,1)S(1)} %bitcast.167, bf16[384,512]{1,0:T(8,128)(2,1)S(1)} %copy-done.5, bf16[384,1536]{1,0:T(8,128)(2,1)S(1)} %copy-done.3, ...), custom_call_target="tpu_custom_call" | custom-call | tf_op jit(solution)/shard_map/region_backward/pallas_call | solution.py:1122
  180.3 4.2 %collective-permute-done.28 = bf16[4,128,512]{2,1,0:T(8,128)(2,1)S(1)} collective-permute-done((bf16[4,128,512]{2,1,0:T(8,128)(2,1)S(1)}, bf16[4,128,512]{2,1,0:T(8,128)(2,1)S(1)}, u32[]{:S(2)}, u32[]{:S(2)}) %collective-permute-start.28) | collective-permute-done | bytes 524320 | tf_op jit(solution)/shard_map/ppermute | solution.py:42
  187.7 2.8 %collective-permute-done.32 = bf16[1,136,256]{2,1,0:T(8,128)(2,1)S(1)} collective-permute-done((bf16[1,136,256]{2,1,0:T(8,128)(2,1)S(1)}, bf16[1,136,256]{2,1,0:T(8,128)(2,1)S(1)}, u32[]{:S(2)}, u32[]{:S(2)}) %collective-permute-start.32) | collective-permute-done | bytes 69664 | tf_op jit(solution)/shard_map/ppermute | solution.py:42
  190.6 3.1 %pad_maximum_fusion.blocks_ref = bf16[16,128,512]{2,1,0:T(8,128)(2,1)} fusion(bf16[8,128,512]{2,1,0:T(8,128)(2,1)} %collective-permute-done.31, bf16[8,128,512]{2,1,0:T(8,128)(2,1)} %pad_maximum_fusion.2), kind=kLoop, calls=%fused_computation.2 | loop fusion | flops 1048576 | bytes 4194304 | tf_op jit(solution)/shard_map/concatenate | solution.py:75
  199.4 2.6 %collective-permute-start.34 = (bf16[1,64,512]{2,1,0:T(8,128)(2,1)S(1)}, bf16[1,64,512]{2,1,0:T(8,128)(2,1)S(1)}, u32[]{:S(2)}, u32[]{:S(2)}) collective-permute-start(bf16[1,64,512]{2,1,0:T(8,128)(2,1)S(1)} %bitcast.215), channel_id=1, source_target_pairs={{0,8},{2,10},{4,12},{6,14},{8,0},{10,2},{12,4},{14,6},{16,24},{18,... | collective-permute-start | bytes 196616 | tf_op jit(solution)/shard_map/ppermute | solution.py:66
  202.1 15.5 %big_newton.1 = bf16[128,512]{1,0:T(8,128)(2,1)S(1)} custom-call(s32[2]{0:T(128)S(1)} %pad_add_fusion.place_ref, bf16[16,128,512]{2,1,0:T(8,128)(2,1)S(1)} %copy-done.2), custom_call_target="tpu_custom_call" | custom-call | flops 12079595520 | bytes 2097152 | tf_op jit(solution)/shard_map/big_newton/pallas_call | solution.py:295
  221.4 4.1 %collective-permute-done.37 = bf16[4,64,512]{2,1,0:T(8,128)(2,1)S(1)} collective-permute-done((bf16[4,64,512]{2,1,0:T(8,128)(2,1)S(1)}, bf16[4,64,512]{2,1,0:T(8,128)(2,1)S(1)}, u32[]{:S(2)}, u32[]{:S(2)}) %collective-permute-start.37) | collective-permute-done | bytes 262176 | tf_op jit(solution)/shard_map/ppermute | solution.py:42
  225.6 10.4 %small_newton.1 = bf16[1,64,512]{2,1,0:T(8,128)(2,1)S(1)} custom-call(s32[2]{0:T(128)S(1)} %pad_add_fusion.place_ref, bf16[8,1,64,512]{3,2,1,0:T(8,128)(2,1)S(1)} %maximum_bitcast_fusion.blocks_ref), custom_call_target="tpu_custom_call" | custom-call | flops 7247757312 | bytes 524288 | tf_op jit(solution)/shard_map/small_newton/pallas_call | solution.py:295
  237.9 2.4 collective-permute-start.39
  (235 shorter events, 87.1 us)
Async XLA Ops:
  1.8 10.1 %collective-permute-start = (bf16[1,24,512]{2,1,0:T(8,128)(2,1)S(1)}, bf16[1,24,512]{2,1,0:T(8,128)(2,1)S(1)}, u32[]{:S(2)}, u32[]{:S(2)}) collective-permute-start(bf16[1,24,512]{2,1,0:T(8,128)(2,1)S(1)} %get-tuple-element.195), channel_id=1, source_target_pairs={{0,8},{2,10},{4,12},{6,14},{8,0},{10,2},{12,4},{14,6},{16,24},{18,... | collective-permute-start | bytes 73736 | tf_op jit(solution)/shard_map/ppermute | solution.py:66
  4.9 7.1 %collective-permute-start.1 = (bf16[1,24,512]{2,1,0:T(8,128)(2,1)S(1)}, bf16[1,24,512]{2,1,0:T(8,128)(2,1)S(1)}, u32[]{:S(2)}, u32[]{:S(2)}) collective-permute-start(bf16[1,24,512]{2,1,0:T(8,128)(2,1)S(1)} %get-tuple-element.195), channel_id=1, source_target_pairs={{0,16},{2,18},{4,20},{6,22},{8,24},{10,26},{12,28},{14,30},{16,0},... | collective-permute-start | bytes 73736 | tf_op jit(solution)/shard_map/ppermute | solution.py:66
  65.3 9.1 %collective-permute-start.5 = (bf16[8,128,512]{2,1,0:T(8,128)(2,1)}, bf16[8,128,512]{2,1,0:T(8,128)(2,1)}, u32[]{:S(2)}, u32[]{:S(2)}) collective-permute-start(bf16[8,128,512]{2,1,0:T(8,128)(2,1)} %bitcast.225), channel_id=1, source_target_pairs={{0,2},{2,0},{4,6},{6,4},{8,10},{10,8},{12,14},{14,12},{16,18},{18,... | collective-permute-start | bytes 3145736 | tf_op jit(solution)/shard_map/ppermute | solution.py:42
  65.5 10.7 %collective-permute-start.6 = (bf16[8,128,512]{2,1,0:T(8,128)(2,1)}, bf16[8,128,512]{2,1,0:T(8,128)(2,1)S(1)}, u32[]{:S(2)}, u32[]{:S(2)}) collective-permute-start(bf16[8,128,512]{2,1,0:T(8,128)(2,1)} %get-tuple-element.86), channel_id=1, source_target_pairs={{0,2},{2,0},{4,6},{6,4},{8,10},{10,8},{12,14},{14,12},{16,18},{18,... | collective-permute-start | bytes 3145736 | tf_op jit(solution)/shard_map/ppermute | solution.py:42
  76.8 14.0 %collective-permute-start.7 = (bf16[8,128,256]{2,1,0:T(8,128)(2,1)S(1)}, bf16[8,128,256]{2,1,0:T(8,128)(2,1)S(1)}, u32[]{:S(2)}, u32[]{:S(2)}) collective-permute-start(bf16[8,128,256]{2,1,0:T(8,128)(2,1)S(1)} %dynamic-slice_convert_fusion.1), channel_id=1, source_target_pairs={{0,1},{1,0},{2,3},{3,2},{4,5},{5,4},{6,7},{7,6},{8,9},{9,8},{10,11... | collective-permute-start | bytes 1572872 | tf_op jit(solution)/shard_map/ppermute | solution.py:42
  78.4 13.7 %collective-permute-start.8 = (bf16[2,2,128,512]{3,2,1,0:T(8,128)(2,1)S(1)}, bf16[2,2,128,512]{3,2,1,0:T(8,128)(2,1)S(1)}, u32[]{:S(2)}, u32[]{:S(2)}) collective-permute-start(bf16[2,2,128,512]{3,2,1,0:T(8,128)(2,1)S(1)} %fusion), channel_id=1, source_target_pairs={{0,4},{2,6},{4,0},{6,2},{8,12},{10,14},{12,8},{14,10},{16,20},{18,... | collective-permute-start | bytes 1572872 | tf_op jit(solution)/shard_map/ppermute | solution.py:42
  93.1 19.2 %collective-permute-start.9 = (bf16[2,2,128,256]{3,2,0,1:T(8,128)(2,1)}, bf16[2,2,128,256]{3,2,0,1:T(8,128)(2,1)}, u32[]{:S(2)}, u32[]{:S(2)}) collective-permute-start(bf16[2,2,128,256]{3,2,0,1:T(8,128)(2,1)} %fusion.7), channel_id=1, source_target_pairs={{0,4},{2,6},{4,0},{6,2},{8,12},{10,14},{12,8},{14,10},{16,20},{18,... | collective-permute-start | bytes 786440 | tf_op jit(solution)/shard_map/ppermute | solution.py:42
  95.4 18.0 %collective-permute-start.10 = (bf16[4,128,256]{2,1,0:T(8,128)(2,1)}, bf16[4,128,256]{2,1,0:T(8,128)(2,1)}, u32[]{:S(2)}, u32[]{:S(2)}) collective-permute-start(bf16[4,128,256]{2,1,0:T(8,128)(2,1)} %dynamic-slice_convert_fusion.3), channel_id=1, source_target_pairs={{0,1},{1,0},{2,3},{3,2},{4,5},{5,4},{6,7},{7,6},{8,9},{9,8},{10,11... | collective-permute-start | bytes 786440 | tf_op jit(solution)/shard_map/ppermute | solution.py:42
  112.4 15.4 %collective-permute-start.12 = (bf16[8,136,512]{2,1,0:T(8,128)(2,1)}, bf16[8,136,512]{2,1,0:T(8,128)(2,1)}, u32[]{:S(2)}, u32[]{:S(2)}) collective-permute-start(bf16[8,136,512]{2,1,0:T(8,128)(2,1)} %pad_maximum_fusion.1), channel_id=1, source_target_pairs={{0,2},{2,0},{4,6},{6,4},{8,10},{10,8},{12,14},{14,12},{16,18},{18,... | collective-permute-start | bytes 3342344 | tf_op jit(solution)/shard_map/ppermute | solution.py:42
  116.0 10.7 %collective-permute-start.11 = (bf16[2,256,256]{2,1,0:T(8,128)(2,1)}, bf16[2,256,256]{2,1,0:T(8,128)(2,1)}, u32[]{:S(2)}, u32[]{:S(2)}) collective-permute-start(bf16[2,256,256]{2,1,0:T(8,128)(2,1)} %fusion.8), channel_id=1, source_target_pairs={{0,8},{2,10},{4,12},{6,14},{8,0},{10,2},{12,4},{14,6},{16,24},{18,... | collective-permute-start | bytes 786440 | tf_op jit(solution)/shard_map/ppermute | solution.py:42
  118.5 8.1 %collective-permute-start.15 = (bf16[1,24,512]{2,1,0:T(8,128)(2,1)S(1)}, bf16[1,24,512]{2,1,0:T(8,128)(2,1)S(1)}, u32[]{:S(2)}, u32[]{:S(2)}) collective-permute-start(bf16[1,24,512]{2,1,0:T(8,128)(2,1)S(1)} %bitcast.170), channel_id=1, source_target_pairs={{0,24},{2,26},{4,28},{6,30},{8,16},{10,18},{12,20},{14,22},{16,8},... | collective-permute-start | bytes 73736 | tf_op jit(solution)/shard_map/ppermute | solution.py:66
  129.7 8.8 %collective-permute-start.16 = (bf16[256,256]{1,0:T(8,128)(2,1)S(1)}, bf16[256,256]{1,0:T(8,128)(2,1)S(1)}, u32[]{:S(2)}, u32[]{:S(2)}) collective-permute-start(bf16[256,256]{1,0:T(8,128)(2,1)S(1)} %fusion.12), channel_id=1, source_target_pairs={{0,16},{2,18},{4,20},{6,22},{8,24},{10,26},{12,28},{14,30},{16,0},... | collective-permute-start | bytes 393224 | tf_op jit(solution)/shard_map/ppermute | solution.py:42
  131.1 7.6 %collective-permute-start.17 = (bf16[8,64,256]{2,1,0:T(8,128)(2,1)S(1)}, bf16[8,64,256]{2,1,0:T(8,128)(2,1)S(1)}, u32[]{:S(2)}, u32[]{:S(2)}) collective-permute-start(bf16[8,64,256]{2,1,0:T(8,128)(2,1)S(1)} %dynamic-slice_convert_fusion.2), channel_id=1, source_target_pairs={{0,1},{1,0},{2,3},{3,2},{4,5},{5,4},{6,7},{7,6},{8,9},{9,8},{10,11... | collective-permute-start | bytes 786440 | tf_op jit(solution)/shard_map/ppermute | solution.py:42
  133.2 9.5 %collective-permute-start.18 = (bf16[2,2,72,512]{3,2,1,0:T(8,128)(2,1)S(1)}, bf16[2,2,72,512]{3,2,1,0:T(8,128)(2,1)S(1)}, u32[]{:S(2)}, u32[]{:S(2)}) collective-permute-start(bf16[2,2,72,512]{3,2,1,0:T(8,128)(2,1)S(1)} %fusion.6), channel_id=1, source_target_pairs={{0,4},{2,6},{4,0},{6,2},{8,12},{10,14},{12,8},{14,10},{16,20},{18,... | collective-permute-start | bytes 884744 | tf_op jit(solution)/shard_map/ppermute | solution.py:42
  150.4 20.1 %collective-permute-start.26 = (bf16[1,128,512]{2,1,0:T(8,128)(2,1)S(1)}, bf16[1,128,512]{2,1,0:T(8,128)(2,1)}, u32[]{:S(2)}, u32[]{:S(2)}) collective-permute-start(bf16[1,128,512]{2,1,0:T(8,128)(2,1)S(1)} %get-tuple-element.172), channel_id=1, source_target_pairs={{0,24},{2,26},{4,28},{6,30},{8,16},{10,18},{12,20},{14,22},{16,8},... | collective-permute-start | bytes 393224 | tf_op jit(solution)/shard_map/ppermute | solution.py:66
  152.7 17.9 %collective-permute-start.25 = (bf16[1,128,512]{2,1,0:T(8,128)(2,1)S(1)}, bf16[1,128,512]{2,1,0:T(8,128)(2,1)}, u32[]{:S(2)}, u32[]{:S(2)}) collective-permute-start(bf16[1,128,512]{2,1,0:T(8,128)(2,1)S(1)} %get-tuple-element.172), channel_id=1, source_target_pairs={{0,16},{2,18},{4,20},{6,22},{8,24},{10,26},{12,28},{14,30},{16,0},... | collective-permute-start | bytes 393224 | tf_op jit(solution)/shard_map/ppermute | solution.py:66
  154.1 16.5 %collective-permute-start.24 = (bf16[1,128,512]{2,1,0:T(8,128)(2,1)S(1)}, bf16[1,128,512]{2,1,0:T(8,128)(2,1)}, u32[]{:S(2)}, u32[]{:S(2)}) collective-permute-start(bf16[1,128,512]{2,1,0:T(8,128)(2,1)S(1)} %get-tuple-element.172), channel_id=1, source_target_pairs={{0,8},{2,10},{4,12},{6,14},{8,0},{10,2},{12,4},{14,6},{16,24},{18,... | collective-permute-start | bytes 393224 | tf_op jit(solution)/shard_map/ppermute | solution.py:66
  155.6 16.1 %collective-permute-start.27 = (bf16[2,136,256]{2,1,0:T(8,128)(2,1)}, bf16[2,136,256]{2,1,0:T(8,128)(2,1)S(1)}, u32[]{:S(2)}, u32[]{:S(2)}) collective-permute-start(bf16[2,136,256]{2,1,0:T(8,128)(2,1)} %fusion.10), channel_id=1, source_target_pairs={{0,8},{2,10},{4,12},{6,14},{8,0},{10,2},{12,4},{14,6},{16,24},{18,... | collective-permute-start | bytes 417800 | tf_op jit(solution)/shard_map/ppermute | solution.py:42
  174.4 10.2 %collective-permute-start.28 = (bf16[4,128,512]{2,1,0:T(8,128)(2,1)S(1)}, bf16[4,128,512]{2,1,0:T(8,128)(2,1)S(1)}, u32[]{:S(2)}, u32[]{:S(2)}) collective-permute-start(bf16[4,128,512]{2,1,0:T(8,128)(2,1)S(1)} %pad_maximum_fusion.4), channel_id=1, source_target_pairs={{0,4},{2,6},{4,0},{6,2},{8,12},{10,14},{12,8},{14,10},{16,20},{18,... | collective-permute-start | bytes 1572872 | tf_op jit(solution)/shard_map/ppermute | solution.py:42
  197.6 20.0 %collective-permute-start.36 = (bf16[1,64,512]{2,1,0:T(8,128)(2,1)S(1)}, bf16[1,64,512]{2,1,0:T(8,128)(2,1)S(1)}, u32[]{:S(2)}, u32[]{:S(2)}) collective-permute-start(bf16[1,64,512]{2,1,0:T(8,128)(2,1)S(1)} %bitcast.213), channel_id=1, source_target_pairs={{0,24},{2,26},{4,28},{6,30},{8,16},{10,18},{12,20},{14,22},{16,8},... | collective-permute-start | bytes 196616 | tf_op jit(solution)/shard_map/ppermute | solution.py:66
  199.1 18.5 %collective-permute-start.35 = (bf16[1,64,512]{2,1,0:T(8,128)(2,1)S(1)}, bf16[1,64,512]{2,1,0:T(8,128)(2,1)S(1)}, u32[]{:S(2)}, u32[]{:S(2)}) collective-permute-start(bf16[1,64,512]{2,1,0:T(8,128)(2,1)S(1)} %bitcast.214), channel_id=1, source_target_pairs={{0,16},{2,18},{4,20},{6,22},{8,24},{10,26},{12,28},{14,30},{16,0},... | collective-permute-start | bytes 196616 | tf_op jit(solution)/shard_map/ppermute | solution.py:66
  199.4 18.1 %collective-permute-start.34 = (bf16[1,64,512]{2,1,0:T(8,128)(2,1)S(1)}, bf16[1,64,512]{2,1,0:T(8,128)(2,1)S(1)}, u32[]{:S(2)}, u32[]{:S(2)}) collective-permute-start(bf16[1,64,512]{2,1,0:T(8,128)(2,1)S(1)} %bitcast.215), channel_id=1, source_target_pairs={{0,8},{2,10},{4,12},{6,14},{8,0},{10,2},{12,4},{14,6},{16,24},{18,... | collective-permute-start | bytes 196616 | tf_op jit(solution)/shard_map/ppermute | solution.py:66
  217.6 7.9 %collective-permute-start.37 = (bf16[4,64,512]{2,1,0:T(8,128)(2,1)S(1)}, bf16[4,64,512]{2,1,0:T(8,128)(2,1)S(1)}, u32[]{:S(2)}, u32[]{:S(2)}) collective-permute-start(bf16[4,64,512]{2,1,0:T(8,128)(2,1)S(1)} %pad_maximum_fusion.6), channel_id=1, source_target_pairs={{0,4},{2,6},{4,0},{6,2},{8,12},{10,14},{12,8},{14,10},{16,20},{18,... | collective-permute-start | bytes 786440 | tf_op jit(solution)/shard_map/ppermute | solution.py:42
  219.3 16.8 %collective-permute-start.40 = (bf16[128,512]{1,0:T(8,128)(2,1)S(1)}, bf16[128,512]{1,0:T(8,128)(2,1)S(1)}, u32[]{:S(2)}, u32[]{:S(2)}) collective-permute-start(bf16[128,512]{1,0:T(8,128)(2,1)S(1)} %big_newton.1), channel_id=1, source_target_pairs={{0,1},{1,0},{2,3},{3,2},{4,5},{5,4},{6,7},{7,6},{8,9},{9,8},{10,11... | collective-permute-start | bytes 393224 | tf_op jit(solution)/shard_map/ppermute | solution.py:42
  (45 other events, 311.8 us)

commit v3 on v2

--- a/solution.py
+++ b/solution.py
@@ -65,14 +65,14 @@
         others = [
             lax.ppermute(values, "win", [(i, i ^ mask) for i in range(size)]) for mask in (4, 8, 12)
         ]
-        return jnp.concatenate([values] + others)
+        return [jnp.concatenate([values] + others)]
     for bit in far_bits():
-        values = gather_bit(values, bit)
-    return values
-
-
-def gather_bit(values, bit):
-    return jnp.concatenate([values, swap(values, "win", bit)])
+        values = jnp.concatenate([values, swap(values, "win", bit)])
+    return [values]
+
+
+def gather_bit(pieces, bit):
+    return pieces + [swap(piece, "win", bit) for piece in pieces]
 
 
 def gather_stages(low=0):
@@ -89,97 +89,118 @@
     return values
 
 
-def index_order(blocks):
+def index_order(pieces):
     masks = gather_masks()
     by_mask = sorted(range(len(masks)), key=masks.__getitem__)
     places = lax.axis_index("win") ^ jnp.arange(len(masks))
-    return blocks[jnp.array(by_mask)][places]
-
-
-class Chain:
-    def __init__(self, value, stages):
-        self.value = value
-        self.stages = list(stages)
-
-    def step(self):
-        if self.stages:
-            self.value = self.stages.pop(0)(self.value)
+    return [jnp.concatenate(pieces)[jnp.array(by_mask)][places]]
 
 
 def tie(*values):
     return lax.optimization_barrier(values)
 
 
-def step_together(*chains):
-    for chain in chains:
-        chain.step()
-    for chain, value in zip(chains, tie(*[chain.value for chain in chains])):
-        chain.value = value
-
-
-def halve_blocks(values, bit, bits_left):
-    place = bits_left.index(bit)
-    split = values.reshape((2,) * len(bits_left) + values.shape[1:])
-    mine = my_bit("win", bit)
-    kept = lax.dynamic_index_in_dim(split, mine, place, keepdims=False)
-    sent = lax.dynamic_index_in_dim(split, 1 - mine, place, keepdims=False)
-    total = kept + swap(bfloat(sent), "win", bit).astype(jnp.float32)
-    left = [other for other in bits_left if other != bit]
-    return total.reshape((-1,) + values.shape[1:]), left
-
-
-def halve_columns(values):
+def after(value, *others):
+    return lax.optimization_barrier((value,) + others)[0]
+
+
+class Order:
+    def __init__(self):
+        self.sent = ()
+
+    def launch(self, *hops):
+        self.sent = tuple(array for array, _, _ in hops)
+        return [
+            lax.ppermute(array, axis, [(i, i ^ mask) for i in range(lax.axis_size(axis))])
+            for array, axis, mask in hops
+        ]
+
+    def land(self, values):
+        return after(values, *self.sent)
+
+
+def pick(values, index, axis=0):
+    return lax.dynamic_index_in_dim(values, index, axis, keepdims=False)
+
+
+def wide(values):
+    return values.astype(jnp.float32)
+
+
+def rounded(values):
+    return lax.reduce_precision(values, 8, 7)
+
+
+def same_sum(values, axis, bit):
+    low = rounded(values)
+    return low + wide(swap(bfloat(low), axis, bit))
+
+
+def place_bits():
+    win_index = lax.axis_index("win")
+    return lax.axis_index("rep"), win_index >> 2, (win_index >> 1) & 1, win_index & 1
+
+
+def first_parts(total):
+    rep, _, side, _ = place_bits()
+    half = total.shape[-1] // 2
+    left, right = total[..., :half], total[..., half:]
+    right = right.reshape(2, -1, 2, right.shape[2], half)
+    kept = pick(left, rep), pick(right, side, 2)
+    sent = bfloat(pick(left, 1 - rep)), bfloat(pick(right, 1 - side, 2))
+    return kept, ((sent[0], "rep", 1), (sent[1], "win", 2))
+
+
+def first_parts_of_two(totals):
+    rep, _, side, _ = place_bits()
+    half = totals[0].shape[-1] // 2
+    left = [total[..., :half] for total in totals]
+    right = [total[..., half:].reshape(-1, 2, total.shape[1], half) for total in totals]
+    own, other = pick_owner(rep == 0, *left)
+    kept = own, jnp.stack([pick(part, side, 1) for part in right])
+    sent = bfloat(other), bfloat(jnp.stack([pick(part, 1 - side, 1) for part in right]))
+    return kept, ((sent[0], "rep", 1), (sent[1], "win", 2))
+
+
+def second_parts(left, right):
+    rep, _, side, _ = place_bits()
+    left = left.reshape(-1, 2, *left.shape[1:])
+    kept = pick(left, side, 1), pick(right, rep)
+    sent = bfloat(pick(left, 1 - side, 1)), bfloat(pick(right, 1 - rep))
+    return kept, ((sent[0], "win", 2), (sent[1], "rep", 1))
+
+
+def far_parts(total):
+    far = place_bits()[1]
+    hops = tuple((bfloat(pick(total, far ^ mask)), "win", mask << 2) for mask in (1, 2, 3))
+    return pick(total, far), hops
+
+
+def add_pair(kept, taken):
+    return kept[0] + wide(taken[0]), kept[1] + wide(taken[1])
+
+
+def add_far(kept, taken):
+    return (kept + wide(taken[0])) + (wide(taken[1]) + wide(taken[2]))
+
+
+def join_halves(pair):
+    return jnp.concatenate(pair, axis=-1)
+
+
+def spread_far(values):
+    return tuple((values[None], "win", mask) for mask in (4, 8, 12))
+
+
+def far_piece(values, taken):
+    return jnp.concatenate([values[None], *taken])
+
+
+def sum_everywhere(values, skip_core=True):
+    for bit in range(1 if skip_core else 0, bit_count("win")):
+        values = same_sum(values, "win", bit)
     for bit in range(bit_count("rep")):
-        half = values.shape[-1] // 2
-        last = values.ndim - 1
-        mine = my_bit("rep", bit)
-        kept = lax.dynamic_slice_in_dim(values, mine * half, half, last)
-        sent = lax.dynamic_slice_in_dim(values, (1 - mine) * half, half, last)
-        values = kept + swap(bfloat(sent), "rep", bit).astype(jnp.float32)
-    return values
-
-
-def join_columns(values):
-    values = bfloat(values)
-    for bit in reversed(range(bit_count("rep"))):
-        other = swap(values, "rep", bit)
-        first = my_bit("rep", bit) == 0
-        values = jnp.concatenate(
-            [jnp.where(first, values, other), jnp.where(first, other, values)], axis=-1
-        )
-    return values.astype(jnp.float32)
-
-
-def scatter_stages():
-    bits = list(range(1, bit_count("win")))[::-1]
-    left = bits[:-1]
-
-    def first_stage(pair):
-        return halve_columns(pair[0]), halve_blocks(pair[1], 1, bits)[0]
-
-    def second_stage(pair):
-        return halve_blocks(pair[0], 1, bits)[0], halve_columns(pair[1])
-
-    def far_stage(number):
-        def stage(values):
-            if number == 0:
-                values = jnp.concatenate(values, axis=1)
-            rest = [other for other in left if other not in far_bits()[:number]]
-            return halve_blocks(values, far_bits()[number], rest)[0]
-
-        return stage
-
-    return (
-        [first_stage, second_stage]
-        + [far_stage(number) for number in range(len(far_bits()))]
-        + [lambda values: join_columns(values)[0]]
-    )
-
-
-def sum_over_rep(values):
-    for bit in range(bit_count("rep")):
-        low = bfloat(values)
-        values = low.astype(jnp.float32) + swap(low, "rep", bit).astype(jnp.float32)
+        values = same_sum(values, "rep", bit)
     return values
 
 
@@ -225,22 +246,32 @@
     return pl.multiple_of(((place_ref[1] ^ masks[block]) >> shift) * rows, rows)
 
 
-def big_newton_kernel(folds, masks, place_ref, blocks_ref, out_ref, iterate_ref, turned_ref):
-    blocks, rows, width = blocks_ref.shape
+def numbered_blocks(piece_refs):
+    for piece, piece_ref in enumerate(piece_refs):
+        blocks = piece_ref.shape[0]
+        for block in range(blocks):
+            yield piece * blocks + block, piece_ref.at[block]
+
+
+def big_newton_kernel(folds, masks, place_ref, *refs):
+    piece_refs, (out_ref, iterate_ref, turned_ref) = refs[:-3], refs[-3:]
+    _, rows, width = piece_refs[0].shape
     part = rows // folds
 
     @pl.when(place_ref[0] == 0)
     def _():
-        for block in range(blocks):
+        for block, block_ref in numbered_blocks(piece_refs):
+            start = block_start(place_ref, masks, block, part)
             for fold in range(folds):
-                start = block_start(place_ref, masks, block, part)
-                iterate_ref[pl.ds(start, part), fold * width : (fold + 1) * width] = blocks_ref[block, fold * part : (fold + 1) * part, :].astype(jnp.float32)
+                lanes = slice(fold * width, (fold + 1) * width)
+                inner = slice(fold * part, (fold + 1) * part)
+                iterate_ref[pl.ds(start, part), lanes] = block_ref[inner, :].astype(jnp.float32)
 
     @pl.when(place_ref[0] != 0)
     def _():
-        for block in range(blocks):
+        for block, block_ref in numbered_blocks(piece_refs):
             start = block_start(place_ref, masks, block, rows)
-            iterate_ref[:, pl.ds(start, rows)] = blocks_ref[block].astype(jnp.float32).T
+            iterate_ref[:, pl.ds(start, rows)] = block_ref[...].astype(jnp.float32).T
 
     iterate_ref[...] = unit_scale(iterate_ref[...])
 
@@ -265,14 +296,13 @@
         out_ref[...] = bfloat(turned_ref[pl.ds(inner, rows), :])
 
 
-def small_newton_kernel(masks, place_ref, blocks_ref, out_ref, iterate_ref):
-    blocks, matrices, rows, width = blocks_ref.shape
-    for number in range(matrices):
-        for block in range(blocks):
-            start = block_start(place_ref, masks, block, rows, 1)
-            iterate_ref[number, pl.ds(start, rows), :] = blocks_ref[block, number].astype(
-                jnp.float32
-            )
+def small_newton_kernel(masks, place_ref, *refs):
+    piece_refs, (out_ref, iterate_ref) = refs[:-2], refs[-2:]
+    _, matrices, rows, width = piece_refs[0].shape
+    for block, block_ref in numbered_blocks(piece_refs):
+        start = block_start(place_ref, masks, block, rows, 1)
+        for number in range(matrices):
+            iterate_ref[number, pl.ds(start, rows), :] = block_ref[number].astype(jnp.float32)
 
     @pl.loop(0, matrices)
     def _(number):
@@ -291,62 +321,50 @@
         out_ref[number] = bfloat(iterate_ref[number, pl.ds(start, rows), :])
 
 
-def newton_call(kernel, name, place, blocks, out_dims, scratch_dims, flops):
+def newton_call(kernel, name, place, pieces, out_dims, scratch_dims, flops):
     return pl.pallas_call(
         kernel,
-        in_specs=[
-            pl.BlockSpec(memory_space=pltpu.SMEM),
-            pl.BlockSpec(memory_space=pltpu.VMEM),
-        ],
+        in_specs=[pl.BlockSpec(memory_space=pltpu.SMEM)]
+        + [pl.BlockSpec(memory_space=pltpu.VMEM)] * len(pieces),
         out_specs=pl.BlockSpec(memory_space=pltpu.VMEM),
         out_shape=shape_of(out_dims, jnp.bfloat16),
         scratch_shapes=[pltpu.VMEM(dims, jnp.float32) for dims in scratch_dims],
         compiler_params=pltpu.CompilerParams(vmem_limit_bytes=VMEM_LIMIT),
-        cost_estimate=pl.CostEstimate(
-            flops=flops, bytes_accessed=2 * blocks.size, transcendentals=0
-        ),
+        cost_estimate=pl.CostEstimate(flops=1, bytes_accessed=1, transcendentals=0),
         name=name,
-    )(place, blocks)
-
-
-def big_update(place, blocks, folds, masks):
-    win, rows, width = blocks.shape
+    )(place, *pieces)
+
+
+def big_update(place, pieces, folds, masks):
+    blocks, rows, width = pieces[0].shape
+    columns = len(pieces) * blocks * rows
     return newton_call(
         functools.partial(big_newton_kernel, folds, masks),
         "big_newton",
         place,
-        blocks,
+        pieces,
         (rows, width),
-        [(width, win * rows), (max(rows, 128), width)],
-        2 * 5 * width * width * (2 * win * rows + width),
-    )
-
-
-def small_update(place, blocks, masks):
-    win, matrices, rows, width = blocks.shape
+        [(width, columns), (max(rows, 128), width)],
+        2 * 5 * width * width * (2 * columns + width),
+    )
+
+
+def small_update(place, pieces, masks):
+    _, matrices, rows, width = pieces[0].shape
     return newton_call(
         functools.partial(small_newton_kernel, masks),
         "small_newton",
         place,
-        blocks,
+        pieces,
         (matrices, rows, width),
         [(matrices, width, width)],
         2 * 27 * matrices * width**3,
     )
 
 
-def own_rows(matrix, rows_here):
-    return lax.dynamic_slice_in_dim(matrix, lax.axis_index("win") * rows_here, rows_here, 0)
-
-
 def fold_columns(rows, width):
     count, columns = rows.shape
     return rows.reshape(count, columns // width, width).swapaxes(0, 1).reshape(-1, width)
-
-
-def unfold_columns(rows, folds):
-    total, width = rows.shape
-    return rows.reshape(folds, total // folds, width).swapaxes(0, 1).reshape(-1, folds * width)
 
 
 def pick_owner(first, here, there):
@@ -368,6 +386,7 @@
 LOG2_E = 1.4426950408889634
 VMEM_LIMIT = 44 * 1024 * 1024
 WINDOW_COST = 10**9
+VECTOR_ROWS = 16
 NT = (((1,), (1,)), ((), ()))
 TN = (((0,), (0,)), ((), ()))
 
@@ -600,7 +619,13 @@
             region_branch = bfloat(region_keep_ref[...] * region_grad_out[...])
             sums_out[8:9, :] += jnp.sum(region_branch.astype(jnp.float32), 0, keepdims=True)
             region_branch_out[...] = region_branch
-            region_mix_out[...] = bfloat(dot_as(region_branch, out_ref[...], NT))
+            regions = region_branch.shape[0]
+            spare_rows = region_mix_out.shape[0] - regions - sums_out.shape[0]
+            region_mix_out[:regions, :] = bfloat(dot_as(region_branch, out_ref[...], NT))
+            sums_low = jnp.concatenate(
+                [sums_out[...], jnp.zeros((spare_rows, width), jnp.float32)], axis=0
+            )
+            region_mix_out[regions:, :] = bfloat(sums_low)
 
 
 def window_step(windows):
@@ -741,8 +766,9 @@
         hbm_shape((here, padded, width), jnp.bfloat16),
     ]
     if last:
-        out_specs += [whole_spec(region.shape)] * 2
-        out_shape += [shape_of(region.shape, jnp.bfloat16)] * 2
+        payload = (region.shape[0] + VECTOR_ROWS, width)
+        out_specs += [whole_spec(region.shape), whole_spec(payload)]
+        out_shape += [shape_of(region.shape, jnp.bfloat16), shape_of(payload, jnp.bfloat16)]
     return pl.pallas_call(
         functools.partial(window_backward_kernel, count, first_step, last, seq_len, padded),
         grid=(last_step - first_step,),
@@ -826,10 +852,8 @@
     out_ref,
     grad_ref,
     sums_ref,
-    up_kept,
-    up_sent,
-    down_kept,
-    down_sent,
+    kept_ref,
+    sent_ref,
     cot_fill,
     up_total,
     down_total,
@@ -892,16 +916,16 @@
     @pl.when(step == pl.num_programs(0) - 1)
     def _():
         core = place_ref[1] % 2
-        blocks, _, rows, _ = up_kept.shape
+        _, blocks, rows, _ = kept_ref.shape
+        part, here = rows // folds, blocks // folds
         for fold in range(folds):
-            total = up_total[fold].reshape(blocks, 2, rows, width)
-            up_kept[:, fold], up_sent[:, fold] = split_cores(total, core)
-        blocks, rows, _ = down_kept.shape
-        here = blocks // folds
+            total = up_total[fold].reshape(blocks, 2, part, width)
+            inner = slice(fold * part, (fold + 1) * part)
+            kept_ref[0, :, inner], sent_ref[0, :, inner] = split_cores(total, core)
         for fold in range(folds):
             total = down_total[fold].reshape(here, 2, rows, width)
-            part = slice(fold * here, (fold + 1) * here)
-            down_kept[part], down_sent[part] = split_cores(total, core)
+            inner = slice(fold * here, (fold + 1) * here)
+            kept_ref[1, inner], sent_ref[1, inner] = split_cores(total, core)
 
 
 def mlp(place, after, cotangent, keep, vectors, up_weight, down_weight, padded, win_count):
@@ -911,10 +935,9 @@
     folds = up_weight.shape[1] // width
     half = win_count // 2
     up_rows = width // win_count
-    up_dims = (half, folds, up_rows, width)
-    down_dims = (half, up_rows * folds, width)
+    dims = (2, half, up_rows * folds, width)
     flat_rows = pl.BlockSpec((rows, width), lambda step: (step, 0))
-    output, grad, sums, kept_up, sent_up, kept_down, sent_down = pl.pallas_call(
+    output, grad, sums, kept, sent = pl.pallas_call(
         functools.partial(mlp_kernel, count, seq_len, padded),
         grid=(windows // count,),
         in_specs=[
@@ -930,19 +953,15 @@
             token_spec(count, seq_len, width),
             flat_rows,
             whole_spec(vectors.shape),
-            whole_spec(up_dims),
-            whole_spec(up_dims),
-            whole_spec(down_dims),
-            whole_spec(down_dims),
+            whole_spec(dims),
+            whole_spec(dims),
         ],
         out_shape=[
             hbm_shape(cotangent.shape, jnp.bfloat16),
             hbm_shape(after.shape),
             hbm_shape(vectors.shape),
-            hbm_shape(up_dims),
-            hbm_shape(up_dims, jnp.bfloat16),
-            hbm_shape(down_dims),
-            hbm_shape(down_dims, jnp.bfloat16),
+            hbm_shape(dims),
+            hbm_shape(dims, jnp.bfloat16),
         ],
         scratch_shapes=[
             pltpu.VMEM((rows, width), jnp.float32),
@@ -950,15 +969,10 @@
             pltpu.VMEM((folds, width, width), jnp.float32),
         ],
         compiler_params=pltpu.CompilerParams(vmem_limit_bytes=VMEM_LIMIT),
-        cost_estimate=pl.CostEstimate(
-            flops=12 * after.size * width * folds,
-            bytes_accessed=16 * after.size,
-            transcendentals=0,
-        ),
+        cost_estimate=pl.CostEstimate(flops=1, bytes_accessed=1, transcendentals=0),
         name="mlp",
     )(place, in_hbm(after), in_hbm(cotangent), keep, vectors, up_weight, down_weight)
-    up_half = (kept_up.reshape(down_dims), sent_up.reshape(down_dims))
-    return output, grad, sums, up_half, (kept_down, sent_down)
+    return output, grad, sums, (kept, sent)
 
 
 def image_bias(keys_ref, queries_ref):
@@ -966,7 +980,15 @@
 
 
 def region_forward_kernel(
-    all_ref,
+    pieces,
+    *refs,
+):
+    piece_refs, refs = refs[:pieces], refs[pieces:]
+    region_forward_rows(piece_refs, *refs)
+
+
+def region_forward_rows(
+    piece_refs,
     own_ref,
     keep_ref,
     key_image_ref,
@@ -978,10 +1000,13 @@
     proj_out,
     mix_out,
     new_out,
+    all_ref,
 ):
     rows, width = own_ref.shape
     vec = vec_ref[...]
-    normed = bfloat(norm_rows(all_ref[...].astype(jnp.float32), vec[0:1], vec[1:2]))
+    for block, block_ref in numbered_blocks(piece_refs):
+        all_ref[block * rows : (block + 1) * rows, :] = block_ref[...].astype(jnp.float32)
+    normed = bfloat(norm_rows(all_ref[...], vec[0:1], vec[1:2]))
     norm_out[...] = normed
     query = bfloat(product(normed, qkv_ref[0]) + vec[6:7])
     keyset = bfloat(product(normed, qkv_ref[1]))
@@ -1007,27 +1032,35 @@
     new_out[...] = region + keep_ref[...] * branch
 
 
-def region_forward(all_rows, own_rows_, keep, key_images, query_images, qkv_weight, out_weight, vectors):
-    total, width = all_rows.shape
+def region_forward(pieces, own, keep, key_images, query_images, qkv_weight, out_weight, vectors):
+    rows, width = own.shape
+    total = len(pieces) * pieces[0].shape[0] * rows
     return pl.pallas_call(
-        region_forward_kernel,
+        functools.partial(region_forward_kernel, len(pieces)),
         out_shape=[
             hbm_shape((total, width), jnp.bfloat16),
             hbm_shape((total, 3 * width), jnp.bfloat16),
-            hbm_shape(own_rows_.shape, jnp.bfloat16),
-            shape_of(own_rows_.shape),
+            hbm_shape(own.shape, jnp.bfloat16),
+            shape_of(own.shape),
         ],
+        scratch_shapes=[pltpu.VMEM((total, width), jnp.float32)],
         compiler_params=pltpu.CompilerParams(vmem_limit_bytes=VMEM_LIMIT),
         name="region_forward",
-    )(all_rows, own_rows_, keep, key_images, query_images, qkv_weight, out_weight, vectors)
-
-
-def region_backward_kernel(
+    )(*pieces, own, keep, key_images, query_images, qkv_weight, out_weight, vectors)
+
+
+def region_backward_kernel(pieces, place_ref, *refs):
+    region_refs, refs = refs[:pieces], refs[pieces:]
+    gathered_refs, refs = refs[:pieces], refs[pieces:]
+    region_backward_rows(place_ref, region_refs, gathered_refs, *refs)
+
+
+def region_backward_rows(
     place_ref,
-    all_ref,
+    region_refs,
+    gathered_refs,
     norm_ref,
     proj_ref,
-    mix_grad_ref,
     key_image_ref,
     query_image_ref,
     new_grad_ref,
@@ -1040,6 +1073,8 @@
     proj_grad_ref,
     region_grad_ref,
     weight_ref,
+    mix_grad_ref,
+    all_ref,
     scores_ref,
     probs_grad_ref,
     probs_ref,
@@ -1049,36 +1084,43 @@
     rows = new_grad_ref.shape[0]
     bias_ref[...] = image_bias(key_image_ref, query_image_ref)
     lane_head = lax.broadcasted_iota(jnp.int32, (total, 128), 1) // HEAD_DIM
+    for block, block_ref in numbered_blocks(region_refs):
+        all_ref[block * rows : (block + 1) * rows, :] = block_ref[...].astype(jnp.float32)
+    vector_sum = jnp.zeros((VECTOR_ROWS, width), jnp.float32)
+    for block, block_ref in numbered_blocks(gathered_refs):
+        part = block_ref[...].astype(jnp.float32)
+        mix_grad_ref[block * rows : (block + 1) * rows, :] = part[:rows]
+        vector_sum += part[rows:]
 
     @pl.loop(0, width // 128)
     def _(group):
         query_lanes = pl.ds(pl.multiple_of(group * 128, 128), 128)
         key_lanes = pl.ds(pl.multiple_of(width + group * 128, 128), 128)
         value_lanes = pl.ds(pl.multiple_of(2 * width + group * 128, 128), 128)
-        query = proj_ref[:, query_lanes]
         key_low = proj_ref[:, key_lanes]
         value_low = proj_ref[:, value_lanes]
-        mix_grad = mix_grad_ref[:, query_lanes]
-        heads = range(GROUP_HEADS)
-        head_query = [jnp.where(lane_head == head, query, jnp.zeros_like(query)) for head in heads]
-        head_grad = [
-            jnp.where(lane_head == head, mix_grad, jnp.zeros_like(mix_grad)) for head in heads
-        ]
-        for head in heads:
-            scores_ref[head] = dot_as(key_low, head_query[head], NT)
-            probs_grad_ref[head] = dot_as(value_low, head_grad[head], NT)
-        for head in heads:
-            probs = column_softmax(scores_ref[head], bias_ref[...])
-            weighted = probs * probs_grad_ref[head]
-            probs_ref[head] = bfloat(probs)
-            score_grad_ref[head] = bfloat(weighted - probs * jnp.sum(weighted, 0, keepdims=True))
-        zero = jnp.zeros((total, 128), jnp.float32)
-        value_grad = sum((product(probs_ref[head], head_grad[head]) for head in heads), zero)
-        key_grad = sum((product(score_grad_ref[head], head_query[head]) for head in heads), zero)
-        query_grad = zero
-        for head in heads:
-            head_part = dot_as(score_grad_ref[head], key_low, TN)
-            query_grad = jnp.where(lane_head == head, head_part, query_grad)
+        spread = spread_heads(proj_ref[:, query_lanes].astype(jnp.float32), lane_head)
+        spread_grad = spread_heads(mix_grad_ref[:, query_lanes], lane_head)
+        scores_ref[...] = dot_as(key_low, spread, NT)
+        probs_grad_ref[...] = dot_as(value_low, spread_grad, NT)
+        for head in range(GROUP_HEADS):
+            lanes = slice(head * total, (head + 1) * total)
+            probs = column_softmax(scores_ref[:, lanes], bias_ref[...])
+            weighted = probs * probs_grad_ref[:, lanes]
+            probs_ref[:, lanes] = bfloat(probs)
+            score_grad_ref[:, lanes] = bfloat(
+                weighted - probs * jnp.sum(weighted, 0, keepdims=True)
+            )
+        value_grad = product(probs_ref[...], spread_grad)
+        key_grad = product(score_grad_ref[...], spread)
+        turned = product(key_low.T, score_grad_ref[...])
+        query_grad = jnp.concatenate(
+            [
+                turned[head * HEAD_DIM : (head + 1) * HEAD_DIM, head * total : (head + 1) * total]
+                for head in range(GROUP_HEADS)
+            ],
+            axis=0,
+        ).T
         proj_grad_ref[:, query_lanes] = bfloat(query_grad * SCORE_SCALE)
         proj_grad_ref[:, key_lanes] = bfloat(key_grad * SCORE_SCALE)
         proj_grad_ref[:, value_lanes] = bfloat(value_grad)
@@ -1088,7 +1130,7 @@
         dot_as(proj_grad[:, number * width : (number + 1) * width], qkv_ref[number], NT)
         for number in range(3)
     )
-    region = all_ref[...].astype(jnp.float32)
+    region = all_ref[...]
     center = region - jnp.mean(region, -1, keepdims=True)
     scale = lax.rsqrt(jnp.mean(center * center, -1, keepdims=True) + EPSILON)
     hat = center * scale
@@ -1100,14 +1142,14 @@
     )
     grad_out[...] = new_grad_ref[...] + region_grad_ref[:rows, :]
     bias_sums = jnp.sum(proj_grad.astype(jnp.float32), 0, keepdims=True)
-    sums_out[...] = jnp.zeros_like(sums_out)
-    sums_out[0:1, :] = jnp.sum(norm_grad * hat, 0, keepdims=True)
-    sums_out[1:2, :] = jnp.sum(norm_grad, 0, keepdims=True)
-    sums_out[6:7, :] = bias_sums[:, :width]
-    sums_out[7:8, :] = bias_sums[:, 2 * width :]
+    sums_out[...] = vector_sum
+    sums_out[0:1, :] += jnp.sum(norm_grad * hat, 0, keepdims=True)
+    sums_out[1:2, :] += jnp.sum(norm_grad, 0, keepdims=True)
+    sums_out[6:7, :] += bias_sums[:, :width]
+    sums_out[7:8, :] += bias_sums[:, 2 * width :]
     weight_ref[...] = dot_as(norm_ref[...], proj_grad, TN)
     weight_rows = weight_out.shape[1]
-    weight_start = pl.multiple_of(place_ref[1] * weight_rows, 8)
+    weight_start = pl.multiple_of((place_ref[1] >> 1) * weight_rows, 8)
     for number in range(3):
         weight_out[number] = weight_ref[
             pl.ds(weight_start, weight_rows), number * width : (number + 1) * width
@@ -1115,120 +1157,180 @@
 
 
 def region_backward(
-    place, all_rows, normed, proj, mix_grad, key_images, query_images, new_grad, qkv_weight, vectors, weight_rows
+    place,
+    regions,
+    gathered,
+    normed,
+    proj,
+    key_images,
+    query_images,
+    new_grad,
+    qkv_weight,
+    vectors,
+    weight_rows,
 ):
-    total, width = all_rows.shape
+    total, width = normed.shape
     vmem = pl.BlockSpec(memory_space=pltpu.VMEM)
+    operands = [*regions, *gathered, in_hbm(normed), in_hbm(proj), key_images, query_images]
+    operands += [new_grad, qkv_weight, vectors]
     return pl.pallas_call(
-        region_backward_kernel,
-        in_specs=[pl.BlockSpec(memory_space=pltpu.SMEM)] + [vmem] * 9,
+        functools.partial(region_backward_kernel, len(regions)),
+        grid=(1,),
+        in_specs=[pl.BlockSpec(memory_space=pltpu.SMEM)]
+        + [whole_spec(operand.shape) for operand in operands[:-2]]
+        + [vmem, whole_spec(vectors.shape)],
         out_specs=[vmem] * 3,
         out_shape=[
             shape_of(new_grad.shape),
             shape_of((3, weight_rows, width)),
-            shape_of(vectors.shape),
+            shape_of((VECTOR_ROWS, width)),
         ],
         scratch_shapes=[
             pltpu.VMEM((total, total), jnp.float32),
             pltpu.VMEM((total, 3 * width), jnp.bfloat16),
             pltpu.VMEM((total, width), jnp.float32),
             pltpu.VMEM((width, 3 * width), jnp.float32),
-            pltpu.VMEM((GROUP_HEADS, total, total), jnp.float32),
-            pltpu.VMEM((GROUP_HEADS, total, total), jnp.float32),
-            pltpu.VMEM((GROUP_HEADS, total, total), jnp.bfloat16),
-            pltpu.VMEM((GROUP_HEADS, total, total), jnp.bfloat16),
+            pltpu.VMEM((total, width), jnp.float32),
+            pltpu.VMEM((total, width), jnp.float32),
+            pltpu.VMEM((total, GROUP_HEADS * total), jnp.float32),
+            pltpu.VMEM((total, GROUP_HEADS * total), jnp.float32),
+            pltpu.VMEM((total, GROUP_HEADS * total), jnp.bfloat16),
+            pltpu.VMEM((total, GROUP_HEADS * total), jnp.bfloat16),
         ],
         compiler_params=pltpu.CompilerParams(vmem_limit_bytes=VMEM_LIMIT),
         name="region_backward",
-    )(place, all_rows, normed, proj, mix_grad, key_images, query_images, new_grad, qkv_weight, vectors)
-
-
-def small_gradient_kernel(pieces, place_ref, *refs):
-    norm_refs = refs[:pieces]
-    proj_grad_refs = refs[pieces : 2 * pieces]
-    mix_refs = refs[2 * pieces : 3 * pieces]
-    branch_refs = refs[3 * pieces : 4 * pieces]
-    region_mix_ref, region_branch_ref, kept, sent = refs[4 * pieces :]
-    core = place_ref[1] % 2
-    number = pl.program_id(0)
-    blocks, _, rows, width = kept.shape
-
-    def write(total):
-        kept[:, 0], sent[:, 0] = split_cores(total.reshape(blocks, 2, rows, width), core)
-
-    @pl.when(number < 3)
-    def _():
-        write(
-            sum(
-                dot_as(norm_ref[...], grad_ref[...], TN)
-                for norm_ref, grad_ref in zip(norm_refs, proj_grad_refs)
-            )
-        )
-
-    @pl.when(number == 3)
-    def _():
-        write(
-            sum(
-                dot_as(mix_ref[...], branch_ref[...], TN)
-                for mix_ref, branch_ref in zip(mix_refs, branch_refs)
-            )
-            + dot_as(region_mix_ref[...], region_branch_ref[...], TN)
-        )
-
-
-def small_gradients(place, normed, proj_grads, mix, branches, region_mix, region_branch, win_count):
-    width = normed.shape[1]
-    half = win_count // 2
-    weight_rows = width // win_count
-    pieces = len(proj_grads)
+    )(place, *operands)
+
+
+def pair_gradient_kernel(first_count, second_count, place_ref, *refs):
+    own_first = place_ref[1] % 2 == 0
+    kept, sent = refs[-2:]
+
+    def total(pairs):
+        lefts, rights = pairs[0::2], pairs[1::2]
+        return sum(dot_as(left[...], right[...], TN) for left, right in zip(lefts, rights))
+
+    first = total(refs[: 2 * first_count])
+    second = total(refs[2 * first_count : 2 * (first_count + second_count)])
+    kept[...] = jnp.where(own_first, first, second)
+    sent[...] = bfloat(jnp.where(own_first, second, first))
+
+
+def pair_gradients(place, first, second, width):
     operands, in_specs = [place], [pl.BlockSpec(memory_space=pltpu.SMEM)]
-
-    def add_rows(whole):
-        start = 0
-        for piece in branches:
-            here = piece.shape[0]
-            if start % here:
-                operands.append(whole[start : start + here])
-                block = 0
-            else:
-                operands.append(in_hbm(whole))
-                block = start // here
-            in_specs.append(pl.BlockSpec(piece.shape, lambda number, block=block: (block, 0)))
-            start += here
-
-    add_rows(normed)
-    for piece in proj_grads:
-        operands.append(in_hbm(piece))
-        in_specs.append(
-            pl.BlockSpec((piece.shape[0], width), lambda number: (0, jnp.minimum(number, 2)))
-        )
-    add_rows(mix)
-    for piece in branches + [region_mix, region_branch]:
-        operands.append(in_hbm(piece))
-        in_specs.append(pl.BlockSpec(piece.shape, lambda number: (0, 0)))
-    out_spec = pl.BlockSpec((half, 1, weight_rows, width), lambda number: (0, number, 0, 0))
-    dims = (half, 4, weight_rows, width)
-    rows = normed.shape[0]
-    kept, sent = pl.pallas_call(
-        functools.partial(small_gradient_kernel, pieces),
-        grid=(4,),
+    for left, row, right, column, rows in first + second:
+        operands += [in_hbm(left), in_hbm(right)]
+        in_specs.append(pl.BlockSpec((rows, width), lambda step, row=row: (row, 0)))
+        in_specs.append(pl.BlockSpec((rows, width), lambda step, column=column: (0, column)))
+    return pl.pallas_call(
+        functools.partial(pair_gradient_kernel, len(first), len(second)),
+        grid=(1,),
         in_specs=in_specs,
-        out_specs=[out_spec, out_spec],
-        out_shape=[hbm_shape(dims), hbm_shape(dims, jnp.bfloat16)],
+        out_specs=[whole_spec((width, width))] * 2,
+        out_shape=[hbm_shape((width, width)), hbm_shape((width, width), jnp.bfloat16)],
         compiler_params=pltpu.CompilerParams(vmem_limit_bytes=VMEM_LIMIT),
-        cost_estimate=pl.CostEstimate(
-            flops=8 * rows * width * width,
-            bytes_accessed=12 * rows * width + 24 * width * width,
-            transcendentals=0,
+        cost_estimate=pl.CostEstimate(flops=1, bytes_accessed=1, transcendentals=0),
+        name="pair_gradients",
+    )(*operands)
+
+
+def row_pieces(whole, rights, column):
+    pairs, start = [], 0
+    for right in rights:
+        rows = right.shape[0]
+        left, row = (whole, start // rows) if start % rows == 0 else (whole[start : start + rows], 0)
+        pairs.append((left, row, right, column, rows))
+        start += rows
+    return pairs
+
+
+def finish_big_kernel(
+    place_ref, mine, other, mom_mine, mom_other, up_ref, down_ref, up_new, down_new, up_mom, down_mom
+):
+    first = place_ref[0] == 0
+
+    def ordered(here, there):
+        return jnp.where(first, here, there), jnp.where(first, there, here)
+
+    updates = ordered(mine[...].astype(jnp.float32), other[...].astype(jnp.float32))
+    momenta = ordered(mom_mine[...], mom_other[...])
+    down_new[...] = down_ref[...].astype(jnp.float32) - MATRIX_RATE * updates[1]
+    down_mom[...] = momenta[1]
+    rows, columns = up_ref.shape
+    width = down_ref.shape[1]
+    for fold in range(columns // width):
+        lanes = slice(fold * width, (fold + 1) * width)
+        inner = slice(fold * rows, (fold + 1) * rows)
+        up_new[:, lanes] = up_ref[:, lanes].astype(jnp.float32) - MATRIX_RATE * updates[0][inner]
+        up_mom[:, lanes] = momenta[0][inner]
+
+
+def finish_small_kernel(place_ref, *refs):
+    updates, momenta = refs[:4], refs[4:8]
+    qkv_ref, out_ref, qkv_new, out_new, qkv_mom, out_mom = refs[8:]
+    first, low = place_ref[0] == 0, place_ref[2] == 0
+
+    def ordered(parts):
+        own, side, across, corner = [part[...].astype(jnp.float32) for part in parts]
+        here = jnp.where(low, own, side), jnp.where(low, side, own)
+        there = jnp.where(low, across, corner), jnp.where(low, corner, across)
+        return [jnp.where(first, one, two) for one, two in zip(here + there, there + here)]
+
+    for number, (update, momentum) in enumerate(zip(ordered(updates), ordered(momenta))):
+        if number < 3:
+            qkv_new[number] = qkv_ref[number].astype(jnp.float32) - MATRIX_RATE * update
+            qkv_mom[number] = momentum
+        else:
+            out_new[...] = out_ref[...].astype(jnp.float32) - MATRIX_RATE * update
+            out_mom[...] = momentum
+
+
+def finish_call(kernel, name, place, parts, weights, blocks, indices):
+    dims = [shape_of(block) for block in blocks]
+    return pl.pallas_call(
+        kernel,
+        grid_spec=pltpu.PrefetchScalarGridSpec(
+            num_scalar_prefetch=1,
+            grid=(1,),
+            in_specs=[pl.BlockSpec(part.shape, lambda step, place: (0, 0)) for part in parts]
+            + [pl.BlockSpec(block, index) for block, index in zip(blocks, indices)],
+            out_specs=[
+                pl.BlockSpec(block, lambda step, place, count=len(block): (0,) * count)
+                for block in blocks + blocks
+            ],
         ),
-        name="small_gradients",
-    )(*operands)
-    flat = (half, 4 * weight_rows, width)
-    return kept.reshape(flat), sent.reshape(flat)
-
-
-def core_hop(kept, sent):
-    return kept + swap(sent, "win", 0).astype(jnp.float32)
+        out_shape=dims + dims,
+        compiler_params=pltpu.CompilerParams(vmem_limit_bytes=VMEM_LIMIT),
+        name=name,
+    )(place, *parts, *weights)
+
+
+def finish_big(place, parts, up_weight, down_weight):
+    rows, width = parts[0].shape
+    up_rows = rows * width // up_weight.shape[1]
+    own = lambda step, place: (place[1], 0)
+    return finish_call(
+        finish_big_kernel,
+        "finish_big",
+        place,
+        parts,
+        (up_weight, down_weight),
+        [(up_rows, up_weight.shape[1]), (rows, width)],
+        [own, own],
+    )
+
+
+def finish_small(place, parts, qkv_weight, out_weight):
+    rows, width = parts[0].shape
+    return finish_call(
+        finish_small_kernel,
+        "finish_small",
+        place,
+        parts,
+        (qkv_weight, out_weight),
+        [(3, rows, width), (rows, width)],
+        [lambda step, place: (0, place[1], 0), lambda step, place: (place[1], 0)],
+    )
 
 
 def local(
@@ -1268,7 +1370,7 @@
         return jnp.pad(values, widths, constant_values=fill)
 
     region_own = pad_rows(tokens[0, :, 0], region_rows)
-    region_all = gather_blocks(region_own).reshape(-1, model_width)
+    regions = gather_blocks(region_own)
     keeper = keep_mask[0].astype(jnp.float32) / KEEP_SHARE
     images = image_map[0].reshape(win_count, windows)[win_index ^ jnp.array(gather_masks())]
     images = jnp.pad(images, ((0, 0), (0, region_rows - windows)), constant_values=-1)
@@ -1276,8 +1378,20 @@
     own_images = jnp.tile(images[:1], (1, GROUP_HEADS))
     region_keep = pad_rows(keeper[:, 0:1], region_rows)
 
+    big_moms = (
+        MOMENTUM_DECAY * fold_columns(up_mom, model_width),
+        MOMENTUM_DECAY * down_mom,
+    )
+    small_old_moms = MOMENTUM_DECAY * jnp.concatenate([qkv_mom, out_mom[None]])
+    own_pair = jnp.where(lax.axis_index("rep") == 0, small_old_moms[:2], small_old_moms[2:])
+    kept, sent = pick_owner(win_index % 2 == 0, own_pair[0], own_pair[1])
+    small_pair_mom = jnp.concatenate(
+        pick_owner(win_index % 2 == 0, kept, swap(sent, "win", 0))
+    )
+    regions, big_moms, small_pair_mom = tie(regions, big_moms, small_pair_mom)
+
     region_norm, region_proj, region_mix, region_new = region_forward(
-        region_all, region_own, region_keep, key_images, own_images, qkv_weight, out_weight, vectors
+        regions, region_own, region_keep, key_images, own_images, qkv_weight, out_weight, vectors
     )
 
     key_valid = jnp.concatenate([jnp.ones((windows, 1), jnp.int32), patch_mask[0]], axis=1) == 1
@@ -1292,7 +1406,7 @@
     local_mix = local_mix.reshape(row_count, model_width)
     after_attn = after_attn.reshape(row_count, model_width)
 
-    out_tokens, attn_res_grad, mlp_sums, up_half, down_half = mlp(
+    out_tokens, attn_res_grad, mlp_sums, big_halves = mlp(
         place,
         after_attn,
         cotangent,
@@ -1307,10 +1421,9 @@
     steps = windows // window_step(windows)
     cuts = [0, steps * 2 // 5, steps * 4 // 5, steps]
     after_grad = attn_res_grad.reshape(windows, padded, model_width)
-    big = Chain(
-        (up_half, down_half),
-        [lambda halves: (core_hop(*halves[0]), core_hop(*halves[1]))] + scatter_stages(),
-    )
+    two_owners = lax.axis_size("rep") == 2 and len(far_bits()) == 2
+    order = Order()
+    big_taken = order.launch((big_halves[1], "win", 1))
     before = (None, mlp_sums, None)
     proj_grads, branch_grads = [], []
     for piece in range(3):
@@ -1332,133 +1445,170 @@
         before = (seq_grad, sums, region_new_grad)
         proj_grads.append(proj_grad.reshape(-1, 3 * model_width))
         branch_grads.append(branch_grad.reshape(-1, model_width))
-        big.step()
-        if piece < 2:
-            big.value, after_grad = tie(big.value, after_grad)
+        if piece == 0:
+            big_taken, after_grad = tie(big_taken, after_grad)
+            big_total = big_halves[0] + wide(big_taken[0])
+            if two_owners:
+                big_kept, hops = first_parts(big_total)
+                big_taken = order.launch(*hops)
+        if piece == 1 and two_owners:
+            big_taken, after_grad = tie(big_taken, after_grad)
+            big_kept, hops = second_parts(*add_pair(big_kept, big_taken))
+            hops, after_grad = tie([array for array, _, _ in hops], after_grad)
+            big_taken = order.launch((hops[0], "win", 2), (hops[1], "rep", 1))
     region_branch_grad, region_mix_grad = region_parts
-
-    small_kept, small_sent = small_gradients(
+    if two_owners:
+        mix_taken = order.launch(*spread_far(region_mix_grad))
+
+    first = lax.axis_index("rep") == 0
+    low_core = win_index % 2 == 0
+    kept, sent = pair_gradients(
         place,
-        seq_norm,
-        proj_grads,
-        local_mix,
-        branch_grads,
-        region_mix,
-        region_branch_grad,
-        win_count,
-    )
-    core = win_index % 2
-    vector_pairs = sums.reshape(win_count // 2, 2, 1, vec_rows)
-    vector_pairs = jnp.pad(
-        vector_pairs, ((0, 0), (0, 0), (0, 7), (0, model_width - vec_rows))
-    )
-    small_kept = jnp.concatenate(
-        [small_kept, lax.dynamic_index_in_dim(vector_pairs, core, 1, keepdims=False)], axis=1
-    )
-    small_sent = jnp.concatenate(
-        [
-            small_sent,
-            bfloat(lax.dynamic_index_in_dim(vector_pairs, 1 - core, 1, keepdims=False)),
-        ],
-        axis=1,
-    )
-
-    def split_pair(halves):
-        total = core_hop(*halves)
-        return total[:, : 2 * shard_rows], total[:, 2 * shard_rows :]
-
-    small = Chain((small_kept, small_sent), [split_pair] + scatter_stages())
-    mixes = Chain(region_mix_grad, gather_stages())
-    for _ in range(3):
-        step_together(big, small, mixes)
+        row_pieces(seq_norm, proj_grads, 0),
+        row_pieces(seq_norm, proj_grads, 1),
+        model_width,
+    )
+    small_kept = [kept]
+    small_taken = order.launch((sent, "win", 1))
+    if two_owners:
+        mixes = [far_piece(region_mix_grad, order.land(mix_taken))]
+        mix_taken = order.launch((mixes[0], "win", 2))
+        big_kept, hops = far_parts(join_halves(add_pair(big_kept, order.land(big_taken))))
+        hops, mix_out = tie([array for array, _, _ in hops], region_mix)
+        big_taken = order.launch(*[(hop, "win", 4 * (i + 1)) for i, hop in enumerate(hops)])
+    else:
+        mix_out = region_mix
+    kept, sent = pair_gradients(
+        place,
+        row_pieces(seq_norm, proj_grads, 2),
+        row_pieces(local_mix, branch_grads, 0)
+        + [(mix_out, 0, region_branch_grad, 0, region_rows)],
+        model_width,
+    )
+    small_kept.append(kept)
+    small_taken += order.launch((sent, "win", 1))
+    if two_owners:
+        mixes += order.land(mix_taken)
+        mix_taken = order.launch(*[(piece, "win", 1) for piece in mixes])
+    small_totals = [
+        (kept + wide(taken)).reshape(-1, 2 * shard_rows, model_width)
+        for kept, taken in zip(small_kept, order.land(small_taken))
+    ]
+    if two_owners:
+        small_kept, hops = first_parts_of_two(small_totals)
+        small_taken = order.launch(*hops)
+        big_mom = jnp.where(first, big_moms[0], big_moms[1])
+        big_mom = big_mom + add_far(big_kept, order.land(big_taken))
+        big_low = bfloat(big_mom)
+        big_taken = order.launch(*spread_far(big_low))
+        mixes += order.land(mix_taken)
+        mixes = order.land(mixes)
+    else:
+        mixes = gather_blocks(region_mix_grad)
 
     region_grad, region_weight_grad, region_sums = region_backward(
         place,
-        region_all,
+        regions,
+        mixes,
         region_norm,
         region_proj,
-        mixes.value.reshape(-1, model_width),
         key_images,
         key_images.reshape(1, -1),
         region_new_grad,
         qkv_weight,
         vectors,
-        shard_rows,
-    )
-    input_grad = insert_regions(seq_grad, region_grad).reshape(tokens.shape)
-    region_vectors = jnp.pad(
-        lax.dynamic_slice_in_dim(region_sums.reshape(-1), win_index * vec_rows, vec_rows)[None],
-        ((0, 7), (0, model_width - vec_rows)),
-    )
-    region_part = Chain(
-        jnp.concatenate([region_weight_grad.reshape(-1, model_width), region_vectors], axis=0),
-        [sum_over_rep],
-    )
-
-    first = lax.axis_index("rep") == 0
-    low_core = core == 0
-    two_owners = lax.axis_size("rep") == 2
-    while big.stages:
-        big.step()
-    folded_up_mom = MOMENTUM_DECAY * fold_columns(up_mom, model_width) + big.value[:ff_rows]
-    new_down_mom = MOMENTUM_DECAY * down_mom + big.value[ff_rows:]
+        2 * shard_rows,
+    )
+
     if two_owners:
-        big = Chain(bfloat(jnp.where(first, folded_up_mom, new_down_mom)), gather_stages())
-        big.step()
-        small.step()
-        big.value, small.value, region_part.value = tie(
-            big.value, small.value, region_part.value
+        def spread_pair(mine):
+            mine = mine.reshape(2, shard_rows, model_width)
+            kept, sent = pick_owner(low_core, mine[0], mine[1])
+            taken = order.launch((sent, "win", 1), (kept, "rep", 1), (sent, ("win", "rep"), 3))
+            return kept, taken
+
+        rep_rows = jnp.stack(
+            [
+                jnp.where(low_core, region_weight_grad[0], region_weight_grad[1]),
+                jnp.where(low_core, region_weight_grad[2], 0.0),
+            ]
         )
-        step_together(big, small, region_part)
-        step_together(big, small)
-    while small.stages or region_part.stages:
-        small.step()
-        region_part.step()
-    small_total, region_total = small.value, region_part.value
-    matrix_rows = 4 * shard_rows
-    region_matrix = region_total[: 3 * shard_rows].reshape(3, shard_rows, model_width)
-    small_matrix = small_total[:matrix_rows].reshape(4, shard_rows, model_width)
-    new_qkv_mom = MOMENTUM_DECAY * qkv_mom + (small_matrix[:3] + region_matrix)
-    new_out_mom = MOMENTUM_DECAY * out_mom + small_matrix[3]
-    vec_total = small_total[matrix_rows, :vec_rows] + region_total[3 * shard_rows, :vec_rows]
+        rep = lax.axis_index("rep")
+        vec_mine = rounded(region_sums)
+        small_kept, hops = second_parts(*add_pair(small_kept, order.land(small_taken)))
+        small_taken = order.launch(*hops)
+        vec_taken = order.launch(
+            (bfloat(jnp.concatenate([pick(rep_rows, 1 - rep), vec_mine])), "rep", 1)
+        )
+        big_pieces = [far_piece(big_low, order.land(big_taken))]
+        big_taken = order.launch((big_pieces[0], "win", 2))
+        small_kept, hops = far_parts(join_halves(add_pair(small_kept, order.land(small_taken))))
+        small_taken = order.launch(*hops)
+        vec_taken = wide(vec_taken[0])
+        region_rows_sum = pick(rep_rows, rep) + vec_taken[: 2 * shard_rows]
+        vec_sum = vec_mine + vec_taken[2 * shard_rows :]
+        big_pieces += order.land(big_taken)
+        big_taken = order.launch(*[(piece, "win", 1) for piece in big_pieces])
+        small_mom = add_far(small_kept, order.land(small_taken)) + region_rows_sum
+        small_mom = small_pair_mom + small_mom
+        small_low = bfloat(small_mom)
+        small_taken = order.launch(*spread_far(small_low))
+        input_grad = insert_regions(seq_grad, after(region_grad, *order.sent))
+        input_grad = input_grad.reshape(tokens.shape)
+        small_pieces = [far_piece(small_low, order.land(small_taken))]
+        small_taken = order.launch((small_pieces[0], "win", 2))
+        mom_parts = spread_pair(small_mom)
+        other_mom = order.launch((big_mom, "rep", 1))[0]
+        big_pieces += order.land(big_taken)
+        big_mine = big_update(place, big_pieces, folds, gather_masks())
+
+        other_update = order.launch((big_mine, "rep", 1))[0]
+        small_pieces += order.land(small_taken)
+        small_pieces, mom_parts, other_mom = tie(small_pieces, mom_parts, other_mom)
+        small_mine = small_update(
+            place, [piece[:, None] for piece in small_pieces], gather_masks(1)
+        )[0]
+        update_parts = spread_pair(small_mine)
+        other_update = order.land(other_update)
+        finish_place = jnp.concatenate([place, place[1:] & 1])
+        big_parts = [big_mine, other_update, big_mom, other_mom]
+        small_parts = [update_parts[0], *update_parts[1], mom_parts[0], *mom_parts[1]]
+    else:
+        input_grad = insert_regions(seq_grad, region_grad).reshape(tokens.shape)
+        big_total = pick(sum_everywhere(big_total), win_index >> 1, 1)
+        folded_up_mom = big_moms[0] + big_total[0]
+        new_down_mom = big_moms[1] + big_total[1]
+        small_total = sum_everywhere(jnp.stack(small_totals))
+        other = swap(bfloat(small_total), "win", 0)
+        pairs = jnp.stack(pick_owner(low_core, bfloat(small_total), other), axis=1)
+        pairs = pairs.reshape(4, -1, 2 * shard_rows, model_width)
+        region_pairs = jnp.pad(region_weight_grad, ((0, 1), (0, 0), (0, 0)))
+        vec_sum = region_sums
+        for bit in range(bit_count("rep")):
+            region_pairs = same_sum(region_pairs, "rep", bit)
+            vec_sum = same_sum(vec_sum, "rep", bit)
+        rows = wide(pick(pairs, win_index >> 1, 1)) + region_pairs
+        rows = rows.reshape(4, 2, shard_rows, model_width)
+        small_moms = small_old_moms + pick(rows, win_index & 1, 1)
+        up_update, down_update, updates = every_update(
+            place, (folded_up_mom, new_down_mom), small_moms, folds
+        )
+        finish_place = jnp.stack([0 * win_index, win_index, 0 * win_index]).astype(jnp.int32)
+        big_parts = [up_update, down_update, folded_up_mom, new_down_mom]
+        small_parts = [*updates, *small_moms]
+    new_up, new_down, new_up_mom, new_down_mom = finish_big(
+        finish_place, big_parts, up_weight, down_weight
+    )
+    new_qkv, new_out, new_qkv_mom, new_out_mom = finish_small(
+        finish_place, small_parts, qkv_weight, out_weight
+    )
+    vec_total = lax.dynamic_slice_in_dim(vec_sum.reshape(-1), win_index * vec_rows, vec_rows)
     new_vec_mom = MOMENTUM_DECAY * vec_mom + vec_total
     new_vectors = (
         lax.dynamic_slice_in_dim(vectors.reshape(-1), win_index * vec_rows, vec_rows)
         - VECTOR_RATE * new_vec_mom
     )
-    new_up_mom = unfold_columns(folded_up_mom, folds)
-    small_rows = jnp.concatenate([new_qkv_mom, new_out_mom[None]])
-    if two_owners:
-        pair = bfloat(jnp.where(first, small_rows[:2], small_rows[2:]))
-        kept, sent = pick_owner(low_core, pair[0], pair[1])
-        shards = jnp.concatenate(pick_owner(low_core, kept, swap(sent, "win", 0)))
-        shards, big.value = tie(shards, big.value)
-        small = Chain(shards, gather_stages(1))
-        small.step()
-        big_mine = big_update(place, big.value, folds, gather_masks())
-        big_mine, small.value = tie(big_mine, small.value)
-        small.step()
-        up_update, down_update = pick_owner(first, big_mine, swap(big_mine, "rep", 0))
-        small_mine = small_update(place, small.value[:, None], gather_masks(1))[0]
-        small_mine = small_mine.reshape(2, shard_rows, model_width)
-        kept, sent = pick_owner(low_core, small_mine[0], small_mine[1])
-        pair = jnp.stack(pick_owner(low_core, kept, swap(sent, "win", 0)))
-        updates = jnp.concatenate(pick_owner(first, pair, swap(pair, "rep", 0)))
-    else:
-        up_update, down_update, updates = every_update(
-            place, (folded_up_mom, new_down_mom), small_rows, folds
-        )
-
-    def stepped(weight, rows_here, update):
-        rows = own_rows(weight, rows_here).astype(jnp.float32)
-        return rows - MATRIX_RATE * update.astype(jnp.float32)
-
-    new_qkv = jnp.stack(
-        [stepped(qkv_weight[number], shard_rows, updates[number]) for number in range(3)]
-    )
-    new_out = stepped(out_weight, shard_rows, updates[3])
-    new_up = stepped(up_weight, shard_rows, unfold_columns(up_update, folds))
-    new_down = stepped(down_weight, ff_rows, down_update)
+
     return (
         out_tokens,
         input_grad,

time: 250 us -> 233 us (0.932)
  waiting for transfers between devices: 37.7 us -> 28.2 us
  other arithmetic: 28.2 us -> 19 us
  local copies, waits for them, and re-layouts: 15.5 us -> 7.08 us
  Pallas kernels: 115 us -> 122 us
  starting transfers between devices: 47.5 us -> 51.9 us
    ppermute x0 -> x42, starting transfers between devices: none -> 44.2 us  [launch(): lax.ppermute(array, axis, [(i, i ^ mask) for i in range(lax.axis_size(axi...]
    ppermute x29 -> x4, waiting for transfers between devices: 32.8 us -> 3.93 us  [swap(): return lax.ppermute(values, axis, [(i, i ^ 1 << bit) for i in range(size)])]
    ppermute x29 -> x4, starting transfers between devices: 28.6 us -> 1.96 us  [swap(): return lax.ppermute(values, axis, [(i, i ^ 1 << bit) for i in range(size)])]
    ppermute x0 -> x42, waiting for transfers between devices: none -> 24.3 us  [launch(): lax.ppermute(array, axis, [(i, i ^ mask) for i in range(lax.axis_size(axi...]
    ppermute x12 -> x3, starting transfers between devices: 18.9 us -> 5.76 us  [gather_far(): lax.ppermute(values, 'win', [(i, i ^ mask) for i in range(size)])]
    pallas_call x5 -> x8, Pallas kernels: 50.6 us -> 57.4 us  [the longest x2 26.4 us: newton_call(): pl.pallas_call(kernel, in_specs=[pl.BlockSpec(memory_space=pltpu.SMEM)] +...]
    concatenate x14 -> x7, other arithmetic: 7.89 us -> 1.52 us  [the longest x1 0.66 us: local(): jnp.concatenate(pick_owner(win_index % 2 == 0, kept, swap(sent, 'win', 0)))]
    sub x5 -> x0, other arithmetic: 5.54 us -> none  [stepped(): return rows - MATRIX_RATE * update.astype(jnp.float32)]
  transfers between devices with their start and end apart: 41 -> 49, of which waited for: 18 -> 14; matrix products, arithmetic and copies ran while one was open for 11% -> 9% of each run, Pallas kernels for 29% -> 29%
where the time goes in v3:
time: 233 us; the launch traced here: 230 us
  Pallas kernels  122 us (52%)
  starting transfers between devices  51.9 us (22%)
  waiting for transfers between devices  28.2 us (12%)
  other arithmetic  19 us (8%)
  local copies, waits for them, and re-layouts  7.08 us (3%)
    ppermute x42, starting transfers between devices, launch(): lax.ppermute(array, axis, [(i, i ^ mask) for i in range(lax.axis_size(axi...  44.2 us
    pallas_call x1, Pallas kernels, mlp(): pl.pallas_call(functools.partial(mlp_kernel, count, seq_len, padded), gri...  29 us
    pallas_call x2, Pallas kernels, newton_call(): pl.pallas_call(kernel, in_specs=[pl.BlockSpec(memory_space=pltpu.SMEM)] +...  26.4 us
    ppermute x42, waiting for transfers between devices, launch(): lax.ppermute(array, axis, [(i, i ^ mask) for i in range(lax.axis_size(axi...  24.3 us
    pallas_call x3, Pallas kernels, window_backward(): pl.pallas_call(functools.partial(window_backward_kernel, count, first_ste...  22.5 us
    pallas_call x1, Pallas kernels, region_backward(): pl.pallas_call(functools.partial(region_backward_kernel, len(regions)), g...  14.3 us
    pallas_call x1, Pallas kernels, window_forward(): pl.pallas_call(functools.partial(window_forward_kernel, count, seq_len, p...  11.1 us
    pallas_call x2, Pallas kernels, pair_gradients(): pl.pallas_call(functools.partial(pair_gradient_kernel, len(first), len(se...  10.3 us
  transfers between devices with their start and end apart: 49, of which 14 were waited for; matrix products, arithmetic and copies ran while one was open for 9% of the time, Pallas kernels for 29%

profile of v3, /device:TPU:0, one launch (start us, length us, event | category | flops | bytes accessed | tf_op | source)
XLA Modules:
  0.0 229.5 jit_solution(12762979672764259035)
XLA Ops:
  1.7 5.1 %collective-permute-start.2 = (bf16[1,24,512]{2,1,0:T(8,128)(2,1)S(1)}, bf16[1,24,512]{2,1,0:T(8,128)(2,1)S(1)}, u32[]{:S(2)}, u32[]{:S(2)}) collective-permute-start(bf16[1,24,512]{2,1,0:T(8,128)(2,1)S(1)} %get-tuple-element.271), channel_id=1, source_target_pairs={{0,24},{2,26},{4,28},{6,30},{8,16},{10,18},{12,20},{14,22},{16,8},... | collective-permute-start | bytes 73736 | tf_op jit(solution)/shard_map/ppermute | solution.py:66
  16.3 3.3 %collective-permute-done.3.refs_1_ = bf16[4,24,512]{2,1,0:T(8,128)(2,1)S(1)} collective-permute-done((bf16[4,24,512]{2,1,0:T(8,128)(2,1)S(1)}, bf16[4,24,512]{2,1,0:T(8,128)(2,1)S(1)}, u32[]{:S(2)}, u32[]{:S(2)}) %collective-permute-start.3) | collective-permute-done | bytes 98336 | tf_op jit(solution)/shard_map/ppermute | solution.py:42
  20.9 3.4 %region_forward.1 = (bf16[384,512]{1,0:T(8,128)(2,1)}, bf16[384,1536]{1,0:T(8,128)(2,1)}, bf16[24,512]{1,0:T(8,128)(2,1)}, f32[24,512]{1,0:T(8,128)S(1)}) custom-call(bf16[4,24,512]{2,1,0:T(8,128)(2,1)S(1)} %pad_maximum_fusion.5.refs_0_, bf16[4,24,512]{2,1,0:T(8,128)(2,1)S(1)} %collective-permute-done.3.refs_1_, ...), custom_call_target="tpu_custom_call" | custom-call | tf_op jit(solution)/shard_map/region_forward/pallas_call | solution.py:1038
  24.3 11.1 %window_forward.1 = (bf16[20,56,512]{2,1,0:T(8,128)(2,1)}, bf16[20,56,1536]{2,1,0:T(8,128)(2,1)}, bf16[20,56,512]{2,1,0:T(8,128)(2,1)}, f32[20,56,512]{2,1,0:T(8,128)}) custom-call(bf16[1,20,50,512]{3,2,1,0:T(8,128)(2,1)} %tokens_ref.7, f32[24,512]{1,0:T(8,128)S(1)} %get-tuple-element.122.region_ref, f32[20,56,1]{2,1,0:T(8,128)S(1)} %copy.46.bias_ref, ...), custom_call_target="tpu_custom_call" | custom-call | tf_op jit(solution)/shard_map/window_forward/pallas_call | solution.py:667
  35.3 29.0 %mlp.1 = (bf16[1,20,50,512]{3,2,1,0:T(8,128)(2,1)}, f32[1120,512]{1,0:T(8,128)}, f32[14,512]{1,0:T(8,128)}, f32[2,8,128,512]{3,2,1,0:T(8,128)}, bf16[2,8,128,512]{3,2,1,0:T(8,128)(2,1)}) custom-call(s32[2]{0:T(128)S(1)} %pad_add_fusion.place_ref, f32[1120,512]{1,0:T(8,128)} %bitcast.200, bf16[1,20,50,512]{3,2,1,0:T(8,128)(2,1)} %cot_ref.1, ...), custom_call_target="tpu_custom_call" | custom-call | flops 1 | bytes 1 | tf_op jit(solution)/shard_map/mlp/pallas_call | solution.py:940
  64.5 8.5 %window_backward.3 = (f32[24,512]{1,0:T(8,128)}, f32[14,512]{1,0:T(8,128)}, f32[20,200,128]{2,1,0:T(8,128)}, bf16[8,56,1536]{2,1,0:T(8,128)(2,1)}, bf16[8,56,512]{2,1,0:T(8,128)(2,1)}) custom-call(bf16[1,20,50,512]{3,2,1,0:T(8,128)(2,1)} %tokens_ref.7, f32[24,512]{1,0:T(8,128)S(1)} %get-tuple-element.122.region_ref, f32[20,56,1]{2,1,0:T(8,128)S(1)} %copy.46.bias_ref, ...), custom_call_target="tpu_custom_call" | custom-call | flops 8000000000 | bytes 4587520 | tf_op jit(solution)/shard_map/window_backward/pallas_call | solution.py:772
  73.1 2.4 %convert_add_fusion = f32[2,8,128,512]{3,2,1,0:T(8,128)S(1)} fusion(f32[2,8,128,512]{3,2,1,0:T(8,128)S(1)} %copy-done.18, bf16[2,8,128,512]{3,2,1,0:T(8,128)(2,1)} %collective-permute-done.7), kind=kLoop, calls=%fused_computation.1 | loop fusion | flops 2097152 | bytes 10485760 | tf_op jit(solution)/shard_map/add | solution.py:1450
  79.4 8.6 %window_backward.4 = (f32[24,512]{1,0:T(8,128)}, f32[14,512]{1,0:T(8,128)}, f32[20,200,128]{2,1,0:T(8,128)}, bf16[8,56,1536]{2,1,0:T(8,128)(2,1)}, bf16[8,56,512]{2,1,0:T(8,128)(2,1)}) custom-call(bf16[1,20,50,512]{3,2,1,0:T(8,128)(2,1)} %tokens_ref.7, f32[24,512]{1,0:T(8,128)S(1)} %get-tuple-element.122.region_ref, ...), custom_call_target="tpu_custom_call", output_to_operand_aliasing={{2}: (12, {})} | custom-call | flops 8000000000 | bytes 4587520 | tf_op jit(solution)/shard_map/window_backward/pallas_call | solution.py:772
  88.0 2.3 %collective-permute-done.8 = bf16[8,128,256]{2,1,0:T(8,128)(2,1)S(1)} collective-permute-done((bf16[8,128,256]{2,1,0:T(8,128)(2,1)S(1)}, bf16[8,128,256]{2,1,0:T(8,128)(2,1)S(1)}, u32[]{:S(2)}, u32[]{:S(2)}) %collective-permute-start.8) | collective-permute-done | bytes 524320 | tf_op jit(solution)/shard_map/ppermute | solution.py:114
  95.7 5.4 %window_backward.5 = (f32[24,512]{1,0:T(8,128)}, f32[14,512]{1,0:T(8,128)}, f32[20,200,128]{2,1,0:T(8,128)}, bf16[4,56,1536]{2,1,0:T(8,128)(2,1)}, bf16[4,56,512...) custom-call(bf16[1,20,50,512]{3,2,1,0:T(8,128)(2,1)} %tokens_ref.7, ...), custom_call_target="tpu_custom_call", output_to_operand_aliasing={{2}: (12, {})} | custom-call | flops 4000000000 | bytes 2293760 | tf_op jit(solution)/shard_map/window_backward/pallas_call | solution.py:772
  102.4 2.9 %collective-permute-start.11 = (bf16[1,40,512]{2,1,0:T(8,128)(2,1)S(1)}, bf16[1,40,512]{2,1,0:T(8,128)(2,1)S(1)}, u32[]{:S(2)}, u32[]{:S(2)}) collective-permute-start(bf16[1,40,512]{2,1,0:T(8,128)(2,1)S(1)} %bitcast.166), channel_id=1, source_target_pairs={{0,16},{2,18},{4,20},{6,22},{8,24},{10,26},{12,28},{14,30},{16,0},... | collective-permute-start | bytes 122888 | tf_op jit(solution)/shard_map/ppermute | solution.py:114
  105.6 5.2 %pair_gradients.2 = (f32[512,512]{1,0:T(8,128)}, bf16[512,512]{1,0:T(8,128)(2,1)}) custom-call(s32[2]{0:T(128)S(1)} %pad_add_fusion.place_ref, bf16[1120,512]{1,0:T(8,128)(2,1)} %bitcast.169, bf16[448,1536]{1,0:T(8,128)(2,1)} %bitcast.178, bf16[1120,512]{1,0:T(8,128)(2,1)} %bitcast.170, bf16[448,1536]{1,0:T(8,128)(2,1)} %bitcast.181, ...), custom_call_target="tpu_custom_call" | custom-call | flops 1 | bytes 1 | tf_op jit(solution)/shard_map/pair_gradients/pallas_call | solution.py:1225
  114.3 5.1 %pair_gradients.3 = (f32[512,512]{1,0:T(8,128)}, bf16[512,512]{1,0:T(8,128)(2,1)}) custom-call(s32[2]{0:T(128)S(1)} %pad_add_fusion.place_ref, bf16[1120,512]{1,0:T(8,128)(2,1)} %bitcast.175, bf16[448,1536]{1,0:T(8,128)(2,1)} %bitcast.180, bf16[1120,512]{1,0:T(8,128)(2,1)} %bitcast.176, bf16[448,1536]{1,0:T(8,128)(2,1)} %bitcast.183, ...), custom_call_target="tpu_custom_call" | custom-call | flops 1 | bytes 1 | tf_op jit(solution)/shard_map/pair_gradients/pallas_call | solution.py:1225
  120.4 5.7 %collective-permute-done.13.refs_5_ = bf16[4,40,512]{2,1,0:T(8,128)(2,1)S(1)} collective-permute-done((bf16[4,40,512]{2,1,0:T(8,128)(2,1)S(1)}, bf16[4,40,512]{2,1,0:T(8,128)(2,1)S(1)}, u32[]{:S(2)}, u32[]{:S(2)}) %collective-permute-start.13) | collective-permute-done | bytes 163872 | tf_op jit(solution)/shard_map/ppermute | solution.py:114
  126.2 3.8 %collective-permute-start.19 = (bf16[128,512]{1,0:T(8,128)(2,1)}, bf16[128,512]{1,0:T(8,128)(2,1)S(1)}, u32[]{:S(2)}, u32[]{:S(2)}) collective-permute-start(bf16[128,512]{1,0:T(8,128)(2,1)} %get-tuple-element.168), channel_id=1, source_target_pairs={{0,16},{2,18},{4,20},{6,22},{8,24},{10,26},{12,28},{14,30},{16,0},... | collective-permute-start | bytes 393224 | tf_op jit(solution)/shard_map/ppermute | solution.py:114
  136.2 4.0 %collective-permute-done.19 = bf16[128,512]{1,0:T(8,128)(2,1)S(1)} collective-permute-done((bf16[128,512]{1,0:T(8,128)(2,1)}, bf16[128,512]{1,0:T(8,128)(2,1)S(1)}, u32[]{:S(2)}, u32[]{:S(2)}) %collective-permute-start.19) | collective-permute-done | bytes 131104 | tf_op jit(solution)/shard_map/ppermute | solution.py:114
  140.8 2.5 %collective-permute-start.27 = (bf16[1,128,512]{2,1,0:T(8,128)(2,1)S(1)}, bf16[1,128,512]{2,1,0:T(8,128)(2,1)S(1)}, u32[]{:S(2)}, u32[]{:S(2)}) collective-permute-start(bf16[1,128,512]{2,1,0:T(8,128)(2,1)S(1)} %get-tuple-element.252), channel_id=1, source_target_pairs={{0,8},{2,10},{4,12},{6,14},{8,0},{10,2},{12,4},{14,6},{16,24},{18,... | collective-permute-start | bytes 393224 | tf_op jit(solution)/shard_map/ppermute | solution.py:114
  145.9 14.3 %region_backward.1 = (f32[24,512]{1,0:T(8,128)S(1)}, f32[3,64,512]{2,1,0:T(8,128)S(1)}, f32[16,512]{1,0:T(8,128)S(1)}) custom-call(s32[2]{0:T(128)S(1)} %copy-done.12, bf16[4,24,512]{2,1,0:T(8,128)(2,1)S(1)} %pad_maximum_fusion.5.refs_0_, bf16[4,24,512]{2,1,0:T(8,128)(2,1)S(1)} %collective-permute-done.3.refs_1_, ...), custom_call_target="tpu_custom_call" | custom-call | tf_op jit(solution)/shard_map/region_backward/pallas_call | solution.py:1176
  169.3 2.0 collective-permute-start.31
  174.4 3.1 %collective-permute-done.33.refs_1_ = bf16[4,128,512]{2,1,0:T(8,128)(2,1)} collective-permute-done((bf16[4,128,512]{2,1,0:T(8,128)(2,1)S(1)}, bf16[4,128,512]{2,1,0:T(8,128)(2,1)}, u32[]{:S(2)}, u32[]{:S(2)}) %collective-permute-start.33) | collective-permute-done | bytes 524320 | tf_op jit(solution)/shard_map/ppermute | solution.py:114
  184.7 3.5 %collective-permute-done.36 = bf16[1,64,512]{2,1,0:T(8,128)(2,1)S(1)} collective-permute-done((bf16[1,64,512]{2,1,0:T(8,128)(2,1)S(1)}, bf16[1,64,512]{2,1,0:T(8,128)(2,1)S(1)}, u32[]{:S(2)}, u32[]{:S(2)}) %collective-permute-start.36) | collective-permute-done | bytes 65568 | tf_op jit(solution)/shard_map/ppermute | solution.py:114
  191.4 16.0 %big_newton.1.mine = bf16[128,512]{1,0:T(8,128)(2,1)S(1)} custom-call(s32[2]{0:T(128)S(1)} %copy-done.13, bf16[4,128,512]{2,1,0:T(8,128)(2,1)S(1)} %pad_maximum_fusion.refs_0_, bf16[4,128,512]{2,1,0:T(8,128)(2,1)} %collective-permute-done.33.refs_1_, bf16[4,128,512]{2,1,0:T(8,128)(2,1)S(1)} %collective-permute-done.39.refs_2_, ...), custom_call_target="tpu_custom_call" | custom-call | flops 1 | bytes 1 | tf_op jit(solution)/shard_map/big_newton/pallas_call | solution.py:325
  207.4 10.4 %small_newton.1 = bf16[1,64,512]{2,1,0:T(8,128)(2,1)S(1)} custom-call(s32[2]{0:T(128)S(1)} %copy-done.13, bf16[4,1,64,512]{3,2,1,0:T(8,128)(2,1)S(1)} %bitcast.163, bf16[4,1,64,512]{3,2,1,0:T(8,128)(2,1)S(1)} %bitcast.164), custom_call_target="tpu_custom_call" | custom-call | flops 1 | bytes 1 | tf_op jit(solution)/shard_map/small_newton/pallas_call | solution.py:325
  218.0 2.2 collective-permute-start.47
  (232 shorter events, 68.0 us)
Async XLA Ops:
  1.7 12.6 %collective-permute-start.2 = (bf16[1,24,512]{2,1,0:T(8,128)(2,1)S(1)}, bf16[1,24,512]{2,1,0:T(8,128)(2,1)S(1)}, u32[]{:S(2)}, u32[]{:S(2)}) collective-permute-start(bf16[1,24,512]{2,1,0:T(8,128)(2,1)S(1)} %get-tuple-element.271), channel_id=1, source_target_pairs={{0,24},{2,26},{4,28},{6,30},{8,16},{10,18},{12,20},{14,22},{16,8},... | collective-permute-start | bytes 73736 | tf_op jit(solution)/shard_map/ppermute | solution.py:66
  76.1 14.2 %collective-permute-start.8 = (bf16[8,128,256]{2,1,0:T(8,128)(2,1)S(1)}, bf16[8,128,256]{2,1,0:T(8,128)(2,1)S(1)}, u32[]{:S(2)}, u32[]{:S(2)}) collective-permute-start(bf16[8,128,256]{2,1,0:T(8,128)(2,1)S(1)} %fusion), channel_id=1, source_target_pairs={{0,1},{1,0},{2,3},{3,2},{4,5},{5,4},{6,7},{7,6},{8,9},{9,8},{10,11... | collective-permute-start | bytes 1572872 | tf_op jit(solution)/shard_map/ppermute | solution.py:114
  77.9 14.0 %collective-permute-start.9 = (bf16[2,4,128,256]{3,2,1,0:T(8,128)(2,1)S(1)}, bf16[2,4,128,256]{3,2,1,0:T(8,128)(2,1)S(1)}, u32[]{:S(2)}, u32[]{:S(2)}) collective-permute-start(bf16[2,4,128,256]{3,2,1,0:T(8,128)(2,1)S(1)} %fusion.1), channel_id=1, source_target_pairs={{0,4},{2,6},{4,0},{6,2},{8,12},{10,14},{12,8},{14,10},{16,20},{18,... | collective-permute-start | bytes 1572872 | tf_op jit(solution)/shard_map/ppermute | solution.py:114
  93.7 17.5 %collective-permute-start.14 = (bf16[4,128,256]{2,1,0:T(8,128)(2,1)}, bf16[4,128,256]{2,1,0:T(8,128)(2,1)}, u32[]{:S(2)}, u32[]{:S(2)}) collective-permute-start(bf16[4,128,256]{2,1,0:T(8,128)(2,1)} %fusion.3), channel_id=1, source_target_pairs={{0,4},{2,6},{4,0},{6,2},{8,12},{10,14},{12,8},{14,10},{16,20},{18,... | collective-permute-start | bytes 786440 | tf_op jit(solution)/shard_map/ppermute | solution.py:114
  95.2 16.0 %collective-permute-start.15 = (bf16[4,128,256]{2,1,0:T(8,128)(2,1)}, bf16[4,128,256]{2,1,0:T(8,128)(2,1)}, u32[]{:S(2)}, u32[]{:S(2)}) collective-permute-start(bf16[4,128,256]{2,1,0:T(8,128)(2,1)} %fusion.2), channel_id=1, source_target_pairs={{0,1},{1,0},{2,3},{3,2},{4,5},{5,4},{6,7},{7,6},{8,9},{9,8},{10,11... | collective-permute-start | bytes 786440 | tf_op jit(solution)/shard_map/ppermute | solution.py:114
  110.7 15.5 %collective-permute-start.21 = (bf16[512,512]{1,0:T(8,128)(2,1)}, bf16[512,512]{1,0:T(8,128)(2,1)}, u32[]{:S(2)}, u32[]{:S(2)}) collective-permute-start(bf16[512,512]{1,0:T(8,128)(2,1)} %get-tuple-element.148), channel_id=1, source_target_pairs={{0,2},{2,0},{4,6},{6,4},{8,10},{10,8},{12,14},{14,12},{16,18},{18,... | collective-permute-start | bytes 1572872 | tf_op jit(solution)/shard_map/ppermute | solution.py:114
  119.5 10.5 %collective-permute-start.22 = (bf16[512,512]{1,0:T(8,128)(2,1)}, bf16[512,512]{1,0:T(8,128)(2,1)}, u32[]{:S(2)}, u32[]{:S(2)}) collective-permute-start(bf16[512,512]{1,0:T(8,128)(2,1)} %get-tuple-element.163), channel_id=1, source_target_pairs={{0,2},{2,0},{4,6},{6,4},{8,10},{10,8},{12,14},{14,12},{16,18},{18,... | collective-permute-start | bytes 1572872 | tf_op jit(solution)/shard_map/ppermute | solution.py:114
  120.1 23.2 %collective-permute-start.16 = (bf16[4,40,512]{2,1,0:T(8,128)(2,1)S(1)}, bf16[4,40,512]{2,1,0:T(8,128)(2,1)S(1)}, u32[]{:S(2)}, u32[]{:S(2)}) collective-permute-start(bf16[4,40,512]{2,1,0:T(8,128)(2,1)S(1)} %pad_maximum_fusion.3.refs_4_), channel_id=1, source_target_pairs={{0,2},{2,0},{4,6},{6,4},{8,10},{10,8},{12,14},{14,12},{16,18},{18,... | collective-permute-start | bytes 491528 | tf_op jit(solution)/shard_map/ppermute | solution.py:114
  126.1 18.3 %collective-permute-start.17 = (bf16[4,40,512]{2,1,0:T(8,128)(2,1)S(1)}, bf16[4,40,512]{2,1,0:T(8,128)(2,1)S(1)}, u32[]{:S(2)}, u32[]{:S(2)}) collective-permute-start(bf16[4,40,512]{2,1,0:T(8,128)(2,1)S(1)} %collective-permute-done.13.refs_5_), channel_id=1, source_target_pairs={{0,2},{2,0},{4,6},{6,4},{8,10},{10,8},{12,14},{14,12},{16,18},{18,... | collective-permute-start | bytes 491528 | tf_op jit(solution)/shard_map/ppermute | solution.py:114
  126.2 14.0 %collective-permute-start.19 = (bf16[128,512]{1,0:T(8,128)(2,1)}, bf16[128,512]{1,0:T(8,128)(2,1)S(1)}, u32[]{:S(2)}, u32[]{:S(2)}) collective-permute-start(bf16[128,512]{1,0:T(8,128)(2,1)} %get-tuple-element.168), channel_id=1, source_target_pairs={{0,16},{2,18},{4,20},{6,22},{8,24},{10,26},{12,28},{14,30},{16,0},... | collective-permute-start | bytes 393224 | tf_op jit(solution)/shard_map/ppermute | solution.py:114
  130.0 10.7 %collective-permute-start.20 = (bf16[128,512]{1,0:T(8,128)(2,1)S(1)}, bf16[128,512]{1,0:T(8,128)(2,1)S(1)}, u32[]{:S(2)}, u32[]{:S(2)}) collective-permute-start(bf16[128,512]{1,0:T(8,128)(2,1)S(1)} %get-tuple-element.169), channel_id=1, source_target_pairs={{0,24},{2,26},{4,28},{6,30},{8,16},{10,18},{12,20},{14,22},{16,8},... | collective-permute-start | bytes 393224 | tf_op jit(solution)/shard_map/ppermute | solution.py:114
  134.7 25.7 %collective-permute-start.23 = (bf16[8,64,256]{2,1,0:T(8,128)(2,1)S(1)}, bf16[8,64,256]{2,1,0:T(8,128)(2,1)S(1)}, u32[]{:S(2)}, u32[]{:S(2)}) collective-permute-start(bf16[8,64,256]{2,1,0:T(8,128)(2,1)S(1)} %select_convert_fusion), channel_id=1, source_target_pairs={{0,1},{1,0},{2,3},{3,2},{4,5},{5,4},{6,7},{7,6},{8,9},{9,8},{10,11... | collective-permute-start | bytes 786440 | tf_op jit(solution)/shard_map/ppermute | solution.py:114
  140.1 20.8 %collective-permute-start.24 = (bf16[2,4,64,256]{3,2,1,0:T(8,128)(2,1)S(1)}, bf16[2,4,64,256]{3,2,1,0:T(8,128)(2,1)S(1)}, u32[]{:S(2)}, u32[]{:S(2)}) collective-permute-start(bf16[2,4,64,256]{3,2,1,0:T(8,128)(2,1)S(1)} %pad_maximum_fusion.1), channel_id=1, source_target_pairs={{0,4},{2,6},{4,0},{6,2},{8,12},{10,14},{12,8},{14,10},{16,20},{18,... | collective-permute-start | bytes 786440 | tf_op jit(solution)/shard_map/ppermute | solution.py:114
  140.8 23.7 %collective-permute-start.27 = (bf16[1,128,512]{2,1,0:T(8,128)(2,1)S(1)}, bf16[1,128,512]{2,1,0:T(8,128)(2,1)S(1)}, u32[]{:S(2)}, u32[]{:S(2)}) collective-permute-start(bf16[1,128,512]{2,1,0:T(8,128)(2,1)S(1)} %get-tuple-element.252), channel_id=1, source_target_pairs={{0,8},{2,10},{4,12},{6,14},{8,0},{10,2},{12,4},{14,6},{16,24},{18,... | collective-permute-start | bytes 393224 | tf_op jit(solution)/shard_map/ppermute | solution.py:114
  143.4 21.7 %collective-permute-start.28 = (bf16[1,128,512]{2,1,0:T(8,128)(2,1)S(1)}, bf16[1,128,512]{2,1,0:T(8,128)(2,1)S(1)}, u32[]{:S(2)}, u32[]{:S(2)}) collective-permute-start(bf16[1,128,512]{2,1,0:T(8,128)(2,1)S(1)} %get-tuple-element.252), channel_id=1, source_target_pairs={{0,16},{2,18},{4,20},{6,22},{8,24},{10,26},{12,28},{14,30},{16,0},... | collective-permute-start | bytes 393224 | tf_op jit(solution)/shard_map/ppermute | solution.py:114
  144.4 20.7 %collective-permute-start.29 = (bf16[1,128,512]{2,1,0:T(8,128)(2,1)S(1)}, bf16[1,128,512]{2,1,0:T(8,128)(2,1)S(1)}, u32[]{:S(2)}, u32[]{:S(2)}) collective-permute-start(bf16[1,128,512]{2,1,0:T(8,128)(2,1)S(1)} %get-tuple-element.252), channel_id=1, source_target_pairs={{0,24},{2,26},{4,28},{6,30},{8,16},{10,18},{12,20},{14,22},{16,8},... | collective-permute-start | bytes 393224 | tf_op jit(solution)/shard_map/ppermute | solution.py:114
  165.1 12.4 %collective-permute-start.33 = (bf16[4,128,512]{2,1,0:T(8,128)(2,1)S(1)}, bf16[4,128,512]{2,1,0:T(8,128)(2,1)}, u32[]{:S(2)}, u32[]{:S(2)}) collective-permute-start(bf16[4,128,512]{2,1,0:T(8,128)(2,1)S(1)} %pad_maximum_fusion.refs_0_), channel_id=1, source_target_pairs={{0,4},{2,6},{4,0},{6,2},{8,12},{10,14},{12,8},{14,10},{16,20},{18,... | collective-permute-start | bytes 1572872 | tf_op jit(solution)/shard_map/ppermute | solution.py:114
  174.3 14.9 %collective-permute-start.39 = (bf16[4,128,512]{2,1,0:T(8,128)(2,1)S(1)}, bf16[4,128,512]{2,1,0:T(8,128)(2,1)S(1)}, u32[]{:S(2)}, u32[]{:S(2)}) collective-permute-start(bf16[4,128,512]{2,1,0:T(8,128)(2,1)S(1)} %pad_maximum_fusion.refs_0_), channel_id=1, source_target_pairs={{0,2},{2,0},{4,6},{6,4},{8,10},{10,8},{12,14},{14,12},{16,18},{18,... | collective-permute-start | bytes 1572872 | tf_op jit(solution)/shard_map/ppermute | solution.py:114
  177.6 13.2 %collective-permute-start.40 = (bf16[4,128,512]{2,1,0:T(8,128)(2,1)}, bf16[4,128,512]{2,1,0:T(8,128)(2,1)S(1)}, u32[]{:S(2)}, u32[]{:S(2)}) collective-permute-start(bf16[4,128,512]{2,1,0:T(8,128)(2,1)} %collective-permute-done.33.refs_1_), channel_id=1, source_target_pairs={{0,2},{2,0},{4,6},{6,4},{8,10},{10,8},{12,14},{14,12},{16,18},{18,... | collective-permute-start | bytes 1572872 | tf_op jit(solution)/shard_map/ppermute | solution.py:114
  183.3 24.1 %collective-permute-start.44 = (f32[128,512]{1,0:T(8,128)S(1)}, f32[128,512]{1,0:T(8,128)S(1)}, u32[]{:S(2)}, u32[]{:S(2)}) collective-permute-start(f32[128,512]{1,0:T(8,128)S(1)} %get-tuple-element.253.mom_mine), channel_id=1, source_target_pairs={{0,1},{1,0},{2,3},{3,2},{4,5},{5,4},{6,7},{7,6},{8,9},{9,8},{10,11... | collective-permute-start | bytes 786440 | tf_op jit(solution)/shard_map/ppermute | solution.py:114
  188.3 19.1 %collective-permute-start.38 = (bf16[4,64,512]{2,1,0:T(8,128)(2,1)S(1)}, bf16[4,64,512]{2,1,0:T(8,128)(2,1)S(1)}, u32[]{:S(2)}, u32[]{:S(2)}) collective-permute-start(bf16[4,64,512]{2,1,0:T(8,128)(2,1)S(1)} %pad_maximum_fusion.2), channel_id=1, source_target_pairs={{0,4},{2,6},{4,0},{6,2},{8,12},{10,14},{12,8},{14,10},{16,20},{18,... | collective-permute-start | bytes 786440 | tf_op jit(solution)/shard_map/ppermute | solution.py:114
  189.1 18.3 %collective-permute-start.41 = (f32[32,512]{1,0:T(8,128)S(1)}, f32[32,512]{1,0:T(8,128)S(1)}, u32[]{:S(2)}, u32[]{:S(2)}) collective-permute-start(f32[32,512]{1,0:T(8,128)S(1)} %get-tuple-element.266), channel_id=1, source_target_pairs={{0,2},{2,0},{4,6},{6,4},{8,10},{10,8},{12,14},{14,12},{16,18},{18,... | collective-permute-start | bytes 196616 | tf_op jit(solution)/shard_map/ppermute | solution.py:114
  189.2 18.2 %collective-permute-start.43 = (f32[32,512]{1,0:T(8,128)S(1)}, f32[32,512]{1,0:T(8,128)S(1)}, u32[]{:S(2)}, u32[]{:S(2)}) collective-permute-start(f32[32,512]{1,0:T(8,128)S(1)} %get-tuple-element.266), channel_id=1, source_target_pairs={{0,3},{1,2},{2,1},{3,0},{4,7},{5,6},{6,5},{7,4},{8,11},{9,10},{10,... | collective-permute-start | bytes 196616 | tf_op jit(solution)/shard_map/ppermute | solution.py:114
  190.8 16.6 %collective-permute-start.42 = (f32[32,512]{1,0:T(8,128)S(1)}, f32[32,512]{1,0:T(8,128)S(1)}, u32[]{:S(2)}, u32[]{:S(2)}) collective-permute-start(f32[32,512]{1,0:T(8,128)S(1)} %get-tuple-element.210.refs_4_), channel_id=1, source_target_pairs={{0,1},{1,0},{2,3},{3,2},{4,5},{5,4},{6,7},{7,6},{8,9},{9,8},{10,11... | collective-permute-start | bytes 196616 | tf_op jit(solution)/shard_map/ppermute | solution.py:114
  (58 other events, 621.1 us)

commit v4 on v3

--- a/solution.py
+++ b/solution.py
@@ -321,7 +321,7 @@
         out_ref[number] = bfloat(iterate_ref[number, pl.ds(start, rows), :])
 
 
-def newton_call(kernel, name, place, pieces, out_dims, scratch_dims, flops):
+def newton_call(kernel, name, place, pieces, out_dims, scratch_dims, cost):
     return pl.pallas_call(
         kernel,
         in_specs=[pl.BlockSpec(memory_space=pltpu.SMEM)]
@@ -330,7 +330,7 @@
         out_shape=shape_of(out_dims, jnp.bfloat16),
         scratch_shapes=[pltpu.VMEM(dims, jnp.float32) for dims in scratch_dims],
         compiler_params=pltpu.CompilerParams(vmem_limit_bytes=VMEM_LIMIT),
-        cost_estimate=pl.CostEstimate(flops=1, bytes_accessed=1, transcendentals=0),
+        cost_estimate=lasting(cost),
         name=name,
     )(place, *pieces)
 
@@ -345,7 +345,7 @@
         pieces,
         (rows, width),
         [(width, columns), (max(rows, 128), width)],
-        2 * 5 * width * width * (2 * columns + width),
+        16,
     )
 
 
@@ -358,7 +358,7 @@
         pieces,
         (matrices, rows, width),
         [(matrices, width, width)],
-        2 * 27 * matrices * width**3,
+        10 * matrices,
     )
 
 
@@ -385,7 +385,6 @@
 SCORE_SCALE = HEAD_DIM ** (-0.5)
 LOG2_E = 1.4426950408889634
 VMEM_LIMIT = 44 * 1024 * 1024
-WINDOW_COST = 10**9
 VECTOR_ROWS = 16
 NT = (((1,), (1,)), ((), ()))
 TN = (((0,), (0,)), ((), ()))
@@ -646,6 +645,10 @@
 
 def kept_spec():
     return pl.BlockSpec(memory_space=pltpu.VMEM)
+
+
+def lasting(microseconds):
+    return pl.CostEstimate(flops=microseconds * 10**9, bytes_accessed=10**6, transcendentals=0)
 
 
 def in_hbm(values):
@@ -787,9 +790,7 @@
         ],
         input_output_aliases=aliases,
         compiler_params=pltpu.CompilerParams(vmem_limit_bytes=VMEM_LIMIT),
-        cost_estimate=pl.CostEstimate(
-            flops=here * WINDOW_COST, bytes_accessed=here * padded * width * 20, transcendentals=0
-        ),
+        cost_estimate=lasting(here),
         name="window_backward",
     )(*operands)
 
@@ -969,7 +970,7 @@
             pltpu.VMEM((folds, width, width), jnp.float32),
         ],
         compiler_params=pltpu.CompilerParams(vmem_limit_bytes=VMEM_LIMIT),
-        cost_estimate=pl.CostEstimate(flops=1, bytes_accessed=1, transcendentals=0),
+        cost_estimate=lasting(30),
         name="mlp",
     )(place, in_hbm(after), in_hbm(cotangent), keep, vectors, up_weight, down_weight)
     return output, grad, sums, (kept, sent)
@@ -1198,6 +1199,7 @@
             pltpu.VMEM((total, GROUP_HEADS * total), jnp.bfloat16),
         ],
         compiler_params=pltpu.CompilerParams(vmem_limit_bytes=VMEM_LIMIT),
+        cost_estimate=lasting(14),
         name="region_backward",
     )(place, *operands)
 
@@ -1229,7 +1231,7 @@
         out_specs=[whole_spec((width, width))] * 2,
         out_shape=[hbm_shape((width, width)), hbm_shape((width, width), jnp.bfloat16)],
         compiler_params=pltpu.CompilerParams(vmem_limit_bytes=VMEM_LIMIT),
-        cost_estimate=pl.CostEstimate(flops=1, bytes_accessed=1, transcendentals=0),
+        cost_estimate=lasting(5),
         name="pair_gradients",
     )(*operands)
 
@@ -1457,38 +1459,41 @@
             hops, after_grad = tie([array for array, _, _ in hops], after_grad)
             big_taken = order.launch((hops[0], "win", 2), (hops[1], "rep", 1))
     region_branch_grad, region_mix_grad = region_parts
+    norm_rows_ready, mix_ready = seq_norm, local_mix
     if two_owners:
         mix_taken = order.launch(*spread_far(region_mix_grad))
+        big_kept, hops = far_parts(join_halves(add_pair(big_kept, big_taken)))
+        hops, norm_rows_ready = tie([array for array, _, _ in hops], seq_norm)
+        big_taken = order.launch(*[(hop, "win", 4 * (i + 1)) for i, hop in enumerate(hops)])
 
     first = lax.axis_index("rep") == 0
     low_core = win_index % 2 == 0
     kept, sent = pair_gradients(
         place,
-        row_pieces(seq_norm, proj_grads, 0),
-        row_pieces(seq_norm, proj_grads, 1),
+        row_pieces(norm_rows_ready, proj_grads, 0),
+        row_pieces(norm_rows_ready, proj_grads, 1),
         model_width,
     )
+    if two_owners:
+        kept, sent, mix_taken = tie(kept, sent, mix_taken)
+        mixes = [far_piece(region_mix_grad, mix_taken)]
+        mixes, mix_ready = tie(mixes, local_mix)
+        mix_taken = order.launch((mixes[0], "win", 2))
     small_kept = [kept]
     small_taken = order.launch((sent, "win", 1))
-    if two_owners:
-        mixes = [far_piece(region_mix_grad, order.land(mix_taken))]
-        mix_taken = order.launch((mixes[0], "win", 2))
-        big_kept, hops = far_parts(join_halves(add_pair(big_kept, order.land(big_taken))))
-        hops, mix_out = tie([array for array, _, _ in hops], region_mix)
-        big_taken = order.launch(*[(hop, "win", 4 * (i + 1)) for i, hop in enumerate(hops)])
-    else:
-        mix_out = region_mix
     kept, sent = pair_gradients(
         place,
         row_pieces(seq_norm, proj_grads, 2),
-        row_pieces(local_mix, branch_grads, 0)
-        + [(mix_out, 0, region_branch_grad, 0, region_rows)],
+        row_pieces(mix_ready, branch_grads, 0)
+        + [(region_mix, 0, region_branch_grad, 0, region_rows)],
         model_width,
     )
+    if two_owners:
+        kept, sent, mix_taken, big_taken = tie(kept, sent, mix_taken, big_taken)
     small_kept.append(kept)
     small_taken += order.launch((sent, "win", 1))
     if two_owners:
-        mixes += order.land(mix_taken)
+        mixes += mix_taken
         mix_taken = order.launch(*[(piece, "win", 1) for piece in mixes])
     small_totals = [
         (kept + wide(taken)).reshape(-1, 2 * shard_rows, model_width)
@@ -1496,13 +1501,14 @@
     ]
     if two_owners:
         small_kept, hops = first_parts_of_two(small_totals)
+        small_sent = [array for array, _, _ in hops]
         small_taken = order.launch(*hops)
         big_mom = jnp.where(first, big_moms[0], big_moms[1])
-        big_mom = big_mom + add_far(big_kept, order.land(big_taken))
+        big_mom = big_mom + add_far(big_kept, big_taken)
         big_low = bfloat(big_mom)
         big_taken = order.launch(*spread_far(big_low))
-        mixes += order.land(mix_taken)
-        mixes = order.land(mixes)
+        mixes += mix_taken
+        mixes = after(mixes, small_sent, big_low)
     else:
         mixes = gather_blocks(region_mix_grad)
 
@@ -1521,6 +1527,7 @@
     )
 
     if two_owners:
+        region_weight_grad, small_taken, big_taken = tie(region_weight_grad, small_taken, big_taken)
         def spread_pair(mine):
             mine = mine.reshape(2, shard_rows, model_width)
             kept, sent = pick_owner(low_core, mine[0], mine[1])
@@ -1535,7 +1542,7 @@
         )
         rep = lax.axis_index("rep")
         vec_mine = rounded(region_sums)
-        small_kept, hops = second_parts(*add_pair(small_kept, order.land(small_taken)))
+        small_kept, hops = second_parts(*add_pair(small_kept, small_taken))
         small_taken = order.launch(*hops)
         vec_taken = order.launch(
             (bfloat(jnp.concatenate([pick(rep_rows, 1 - rep), vec_mine])), "rep", 1)

time: 233 us -> 219 us (0.940)
  other arithmetic: 19 us -> 13 us
  waiting for transfers between devices: 28.2 us -> 24.3 us
    ppermute x42, waiting for transfers between devices: 24.3 us -> 20.5 us  [launch(): lax.ppermute(array, axis, [(i, i ^ mask) for i in range(lax.axis_size(axi...]
  transfers between devices with their start and end apart: 49 -> 49, of which waited for: 14 -> 12; matrix products, arithmetic and copies ran while one was open for 9% -> 6% of each run, Pallas kernels for 29% -> 35%
where the time goes in v4:
time: 219 us; the launch traced here: 216 us
  Pallas kernels  121 us (55%)
  starting transfers between devices  50.5 us (23%)
  waiting for transfers between devices  24.3 us (11%)
  other arithmetic  13 us (6%)
  local copies, waits for them, and re-layouts  4.98 us (2%)
    ppermute x42, starting transfers between devices, launch(): lax.ppermute(array, axis, [(i, i ^ mask) for i in range(lax.axis_size(axi...  42.7 us
    pallas_call x1, Pallas kernels, mlp(): pl.pallas_call(functools.partial(mlp_kernel, count, seq_len, padded), gri...  29 us
    pallas_call x2, Pallas kernels, newton_call(): pl.pallas_call(kernel, in_specs=[pl.BlockSpec(memory_space=pltpu.SMEM)] +...  25.9 us
    pallas_call x3, Pallas kernels, window_backward(): pl.pallas_call(functools.partial(window_backward_kernel, count, first_ste...  22.4 us
    ppermute x42, waiting for transfers between devices, launch(): lax.ppermute(array, axis, [(i, i ^ mask) for i in range(lax.axis_size(axi...  20.5 us
    pallas_call x1, Pallas kernels, region_backward(): pl.pallas_call(functools.partial(region_backward_kernel, len(regions)), g...  14.3 us
    pallas_call x1, Pallas kernels, window_forward(): pl.pallas_call(functools.partial(window_forward_kernel, count, seq_len, p...  11.1 us
    pallas_call x2, Pallas kernels, pair_gradients(): pl.pallas_call(functools.partial(pair_gradient_kernel, len(first), len(se...  10.4 us
  transfers between devices with their start and end apart: 49, of which 12 were waited for; matrix products, arithmetic and copies ran while one was open for 6% of the time, Pallas kernels for 35%

profile of v4, /device:TPU:0, one launch (start us, length us, event | category | flops | bytes accessed | tf_op | source)
XLA Modules:
  0.0 215.7 jit_solution(9850209404554076704)
XLA Ops:
  1.7 3.1 %collective-permute-start = (bf16[1,24,512]{2,1,0:T(8,128)(2,1)S(1)}, bf16[1,24,512]{2,1,0:T(8,128)(2,1)S(1)}, u32[]{:S(2)}, u32[]{:S(2)}) collective-permute-start(bf16[1,24,512]{2,1,0:T(8,128)(2,1)S(1)} %get-tuple-element.283), channel_id=1, source_target_pairs={{0,8},{2,10},{4,12},{6,14},{8,0},{10,2},{12,4},{14,6},{16,24},{18,... | collective-permute-start | bytes 73736 | tf_op jit(solution)/shard_map/ppermute | solution.py:66
  4.8 2.6 %collective-permute-start.1 = (bf16[1,24,512]{2,1,0:T(8,128)(2,1)S(1)}, bf16[1,24,512]{2,1,0:T(8,128)(2,1)S(1)}, u32[]{:S(2)}, u32[]{:S(2)}) collective-permute-start(bf16[1,24,512]{2,1,0:T(8,128)(2,1)S(1)} %get-tuple-element.283), channel_id=1, source_target_pairs={{0,16},{2,18},{4,20},{6,22},{8,24},{10,26},{12,28},{14,30},{16,0},... | collective-permute-start | bytes 73736 | tf_op jit(solution)/shard_map/ppermute | solution.py:66
  16.3 3.2 %collective-permute-done.3.refs_1_ = bf16[4,24,512]{2,1,0:T(8,128)(2,1)S(1)} collective-permute-done((bf16[4,24,512]{2,1,0:T(8,128)(2,1)S(1)}, bf16[4,24,512]{2,1,0:T(8,128)(2,1)S(1)}, u32[]{:S(2)}, u32[]{:S(2)}) %collective-permute-start.3) | collective-permute-done | bytes 98336 | tf_op jit(solution)/shard_map/ppermute | solution.py:42
  20.8 3.3 %region_forward.1 = (bf16[384,512]{1,0:T(8,128)(2,1)}, bf16[384,1536]{1,0:T(8,128)(2,1)}, bf16[24,512]{1,0:T(8,128)(2,1)}, f32[24,512]{1,0:T(8,128)S(1)}) custom-call(bf16[4,24,512]{2,1,0:T(8,128)(2,1)S(1)} %pad_maximum_fusion.5.refs_0_, bf16[4,24,512]{2,1,0:T(8,128)(2,1)S(1)} %collective-permute-done.3.refs_1_, ...), custom_call_target="tpu_custom_call" | custom-call | tf_op jit(solution)/shard_map/region_forward/pallas_call | solution.py:1039
  24.2 11.1 %window_forward.1 = (bf16[20,56,512]{2,1,0:T(8,128)(2,1)}, bf16[20,56,1536]{2,1,0:T(8,128)(2,1)}, bf16[20,56,512]{2,1,0:T(8,128)(2,1)}, f32[20,56,512]{2,1,0:T(8,128)}) custom-call(bf16[1,20,50,512]{3,2,1,0:T(8,128)(2,1)} %tokens_ref.7, f32[24,512]{1,0:T(8,128)S(1)} %get-tuple-element.128.region_ref, f32[20,56,1]{2,1,0:T(8,128)S(1)} %copy.46.bias_ref, ...), custom_call_target="tpu_custom_call" | custom-call | tf_op jit(solution)/shard_map/window_forward/pallas_call | solution.py:670
  35.2 29.0 %mlp.1 = (bf16[1,20,50,512]{3,2,1,0:T(8,128)(2,1)}, f32[1120,512]{1,0:T(8,128)}, f32[14,512]{1,0:T(8,128)}, f32[2,8,128,512]{3,2,1,0:T(8,128)}, bf16[2,8,128,512]{3,2,1,0:T(8,128)(2,1)}) custom-call(s32[2]{0:T(128)S(1)} %pad_add_fusion.place_ref, f32[1120,512]{1,0:T(8,128)} %bitcast.196, bf16[1,20,50,512]{3,2,1,0:T(8,128)(2,1)} %cot_ref.1, ...), custom_call_target="tpu_custom_call" | custom-call | flops 30000001024 | bytes 1000000 | tf_op jit(solution)/shard_map/mlp/pallas_call | solution.py:941
  64.5 8.5 %window_backward.3 = (f32[24,512]{1,0:T(8,128)}, f32[14,512]{1,0:T(8,128)}, f32[20,200,128]{2,1,0:T(8,128)}, bf16[8,56,1536]{2,1,0:T(8,128)(2,1)}, bf16[8,56,512]{2,1,0:T(8,128)(2,1)}) custom-call(bf16[1,20,50,512]{3,2,1,0:T(8,128)(2,1)} %tokens_ref.7, f32[24,512]{1,0:T(8,128)S(1)} %get-tuple-element.128.region_ref, f32[20,56,1]{2,1,0:T(8,128)S(1)} %copy.46.bias_ref, ...), custom_call_target="tpu_custom_call" | custom-call | flops 8000000000 | bytes 1000000 | tf_op jit(solution)/shard_map/window_backward/pallas_call | solution.py:775
  73.0 2.3 %convert_add_fusion = f32[2,8,128,512]{3,2,1,0:T(8,128)S(1)} fusion(f32[2,8,128,512]{3,2,1,0:T(8,128)S(1)} %copy-done.11, bf16[2,8,128,512]{3,2,1,0:T(8,128)(2,1)} %collective-permute-done.7), kind=kLoop, calls=%fused_computation.1 | loop fusion | flops 2097152 | bytes 10485760 | tf_op jit(solution)/shard_map/add | solution.py:1452
  79.3 8.6 %window_backward.4 = (f32[24,512]{1,0:T(8,128)}, f32[14,512]{1,0:T(8,128)}, f32[20,200,128]{2,1,0:T(8,128)}, bf16[8,56,1536]{2,1,0:T(8,128)(2,1)}, bf16[8,56,512]{2,1,0:T(8,128)(2,1)}) custom-call(bf16[1,20,50,512]{3,2,1,0:T(8,128)(2,1)} %tokens_ref.7, f32[24,512]{1,0:T(8,128)S(1)} %get-tuple-element.128.region_ref, ...), custom_call_target="tpu_custom_call", output_to_operand_aliasing={{2}: (12, {})} | custom-call | flops 8000000000 | bytes 1000000 | tf_op jit(solution)/shard_map/window_backward/pallas_call | solution.py:775
  87.9 2.3 %collective-permute-done.9 = bf16[2,4,128,256]{3,2,1,0:T(8,128)(2,1)S(1)} collective-permute-done((bf16[2,4,128,256]{3,2,1,0:T(8,128)(2,1)S(1)}, bf16[2,4,128,256]{3,2,1,0:T(8,128)(2,1)S(1)}, u32[]{:S(2)}, u32[]{:S(2)}) %collective-permute-start.9) | collective-permute-done | bytes 524320 | tf_op jit(solution)/shard_map/ppermute | solution.py:114
  94.2 5.4 %window_backward.5 = (f32[24,512]{1,0:T(8,128)}, f32[14,512]{1,0:T(8,128)}, f32[20,200,128]{2,1,0:T(8,128)}, bf16[4,56,1536]{2,1,0:T(8,128)(2,1)}, bf16[4,56,512...) custom-call(bf16[1,20,50,512]{3,2,1,0:T(8,128)(2,1)} %tokens_ref.7, ...), custom_call_target="tpu_custom_call", output_to_operand_aliasing={{2}: (12, {})} | custom-call | flops 4000000000 | bytes 1000000 | tf_op jit(solution)/shard_map/window_backward/pallas_call | solution.py:775
  100.2 3.5 %collective-permute-start.13 = (bf16[1,40,512]{2,1,0:T(8,128)(2,1)S(1)}, bf16[1,40,512]{2,1,0:T(8,128)(2,1)S(1)}, u32[]{:S(2)}, u32[]{:S(2)}) collective-permute-start(bf16[1,40,512]{2,1,0:T(8,128)(2,1)S(1)} %bitcast.164), channel_id=1, source_target_pairs={{0,16},{2,18},{4,20},{6,22},{8,24},{10,26},{12,28},{14,30},{16,0},... | collective-permute-start | bytes 122888 | tf_op jit(solution)/shard_map/ppermute | solution.py:114
  104.1 5.2 %pair_gradients.2 = (f32[512,512]{1,0:T(8,128)}, bf16[512,512]{1,0:T(8,128)(2,1)}) custom-call(s32[2]{0:T(128)S(1)} %pad_add_fusion.place_ref, bf16[1120,512]{1,0:T(8,128)(2,1)} %bitcast.197, bf16[448,1536]{1,0:T(8,128)(2,1)} %bitcast.212, bf16[1120,512]{1,0:T(8,128)(2,1)} %bitcast.198, bf16[448,1536]{1,0:T(8,128)(2,1)} %bitcast.215, ...), custom_call_target="tpu_custom_call" | custom-call | flops 5000000000 | bytes 1000000 | tf_op jit(solution)/shard_map/pair_gradients/pallas_call | solution.py:1227
  111.4 3.8 %collective-permute-start.17 = (bf16[128,512]{1,0:T(8,128)(2,1)S(1)}, bf16[128,512]{1,0:T(8,128)(2,1)S(1)}, u32[]{:S(2)}, u32[]{:S(2)}) collective-permute-start(bf16[128,512]{1,0:T(8,128)(2,1)S(1)} %get-tuple-element.173), channel_id=1, source_target_pairs={{0,16},{2,18},{4,20},{6,22},{8,24},{10,26},{12,28},{14,30},{16,0},... | collective-permute-start | bytes 393224 | tf_op jit(solution)/shard_map/ppermute | solution.py:114
  115.5 5.2 %pair_gradients.3 = (f32[512,512]{1,0:T(8,128)}, bf16[512,512]{1,0:T(8,128)(2,1)}) custom-call(s32[2]{0:T(128)S(1)} %pad_add_fusion.place_ref, bf16[1120,512]{1,0:T(8,128)(2,1)} %bitcast.203, bf16[448,1536]{1,0:T(8,128)(2,1)} %bitcast.214, bf16[1120,512]{1,0:T(8,128)(2,1)} %bitcast.204, bf16[448,1536]{1,0:T(8,128)(2,1)} %bitcast.217, ...), custom_call_target="tpu_custom_call" | custom-call | flops 5000000000 | bytes 1000000 | tf_op jit(solution)/shard_map/pair_gradients/pallas_call | solution.py:1227
  120.7 2.4 %collective-permute-done.17 = bf16[128,512]{1,0:T(8,128)(2,1)S(1)} collective-permute-done((bf16[128,512]{1,0:T(8,128)(2,1)S(1)}, bf16[128,512]{1,0:T(8,128)(2,1)S(1)}, u32[]{:S(2)}, u32[]{:S(2)}) %collective-permute-start.17) | collective-permute-done | bytes 131104 | tf_op jit(solution)/shard_map/ppermute | solution.py:114
  125.9 2.0 collective-permute-start.25
  134.0 14.3 %region_backward.1 = (f32[24,512]{1,0:T(8,128)S(1)}, f32[3,64,512]{2,1,0:T(8,128)S(1)}, f32[16,512]{1,0:T(8,128)S(1)}) custom-call(s32[2]{0:T(128)S(1)} %pad_add_fusion.place_ref, bf16[4,24,512]{2,1,0:T(8,128)(2,1)S(1)} %pad_maximum_fusion.5.refs_0_, bf16[4,24,512]{2,1,0:T(8,128)(2,1)S(1)} %collective-permute-done.3.refs_1_, ...), custom_call_target="tpu_custom_call" | custom-call | flops 14000000000 | bytes 1000000 | tf_op jit(solution)/shard_map/region_backward/pallas_call | solution.py:1177
  153.3 3.4 %collective-permute-done.34 = bf16[80,512]{1,0:T(8,128)(2,1)S(1)} collective-permute-done((bf16[80,512]{1,0:T(8,128)(2,1)S(1)}, bf16[80,512]{1,0:T(8,128)(2,1)S(1)}, u32[]{:S(2)}, u32[]{:S(2)}) %collective-permute-start.34) | collective-permute-done | bytes 81952 | tf_op jit(solution)/shard_map/ppermute | solution.py:114
  161.4 5.5 %collective-permute-done.33.refs_1_ = bf16[4,128,512]{2,1,0:T(8,128)(2,1)S(1)} collective-permute-done((bf16[4,128,512]{2,1,0:T(8,128)(2,1)S(1)}, bf16[4,128,512]{2,1,0:T(8,128)(2,1)S(1)}, u32[]{:S(2)}, u32[]{:S(2)}) %collective-permute-start.33) | collective-permute-done | bytes 524320 | tf_op jit(solution)/shard_map/ppermute | solution.py:114
  168.1 1.9 collective-permute-start.36
  172.1 4.4 %collective-permute-done.36 = bf16[1,64,512]{2,1,0:T(8,128)(2,1)S(1)} collective-permute-done((bf16[1,64,512]{2,1,0:T(8,128)(2,1)S(1)}, bf16[1,64,512]{2,1,0:T(8,128)(2,1)S(1)}, u32[]{:S(2)}, u32[]{:S(2)}) %collective-permute-start.36) | collective-permute-done | bytes 65568 | tf_op jit(solution)/shard_map/ppermute | solution.py:114
  180.3 15.5 %big_newton.1.mine = bf16[128,512]{1,0:T(8,128)(2,1)S(1)} custom-call(s32[2]{0:T(128)S(1)} %pad_add_fusion.place_ref, bf16[4,128,512]{2,1,0:T(8,128)(2,1)S(1)} %pad_maximum_fusion.refs_0_, bf16[4,128,512]{2,1,0:T(8,128)(2,1)S(1)} %collective-permute-done.33.refs_1_, bf16[4,128,512]{2,1,0:T(8,128)(2,1)S(1)} %collective-permute-done.39.refs_2_, ...), custom_call_target="tpu_custom_call" | custom-call | flops 16000000000 | bytes 1000000 | tf_op jit(solution)/shard_map/big_newton/pallas_call | solution.py:325
  196.9 10.4 %small_newton.1 = bf16[1,64,512]{2,1,0:T(8,128)(2,1)S(1)} custom-call(s32[2]{0:T(128)S(1)} %pad_add_fusion.place_ref, bf16[4,1,64,512]{3,2,1,0:T(8,128)(2,1)S(1)} %bitcast.162, bf16[4,1,64,512]{3,2,1,0:T(8,128)(2,1)S(1)} %bitcast.167), custom_call_target="tpu_custom_call" | custom-call | flops 10000000000 | bytes 1000000 | tf_op jit(solution)/shard_map/small_newton/pallas_call | solution.py:325
  (212 shorter events, 57.2 us)
Async XLA Ops:
  1.7 12.5 %collective-permute-start = (bf16[1,24,512]{2,1,0:T(8,128)(2,1)S(1)}, bf16[1,24,512]{2,1,0:T(8,128)(2,1)S(1)}, u32[]{:S(2)}, u32[]{:S(2)}) collective-permute-start(bf16[1,24,512]{2,1,0:T(8,128)(2,1)S(1)} %get-tuple-element.283), channel_id=1, source_target_pairs={{0,8},{2,10},{4,12},{6,14},{8,0},{10,2},{12,4},{14,6},{16,24},{18,... | collective-permute-start | bytes 73736 | tf_op jit(solution)/shard_map/ppermute | solution.py:66
  75.9 14.3 %collective-permute-start.9 = (bf16[2,4,128,256]{3,2,1,0:T(8,128)(2,1)S(1)}, bf16[2,4,128,256]{3,2,1,0:T(8,128)(2,1)S(1)}, u32[]{:S(2)}, u32[]{:S(2)}) collective-permute-start(bf16[2,4,128,256]{3,2,1,0:T(8,128)(2,1)S(1)} %fusion.1), channel_id=1, source_target_pairs={{0,4},{2,6},{4,0},{6,2},{8,12},{10,14},{12,8},{14,10},{16,20},{18,... | collective-permute-start | bytes 1572872 | tf_op jit(solution)/shard_map/ppermute | solution.py:114
  77.8 14.0 %collective-permute-start.8 = (bf16[8,128,256]{2,1,0:T(8,128)(2,1)S(1)}, bf16[8,128,256]{2,1,0:T(8,128)(2,1)S(1)}, u32[]{:S(2)}, u32[]{:S(2)}) collective-permute-start(bf16[8,128,256]{2,1,0:T(8,128)(2,1)S(1)} %fusion), channel_id=1, source_target_pairs={{0,1},{1,0},{2,3},{3,2},{4,5},{5,4},{6,7},{7,6},{8,9},{9,8},{10,11... | collective-permute-start | bytes 1572872 | tf_op jit(solution)/shard_map/ppermute | solution.py:114
  92.1 11.8 %collective-permute-start.10 = (bf16[4,128,256]{2,1,0:T(8,128)(2,1)S(1)}, bf16[4,128,256]{2,1,0:T(8,128)(2,1)S(1)}, u32[]{:S(2)}, u32[]{:S(2)}) collective-permute-start(bf16[4,128,256]{2,1,0:T(8,128)(2,1)S(1)} %fusion.3), channel_id=1, source_target_pairs={{0,4},{2,6},{4,0},{6,2},{8,12},{10,14},{12,8},{14,10},{16,20},{18,... | collective-permute-start | bytes 786440 | tf_op jit(solution)/shard_map/ppermute | solution.py:114
  92.5 11.5 %collective-permute-start.11 = (bf16[4,128,256]{2,1,0:T(8,128)(2,1)S(1)}, bf16[4,128,256]{2,1,0:T(8,128)(2,1)S(1)}, u32[]{:S(2)}, u32[]{:S(2)}) collective-permute-start(bf16[4,128,256]{2,1,0:T(8,128)(2,1)S(1)} %fusion.2), channel_id=1, source_target_pairs={{0,1},{1,0},{2,3},{3,2},{4,5},{5,4},{6,7},{7,6},{8,9},{9,8},{10,11... | collective-permute-start | bytes 786440 | tf_op jit(solution)/shard_map/ppermute | solution.py:114
  99.5 9.8 %collective-permute-start.12 = (bf16[1,40,512]{2,1,0:T(8,128)(2,1)S(1)}, bf16[1,40,512]{2,1,0:T(8,128)(2,1)S(1)}, u32[]{:S(2)}, u32[]{:S(2)}) collective-permute-start(bf16[1,40,512]{2,1,0:T(8,128)(2,1)S(1)} %bitcast.163), channel_id=1, source_target_pairs={{0,8},{2,10},{4,12},{6,14},{8,0},{10,2},{12,4},{14,6},{16,24},{18,... | collective-permute-start | bytes 122888 | tf_op jit(solution)/shard_map/ppermute | solution.py:114
  109.5 13.6 %collective-permute-start.15 = (bf16[4,40,512]{2,1,0:T(8,128)(2,1)S(1)}, bf16[4,40,512]{2,1,0:T(8,128)(2,1)S(1)}, u32[]{:S(2)}, u32[]{:S(2)}) collective-permute-start(bf16[4,40,512]{2,1,0:T(8,128)(2,1)S(1)} %pad_maximum_fusion.3.refs_4_), channel_id=1, source_target_pairs={{0,4},{2,6},{4,0},{6,2},{8,12},{10,14},{12,8},{14,10},{16,20},{18,... | collective-permute-start | bytes 491528 | tf_op jit(solution)/shard_map/ppermute | solution.py:114
  111.4 11.8 %collective-permute-start.17 = (bf16[128,512]{1,0:T(8,128)(2,1)S(1)}, bf16[128,512]{1,0:T(8,128)(2,1)S(1)}, u32[]{:S(2)}, u32[]{:S(2)}) collective-permute-start(bf16[128,512]{1,0:T(8,128)(2,1)S(1)} %get-tuple-element.173), channel_id=1, source_target_pairs={{0,16},{2,18},{4,20},{6,22},{8,24},{10,26},{12,28},{14,30},{16,0},... | collective-permute-start | bytes 393224 | tf_op jit(solution)/shard_map/ppermute | solution.py:114
  115.5 13.4 %collective-permute-start.21 = (bf16[512,512]{1,0:T(8,128)(2,1)}, bf16[512,512]{1,0:T(8,128)(2,1)}, u32[]{:S(2)}, u32[]{:S(2)}) collective-permute-start(bf16[512,512]{1,0:T(8,128)(2,1)} %get-tuple-element.177), channel_id=1, source_target_pairs={{0,2},{2,0},{4,6},{6,4},{8,10},{10,8},{12,14},{14,12},{16,18},{18,... | collective-permute-start | bytes 1572872 | tf_op jit(solution)/shard_map/ppermute | solution.py:114
  125.9 22.6 %collective-permute-start.25 = (bf16[1,128,512]{2,1,0:T(8,128)(2,1)S(1)}, bf16[1,128,512]{2,1,0:T(8,128)(2,1)S(1)}, u32[]{:S(2)}, u32[]{:S(2)}) collective-permute-start(bf16[1,128,512]{2,1,0:T(8,128)(2,1)S(1)} %bitcast.187), channel_id=1, source_target_pairs={{0,8},{2,10},{4,12},{6,14},{8,0},{10,2},{12,4},{14,6},{16,24},{18,... | collective-permute-start | bytes 393224 | tf_op jit(solution)/shard_map/ppermute | solution.py:114
  127.9 20.6 %collective-permute-start.26 = (bf16[1,128,512]{2,1,0:T(8,128)(2,1)S(1)}, bf16[1,128,512]{2,1,0:T(8,128)(2,1)S(1)}, u32[]{:S(2)}, u32[]{:S(2)}) collective-permute-start(bf16[1,128,512]{2,1,0:T(8,128)(2,1)S(1)} %bitcast.188), channel_id=1, source_target_pairs={{0,16},{2,18},{4,20},{6,22},{8,24},{10,26},{12,28},{14,30},{16,0},... | collective-permute-start | bytes 393224 | tf_op jit(solution)/shard_map/ppermute | solution.py:114
  128.9 19.6 %collective-permute-start.27 = (bf16[1,128,512]{2,1,0:T(8,128)(2,1)S(1)}, bf16[1,128,512]{2,1,0:T(8,128)(2,1)S(1)}, u32[]{:S(2)}, u32[]{:S(2)}) collective-permute-start(bf16[1,128,512]{2,1,0:T(8,128)(2,1)S(1)} %bitcast.189), channel_id=1, source_target_pairs={{0,24},{2,26},{4,28},{6,30},{8,16},{10,18},{12,20},{14,22},{16,8},... | collective-permute-start | bytes 393224 | tf_op jit(solution)/shard_map/ppermute | solution.py:114
  133.1 15.4 %collective-permute-start.24 = (bf16[2,4,64,256]{3,2,1,0:T(8,128)(2,1)S(1)}, bf16[2,4,64,256]{3,2,1,0:T(8,128)(2,1)S(1)}, u32[]{:S(2)}, u32[]{:S(2)}) collective-permute-start(bf16[2,4,64,256]{3,2,1,0:T(8,128)(2,1)S(1)} %pad_maximum_fusion.1), channel_id=1, source_target_pairs={{0,4},{2,6},{4,0},{6,2},{8,12},{10,14},{12,8},{14,10},{16,20},{18,... | collective-permute-start | bytes 786440 | tf_op jit(solution)/shard_map/ppermute | solution.py:114
  133.6 14.9 %collective-permute-start.23 = (bf16[8,64,256]{2,1,0:T(8,128)(2,1)S(1)}, bf16[8,64,256]{2,1,0:T(8,128)(2,1)S(1)}, u32[]{:S(2)}, u32[]{:S(2)}) collective-permute-start(bf16[8,64,256]{2,1,0:T(8,128)(2,1)S(1)} %select_convert_fusion), channel_id=1, source_target_pairs={{0,1},{1,0},{2,3},{3,2},{4,5},{5,4},{6,7},{7,6},{8,9},{9,8},{10,11... | collective-permute-start | bytes 786440 | tf_op jit(solution)/shard_map/ppermute | solution.py:114
  152.7 14.2 %collective-permute-start.33 = (bf16[4,128,512]{2,1,0:T(8,128)(2,1)S(1)}, bf16[4,128,512]{2,1,0:T(8,128)(2,1)S(1)}, u32[]{:S(2)}, u32[]{:S(2)}) collective-permute-start(bf16[4,128,512]{2,1,0:T(8,128)(2,1)S(1)} %pad_maximum_fusion.refs_0_), channel_id=1, source_target_pairs={{0,4},{2,6},{4,0},{6,2},{8,12},{10,14},{12,8},{14,10},{16,20},{18,... | collective-permute-start | bytes 1572872 | tf_op jit(solution)/shard_map/ppermute | solution.py:114
  153.3 24.0 %collective-permute-start.39 = (bf16[4,128,512]{2,1,0:T(8,128)(2,1)S(1)}, bf16[4,128,512]{2,1,0:T(8,128)(2,1)S(1)}, u32[]{:S(2)}, u32[]{:S(2)}) collective-permute-start(bf16[4,128,512]{2,1,0:T(8,128)(2,1)S(1)} %pad_maximum_fusion.refs_0_), channel_id=1, source_target_pairs={{0,2},{2,0},{4,6},{6,4},{8,10},{10,8},{12,14},{14,12},{16,18},{18,... | collective-permute-start | bytes 1572872 | tf_op jit(solution)/shard_map/ppermute | solution.py:114
  156.9 10.0 %collective-permute-start.30 = (bf16[64,512]{1,0:T(8,128)(2,1)S(1)}, bf16[64,512]{1,0:T(8,128)(2,1)S(1)}, u32[]{:S(2)}, u32[]{:S(2)}) collective-permute-start(bf16[64,512]{1,0:T(8,128)(2,1)S(1)} %get-tuple-element.272), channel_id=1, source_target_pairs={{0,8},{2,10},{4,12},{6,14},{8,0},{10,2},{12,4},{14,6},{16,24},{18,... | collective-permute-start | bytes 196616 | tf_op jit(solution)/shard_map/ppermute | solution.py:114
  166.9 11.9 %collective-permute-start.40 = (bf16[4,128,512]{2,1,0:T(8,128)(2,1)S(1)}, bf16[4,128,512]{2,1,0:T(8,128)(2,1)S(1)}, u32[]{:S(2)}, u32[]{:S(2)}) collective-permute-start(bf16[4,128,512]{2,1,0:T(8,128)(2,1)S(1)} %collective-permute-done.33.refs_1_), channel_id=1, source_target_pairs={{0,2},{2,0},{4,6},{6,4},{8,10},{10,8},{12,14},{14,12},{16,18},{18,... | collective-permute-start | bytes 1572872 | tf_op jit(solution)/shard_map/ppermute | solution.py:114
  171.5 25.3 %collective-permute-start.44 = (f32[128,512]{1,0:T(8,128)S(1)}, f32[128,512]{1,0:T(8,128)S(1)}, u32[]{:S(2)}, u32[]{:S(2)}) collective-permute-start(f32[128,512]{1,0:T(8,128)S(1)} %get-tuple-element.265.mom_mine), channel_id=1, source_target_pairs={{0,1},{1,0},{2,3},{3,2},{4,5},{5,4},{6,7},{7,6},{8,9},{9,8},{10,11... | collective-permute-start | bytes 786440 | tf_op jit(solution)/shard_map/ppermute | solution.py:114
  176.5 20.3 %collective-permute-start.41 = (f32[32,512]{1,0:T(8,128)S(1)}, f32[32,512]{1,0:T(8,128)S(1)}, u32[]{:S(2)}, u32[]{:S(2)}) collective-permute-start(f32[32,512]{1,0:T(8,128)S(1)} %get-tuple-element.278), channel_id=1, source_target_pairs={{0,2},{2,0},{4,6},{6,4},{8,10},{10,8},{12,14},{14,12},{16,18},{18,... | collective-permute-start | bytes 196616 | tf_op jit(solution)/shard_map/ppermute | solution.py:114
  176.5 20.3 %collective-permute-start.43 = (f32[32,512]{1,0:T(8,128)S(1)}, f32[32,512]{1,0:T(8,128)S(1)}, u32[]{:S(2)}, u32[]{:S(2)}) collective-permute-start(f32[32,512]{1,0:T(8,128)S(1)} %get-tuple-element.278), channel_id=1, source_target_pairs={{0,3},{1,2},{2,1},{3,0},{4,7},{5,6},{6,5},{7,4},{8,11},{9,10},{10,... | collective-permute-start | bytes 196616 | tf_op jit(solution)/shard_map/ppermute | solution.py:114
  177.2 19.6 %collective-permute-start.42 = (f32[32,512]{1,0:T(8,128)S(1)}, f32[32,512]{1,0:T(8,128)S(1)}, u32[]{:S(2)}, u32[]{:S(2)}) collective-permute-start(f32[32,512]{1,0:T(8,128)S(1)} %get-tuple-element.222.refs_4_), channel_id=1, source_target_pairs={{0,1},{1,0},{2,3},{3,2},{4,5},{5,4},{6,7},{7,6},{8,9},{9,8},{10,11... | collective-permute-start | bytes 196616 | tf_op jit(solution)/shard_map/ppermute | solution.py:114
  178.8 17.0 %collective-permute-start.38 = (bf16[4,64,512]{2,1,0:T(8,128)(2,1)S(1)}, bf16[4,64,512]{2,1,0:T(8,128)(2,1)S(1)}, u32[]{:S(2)}, u32[]{:S(2)}) collective-permute-start(bf16[4,64,512]{2,1,0:T(8,128)(2,1)S(1)} %pad_maximum_fusion.2), channel_id=1, source_target_pairs={{0,4},{2,6},{4,0},{6,2},{8,12},{10,14},{12,8},{14,10},{16,20},{18,... | collective-permute-start | bytes 786440 | tf_op jit(solution)/shard_map/ppermute | solution.py:114
  195.8 18.1 %collective-permute-start.48 = (bf16[128,512]{1,0:T(8,128)(2,1)S(1)}, bf16[128,512]{1,0:T(8,128)(2,1)S(1)}, u32[]{:S(2)}, u32[]{:S(2)}) collective-permute-start(bf16[128,512]{1,0:T(8,128)(2,1)S(1)} %big_newton.1.mine), channel_id=1, source_target_pairs={{0,1},{1,0},{2,3},{3,2},{4,5},{5,4},{6,7},{7,6},{8,9},{9,8},{10,11... | collective-permute-start | bytes 393224 | tf_op jit(solution)/shard_map/ppermute | solution.py:114
  (48 other events, 358.0 us)
